TPU v7x, 128 devices: a whole 4x4x4 slice. The times are simulated.
128 devices in a mesh: gx: 16 (over z, x), gy: 8 (over y, core).
Axes of the slice: x: 4, y: 4, z: 4, core: 2. Of those that a mesh axis runs over, the one named last changes fastest.
Arguments:
- level_set: float32 [512, 256, 128], P('gx', 'gy'), may hold values from -6 to 6
- sensitivity: float32 [512, 256, 128], P('gx', 'gy'), may hold values from -6 to 6
- smooth_taps: float32 [25], replicated, may hold values from 0.1 to 0.3
- slope_taps: float32 [25], replicated, as said below
- band: int32 [32, 16, 4], P('gx', 'gy'), may hold values from 0 to 1
- time_step: float32 [1], replicated, may hold values from 0.05 to 0.15
Outputs:
- updated: float32 [512, 256, 128], P('gx', 'gy')
Inputs may be any that keep to these rules, and one draw needn't show every extreme that they name: slope_taps[24 - k] = -slope_taps[k]; the middle tap is zero.
All inputs are finite; a program needn't handle non-finite values.
Results may differ from a plain program's by a relative error of at most 0.00002.
Values sent between devices are 32-bit elements; how exact they have to be, the bound alone decides.
No kernel may reach another device: no remote copies, remote signals or barrier semaphores. Data moves between devices by JAX's collectives and lax.ppermute only.
A program may use at most 64 MiB of HBM per device.

v0:
```python
import jax
import jax.numpy as jnp
from jax import lax
from jax.sharding import PartitionSpec as P

UPDATES = 2


opening_depth = ((0, 0), (1, 0), (1, 1))
opening_cross = ((0, 0), (1, 0), (1, 1), (2, 0))
opening_along = ((0, 0), (2, 0), (1, 1), (3, 0))
later_depth = ((0, 0), (0, 1))
later_cross = ((0, 0), (0, 1), (1, 0))
later_along = ((1, 0), (0, 1), (2, 0))


def with_halo(block, sides, width):
    for axis, dim in sides:
        count = lax.axis_size(axis)
        forward = [(i, i + 1) for i in range(count - 1)]
        backward = [(target, source) for source, target in forward]
        low = lax.ppermute(
            lax.slice_in_dim(block, block.shape[dim] - width, None, axis=dim), axis, forward
        )
        high = lax.ppermute(lax.slice_in_dim(block, 0, width, axis=dim), axis, backward)
        block = jnp.concatenate([low, block, high], axis=dim)
    return block


def pad_margin(stack, axis):
    widths = [(0, 0)] * stack.ndim
    widths[axis] = (12, 12)
    return jnp.pad(stack, widths)


def taps_sum(padded, taps, axis, length):
    summed = taps[0] * lax.slice_in_dim(padded, 0, length, axis=axis)
    for offset in range(1, 25):
        summed = summed + taps[offset] * lax.slice_in_dim(
            padded, offset, offset + length, axis=axis
        )
    return summed


def apply_plan(padded, plan, tap_sets, axis, length):
    results = [
        taps_sum(padded[source], tap_sets[filter_kind], axis - 1, length)
        for source, filter_kind in plan
    ]
    return jnp.stack(results)


def per_device(level_set, sensitivity, smooth_taps, slope_taps, band, time_step):
    rows_x, rows_y, depth = level_set.shape
    tap_sets = (smooth_taps, slope_taps)
    blocks_x, blocks_y, blocks_z = band.shape
    mask = jnp.broadcast_to(
        band.astype(jnp.float32)[:, None, :, None, :, None],
        (blocks_x, rows_x // blocks_x, blocks_y, rows_y // blocks_y, blocks_z, depth // blocks_z),
    ).reshape(rows_x, rows_y, depth)
    step_size = time_step[0]
    phi = level_set
    speed = jnp.zeros_like(level_set)
    for update_index in range(UPDATES):
        if update_index == 0:
            fields = jnp.stack([sensitivity, phi])
            plans = (opening_depth, opening_cross, opening_along)
        else:
            fields = phi[None]
            plans = (later_depth, later_cross, later_along)
        depth_out = apply_plan(pad_margin(fields, 3), plans[0], tap_sets, 3, depth)
        piece = lax.all_to_all(depth_out, "gx", split_axis=2, concat_axis=1, tiled=True)
        done = apply_plan(pad_margin(piece, 1), plans[1], tap_sets, 1, piece.shape[1])
        cross_out = lax.all_to_all(done, "gx", split_axis=1, concat_axis=2, tiled=True)
        along_piece = lax.all_to_all(cross_out, "gy", split_axis=1, concat_axis=2, tiled=True)
        along_done = apply_plan(
            pad_margin(along_piece, 2), plans[2], tap_sets, 2, along_piece.shape[2]
        )
        along_out = lax.all_to_all(along_done, "gy", split_axis=2, concat_axis=1, tiled=True)
        if update_index == 0:
            velocity = along_out[0]
            gradient = along_out[1:]
        else:
            gradient = along_out
        magnitude = jnp.sqrt(
            gradient[0] * gradient[0] + gradient[1] * gradient[1] + gradient[2] * gradient[2] + 1.0
        )
        normal_x = gradient[0] / magnitude
        normal_y = gradient[1] / magnitude
        normal_z = gradient[2] / magnitude
        if update_index == 0:
            outgoing = jnp.stack([normal_x, normal_y, velocity])
        else:
            outgoing = jnp.stack([normal_x, normal_y])
        border = with_halo(outgoing, (("gx", 1), ("gy", 2)), 1)
        depth_normal = jnp.pad(normal_z, ((0, 0), (0, 0), (1, 1)))
        curvature = (
            0.5 * (border[0, 2:, 1:-1] - border[0, :-2, 1:-1])
            + 0.5 * (border[1, 1:-1, 2:] - border[1, 1:-1, :-2])
            + 0.5 * (depth_normal[:, :, 2:] - depth_normal[:, :, :-2])
        )
        if update_index == 0:
            velocity_rim = border[2]
            depth_velocity = jnp.pad(velocity, ((0, 0), (0, 0), (1, 1)))
            speed = (
                velocity_rim[1:-1, 1:-1]
                + velocity_rim[2:, 1:-1]
                + velocity_rim[:-2, 1:-1]
                + velocity_rim[1:-1, 2:]
                + velocity_rim[1:-1, :-2]
                + depth_velocity[:, :, 2:]
                + depth_velocity[:, :, :-2]
            ) / 7.0
        phi = phi - mask * step_size * magnitude * (speed - 0.5 * curvature)
    return phi


def solution(mesh):
    return jax.shard_map(
        per_device,
        mesh=mesh,
        in_specs=(P("gx", "gy", None), P("gx", "gy", None), P(), P(), P("gx", "gy", None), P()),
        out_specs=P("gx", "gy", None),
        check_vma=False,
    )
```

profile of v0, /device:TPU:14, one launch (start us, length us, event | category | flops | bytes accessed | tf_op | source)
XLA Modules:
  0.0 609.4 jit_solution(5766003944179479216)
XLA Ops:
  9.2 18.8 %fusion.208 = f32[1,32,32,128]{3,2,1,0:T(8,128)S(1)} fusion(f32[32,32,152]{2,1,0:T(8,128)S(1)} %get-tuple-element.17, f32[]{:T(128)} %bitcast.28, f32[]{:T(128)} %bitcast.27, f32[]{:T(128)} %bitcast.26, f32[]{:T(128)} %bitcast.25, f32[]{:T(128)} %bitcast.24, f32[]{:T(128)} %bitcast.23, f32[]{:T(128)} %bitcast.22, f32[]{:T(128)} %bitcast.21, f32[]{:T(128)} %bitcast.20, ...), kind=kLoop, calls=%fused_computation.450 | loop fusion | flops 6422528 | bytes 13631588 | tf_op jit(solution)/shard_map/stack | solution.py:50
  28.0 18.8 %add_bitcast_fusion.3 = f32[1,32,32,128]{3,2,1,0:T(8,128)S(1)} fusion(f32[32,32,152]{2,1,0:T(8,128)S(1)} %get-tuple-element.18, f32[]{:T(128)} %bitcast.28, f32[]{:T(128)} %bitcast.27, f32[]{:T(128)} %bitcast.26, f32[]{:T(128)} %bitcast.25, f32[]{:T(128)} %bitcast.24, f32[]{:T(128)} %bitcast.23, f32[]{:T(128)} %bitcast.22, f32[]{:T(128)} %bitcast.21, ...), kind=kLoop, calls=%fused_computation.610 | loop fusion | flops 6422528 | bytes 13631588 | tf_op jit(solution)/shard_map/stack | solution.py:50
  46.8 19.0 %add_bitcast_fusion.2 = f32[1,32,32,128]{3,2,1,0:T(8,128)S(1)} fusion(f32[32,32,152]{2,1,0:T(8,128)S(1)} %get-tuple-element.18, f32[]{:T(128)} %bitcast.56, f32[]{:T(128)} %bitcast.55, f32[]{:T(128)} %bitcast.54, f32[]{:T(128)} %bitcast.53, f32[]{:T(128)} %bitcast.52, f32[]{:T(128)} %bitcast.51, f32[]{:T(128)} %bitcast.50, f32[]{:T(128)} %bitcast.49, ...), kind=kLoop, calls=%fused_computation.609 | loop fusion | flops 6422528 | bytes 13631588 | tf_op jit(solution)/shard_map/stack | solution.py:50
  66.9 28.7 %all_to_all.138 = f32[3,32,32,128]{3,1,0,2:T(8,128)S(1)} all-to-all(f32[3,32,32,128]{3,1,0,2:T(8,128)S(1)} %copy.105), channel_id=1, replica_groups=mesh['gx'=16,'gy'=8] {'gx'}, dimensions={2} | all-to-all | bytes 3145728 | tf_op jit(solution)/shard_map/all_to_all | solution.py:72
  97.3 16.1 %fusion.321 = f32[1,512,2,128]{3,1,2,0:T(8,128)S(1)} fusion(f32[1,16,32,2,128]{4,2,1,3,0:T(8,128)S(1)} %copy.108, f32[3,512,2,128]{3,1,2,0:T(8,128)S(1)} %bitcast.369, f32[]{:T(128)} %bitcast.28, f32[]{:T(128)} %bitcast.27, f32[]{:T(128)} %bitcast.26, f32[]{:T(128)} %bitcast.25, f32[]{:T(128)} %bitcast.24, f32[]{:T(128)} %bitcast.23, f32[]{:T(128)} %bitcast.22, ...), kind=kLoop, calls=%fused_computation.598 | loop fusion | flops 6291456 | bytes 2621536 | tf_op jit(solution)/shard_map/add | solution.py:39
  113.4 16.3 %fusion.297 = f32[1,512,2,128]{3,1,2,0:T(8,128)S(1)} fusion(f32[1,16,32,2,128]{4,2,1,3,0:T(8,128)S(1)} %copy.110, f32[3,512,2,128]{3,1,2,0:T(8,128)S(1)} %bitcast.370, f32[]{:T(128)} %bitcast.56, f32[]{:T(128)} %bitcast.55, f32[]{:T(128)} %bitcast.54, f32[]{:T(128)} %bitcast.53, f32[]{:T(128)} %bitcast.52, f32[]{:T(128)} %bitcast.51, f32[]{:T(128)} %bitcast.50, ...), kind=kLoop, calls=%fused_computation.572 | loop fusion | flops 6291456 | bytes 2621536 | tf_op jit(solution)/shard_map/add | solution.py:39
  129.8 16.1 %fusion.309 = f32[1,512,2,128]{3,1,2,0:T(8,128)S(1)} fusion(f32[1,16,32,2,128]{4,2,1,3,0:T(8,128)S(1)} %copy.109, f32[3,512,2,128]{3,1,2,0:T(8,128)S(1)} %bitcast.371, f32[]{:T(128)} %bitcast.28, f32[]{:T(128)} %bitcast.27, f32[]{:T(128)} %bitcast.26, f32[]{:T(128)} %bitcast.25, f32[]{:T(128)} %bitcast.24, f32[]{:T(128)} %bitcast.23, f32[]{:T(128)} %bitcast.22, ...), kind=kLoop, calls=%fused_computation.585 | loop fusion | flops 6291456 | bytes 2621536 | tf_op jit(solution)/shard_map/add | solution.py:39
  163.7 30.4 %all_to_all.139 = f32[4,512,2,128]{3,2,0,1:T(2,128)S(1)} all-to-all(f32[4,512,2,128]{3,2,0,1:T(2,128)S(1)} %copy.112), channel_id=1, replica_groups=mesh['gx'=16,'gy'=8] {'gx'}, dimensions={1} | all-to-all | bytes 4194304 | tf_op jit(solution)/shard_map/all_to_all | solution.py:74
  196.0 30.9 %all_to_all.140 = f32[4,32,32,128]{3,2,0,1:T(8,128)S(1)} all-to-all(f32[4,32,32,128]{3,2,0,1:T(8,128)S(1)} %copy.115), channel_id=1, replica_groups=mesh['gx'=16,'gy'=8] {'gy'}, dimensions={1} | all-to-all | bytes 4194304 | tf_op jit(solution)/shard_map/all_to_all | solution.py:75
  227.4 16.8 %fusion.183 = f32[1,4,256,128]{3,2,1,0:T(8,128)S(1)} fusion(f32[4,280,128]{2,1,0:T(8,128)S(1)} %get-tuple-element.13, f32[]{:T(128)} %bitcast.28, f32[]{:T(128)} %bitcast.27, f32[]{:T(128)} %bitcast.26, f32[]{:T(128)} %bitcast.25, f32[]{:T(128)} %bitcast.24, f32[]{:T(128)} %bitcast.23, f32[]{:T(128)} %bitcast.22, f32[]{:T(128)} %bitcast.21, f32[]{:T(128)} %bitcast.20, ...), kind=kLoop, calls=%fused_computation.398 | loop fusion | flops 6422528 | bytes 13631588 | tf_op jit(solution)/shard_map/stack | solution.py:50
  244.2 16.8 %fusion.158 = f32[1,4,256,128]{3,2,1,0:T(8,128)S(1)} fusion(f32[4,280,128]{2,1,0:T(8,128)S(1)} %get-tuple-element.14, f32[]{:T(128)} %bitcast.28, f32[]{:T(128)} %bitcast.27, f32[]{:T(128)} %bitcast.26, f32[]{:T(128)} %bitcast.25, f32[]{:T(128)} %bitcast.24, f32[]{:T(128)} %bitcast.23, f32[]{:T(128)} %bitcast.22, f32[]{:T(128)} %bitcast.21, f32[]{:T(128)} %bitcast.20, ...), kind=kLoop, calls=%fused_computation.348 | loop fusion | flops 6422528 | bytes 13631588 | tf_op jit(solution)/shard_map/stack | solution.py:50
  261.0 17.0 %fusion.133 = f32[1,4,256,128]{3,2,1,0:T(8,128)S(1)} fusion(f32[4,280,128]{2,1,0:T(8,128)S(1)} %get-tuple-element.15, f32[]{:T(128)} %bitcast.56, f32[]{:T(128)} %bitcast.55, f32[]{:T(128)} %bitcast.54, f32[]{:T(128)} %bitcast.53, f32[]{:T(128)} %bitcast.52, f32[]{:T(128)} %bitcast.51, f32[]{:T(128)} %bitcast.50, f32[]{:T(128)} %bitcast.49, f32[]{:T(128)} %bitcast.48, ...), kind=kLoop, calls=%fused_computation.298 | loop fusion | flops 6422528 | bytes 13631588 | tf_op jit(solution)/shard_map/stack | solution.py:50
  278.1 16.8 %fusion.108 = f32[1,4,256,128]{3,2,1,0:T(8,128)S(1)} fusion(f32[4,280,128]{2,1,0:T(8,128)S(1)} %get-tuple-element.16, f32[]{:T(128)} %bitcast.28, f32[]{:T(128)} %bitcast.27, f32[]{:T(128)} %bitcast.26, f32[]{:T(128)} %bitcast.25, f32[]{:T(128)} %bitcast.24, f32[]{:T(128)} %bitcast.23, f32[]{:T(128)} %bitcast.22, f32[]{:T(128)} %bitcast.21, f32[]{:T(128)} %bitcast.20, ...), kind=kLoop, calls=%fused_computation.248 | loop fusion | flops 6422528 | bytes 13631588 | tf_op jit(solution)/shard_map/stack | solution.py:50
  303.4 25.1 %all-to-all-done.3 = f32[4,4,256,128]{3,1,0,2:T(4,128)S(1)} async-done(((f32[4,4,256,128]{3,1,0,2:T(4,128)}), f32[4,4,256,128]{3,1,0,2:T(4,128)S(1)}, u32[]{:S(2)}, u32[]{:S(2)}) %all-to-all-start.3) | async-done | bytes 2097184 | tf_op jit(solution)/shard_map/all_to_all | solution.py:79
  350.7 19.0 %add_bitcast_fusion = f32[1,32,32,128]{3,2,1,0:T(8,128)S(1)} fusion(f32[32,32,152]{2,1,0:T(8,128)S(1)} %pad_bitcast_fusion, f32[]{:T(128)} %bitcast.56, f32[]{:T(128)} %bitcast.55, f32[]{:T(128)} %bitcast.54, f32[]{:T(128)} %bitcast.53, f32[]{:T(128)} %bitcast.52, f32[]{:T(128)} %bitcast.51, f32[]{:T(128)} %bitcast.50, f32[]{:T(128)} %bitcast.49, ...), kind=kLoop, calls=%fused_computation.603 | loop fusion | flops 6422528 | bytes 13631588 | tf_op jit(solution)/shard_map/stack | solution.py:50
  369.8 18.8 %add_bitcast_fusion.1 = f32[1,32,32,128]{3,2,1,0:T(8,128)S(1)} fusion(f32[32,32,152]{2,1,0:T(8,128)S(1)} %pad_bitcast_fusion, f32[]{:T(128)} %bitcast.28, f32[]{:T(128)} %bitcast.27, f32[]{:T(128)} %bitcast.26, f32[]{:T(128)} %bitcast.25, f32[]{:T(128)} %bitcast.24, f32[]{:T(128)} %bitcast.23, f32[]{:T(128)} %bitcast.22, f32[]{:T(128)} %bitcast.21, ...), kind=kLoop, calls=%fused_computation.604 | loop fusion | flops 6422528 | bytes 13631588 | tf_op jit(solution)/shard_map/stack | solution.py:50
  389.3 19.3 %all_to_all.141 = f32[2,32,32,128]{3,1,0,2:T(8,128)S(1)} all-to-all(f32[2,32,32,128]{3,1,0,2:T(8,128)S(1)} %copy.127), channel_id=1, replica_groups=mesh['gx'=16,'gy'=8] {'gx'}, dimensions={2} | all-to-all | bytes 2097152 | tf_op jit(solution)/shard_map/all_to_all | solution.py:72
  426.2 16.3 %fusion.258 = f32[1,512,2,128]{3,1,2,0:T(8,128)S(1)} fusion(f32[1,16,32,2,128]{4,2,1,3,0:T(8,128)S(1)} %copy.131, f32[2,512,2,128]{3,1,2,0:T(8,128)S(1)} %bitcast.379, f32[]{:T(128)} %bitcast.56, f32[]{:T(128)} %bitcast.55, f32[]{:T(128)} %bitcast.54, f32[]{:T(128)} %bitcast.53, f32[]{:T(128)} %bitcast.52, f32[]{:T(128)} %bitcast.51, f32[]{:T(128)} %bitcast.50, ...), kind=kLoop, calls=%fused_computation.528 | loop fusion | flops 6291456 | bytes 2097248 | tf_op jit(solution)/shard_map/add | solution.py:39
  460.0 23.1 %all_to_all.142 = f32[3,512,2,128]{3,2,0,1:T(2,128)S(1)} all-to-all(f32[3,512,2,128]{3,2,0,1:T(2,128)S(1)} %copy.133), channel_id=1, replica_groups=mesh['gx'=16,'gy'=8] {'gx'}, dimensions={1} | all-to-all | bytes 3145728 | tf_op jit(solution)/shard_map/all_to_all | solution.py:74
  484.3 27.2 %all_to_all.143 = f32[3,32,32,128]{3,2,0,1:T(8,128)S(1)} all-to-all(f32[3,32,32,128]{3,2,0,1:T(8,128)S(1)} %copy.136), channel_id=1, replica_groups=mesh['gx'=16,'gy'=8] {'gy'}, dimensions={1} | all-to-all | bytes 3145728 | tf_op jit(solution)/shard_map/all_to_all | solution.py:75
  511.7 16.8 %fusion.79 = f32[1,4,256,128]{3,2,1,0:T(8,128)S(1)} fusion(f32[4,280,128]{2,1,0:T(8,128)S(1)} %get-tuple-element.28, f32[]{:T(128)} %bitcast.28, f32[]{:T(128)} %bitcast.27, f32[]{:T(128)} %bitcast.26, f32[]{:T(128)} %bitcast.25, f32[]{:T(128)} %bitcast.24, f32[]{:T(128)} %bitcast.23, f32[]{:T(128)} %bitcast.22, f32[]{:T(128)} %bitcast.21, f32[]{:T(128)} %bitcast.20, ...), kind=kLoop, calls=%fused_computation.173 | loop fusion | flops 6422528 | bytes 13631588 | tf_op jit(solution)/shard_map/stack | solution.py:50
  528.6 16.8 %fusion.29 = f32[1,4,256,128]{3,2,1,0:T(8,128)S(1)} fusion(f32[4,280,128]{2,1,0:T(8,128)S(1)} %get-tuple-element.30, f32[]{:T(128)} %bitcast.28, f32[]{:T(128)} %bitcast.27, f32[]{:T(128)} %bitcast.26, f32[]{:T(128)} %bitcast.25, f32[]{:T(128)} %bitcast.24, f32[]{:T(128)} %bitcast.23, f32[]{:T(128)} %bitcast.22, f32[]{:T(128)} %bitcast.21, f32[]{:T(128)} %bitcast.20, ...), kind=kLoop, calls=%fused_computation.73 | loop fusion | flops 6422528 | bytes 13631588 | tf_op jit(solution)/shard_map/stack | solution.py:50
  545.4 17.0 %fusion.54 = f32[1,4,256,128]{3,2,1,0:T(8,128)S(1)} fusion(f32[4,280,128]{2,1,0:T(8,128)S(1)} %get-tuple-element.29, f32[]{:T(128)} %bitcast.56, f32[]{:T(128)} %bitcast.55, f32[]{:T(128)} %bitcast.54, f32[]{:T(128)} %bitcast.53, f32[]{:T(128)} %bitcast.52, f32[]{:T(128)} %bitcast.51, f32[]{:T(128)} %bitcast.50, f32[]{:T(128)} %bitcast.49, f32[]{:T(128)} %bitcast.48, ...), kind=kLoop, calls=%fused_computation.123 | loop fusion | flops 6422528 | bytes 13631588 | tf_op jit(solution)/shard_map/stack | solution.py:50
  563.6 24.2 %all_to_all.144 = f32[3,4,256,128]{3,1,0,2:T(4,128)S(1)} all-to-all(f32[3,4,256,128]{3,1,0,2:T(4,128)S(1)} %copy.139), channel_id=1, replica_groups=mesh['gx'=16,'gy'=8] {'gy'}, dimensions={2} | all-to-all | bytes 3145728 | tf_op jit(solution)/shard_map/all_to_all | solution.py:79
  (95 shorter events, 121.1 us)
Async XLA Ops:
  297.8 30.7 %all-to-all-start.3 = ((f32[4,4,256,128]{3,1,0,2:T(4,128)}), f32[4,4,256,128]{3,1,0,2:T(4,128)S(1)}, u32[]{:S(2)}, u32[]{:S(2)}) async-start(f32[4,4,256,128]{3,1,0,2:T(4,128)} %copy.118), calls=%async_computation.3 | async-start | bytes 4194304 | tf_op jit(solution)/shard_map/all_to_all | solution.py:79
  329.7 6.1 %copy-start.1 = (s32[2,2,4]{2,1,0:T(2,128)S(1)}, s32[2,2,4]{2,1,0:T(2,128)}, u32[]{:S(2)}) copy-start(s32[2,2,4]{2,1,0:T(2,128)} %param.10) | copy-start | bytes 196
  330.0 10.2 %collective-permute-start = (f32[3,1,32,128]{3,2,1,0:T(8,128)S(1)}, f32[3,1,32,128]{3,2,1,0:T(8,128)S(1)}, u32[]{:S(2)}, u32[]{:S(2)}) collective-permute-start(f32[3,1,32,128]{3,2,1,0:T(8,128)S(1)} %get-tuple-element.31), channel_id=1, source_target_pairs={{0,8},{8,16},{16,24},{24,32},{32,40},{40,48},{48,56},{56,64},{64,7... | collective-permute-start | bytes 147464 | tf_op jit(solution)/shard_map/ppermute | solution.py:22
  333.9 8.1 %collective-permute-start.1 = (f32[3,1,32,128]{3,2,1,0:T(8,128)S(1)}, f32[3,1,32,128]{3,2,1,0:T(8,128)S(1)}, u32[]{:S(2)}, u32[]{:S(2)}) collective-permute-start(f32[3,1,32,128]{3,2,1,0:T(8,128)S(1)} %get-tuple-element.32), channel_id=1, source_target_pairs={{8,0},{16,8},{24,16},{32,24},{40,32},{48,40},{56,48},{64,56},{72,6... | collective-permute-start | bytes 147464 | tf_op jit(solution)/shard_map/ppermute | solution.py:25
  342.0 4.9 collective-permute-start.3
  344.0 5.7 copy-start
  344.0 5.6 collective-permute-start.2
  588.6 5.9 collective-permute-start.5
  592.4 7.9 %collective-permute-start.4 = (f32[2,1,32,128]{3,2,1,0:T(8,128)S(1)}, f32[2,1,32,128]{3,2,1,0:T(8,128)S(1)}, u32[]{:S(2)}, u32[]{:S(2)}) collective-permute-start(f32[2,1,32,128]{3,2,1,0:T(8,128)S(1)} %get-tuple-element.42), channel_id=1, source_target_pairs={{8,0},{16,8},{24,16},{32,24},{40,32},{48,40},{56,48},{64,56},{72,6... | collective-permute-start | bytes 98312 | tf_op jit(solution)/shard_map/ppermute | solution.py:25
  600.4 4.6 collective-permute-start.6
  602.3 5.3 collective-permute-start.7
where the time goes:
time: 619 us; the launch traced here: 609 us
  other arithmetic  335 us (54%)
  blocking collectives  184 us (30%)
  waiting for transfers between devices  37.8 us (6%)
  starting transfers between devices  25.7 us (4%)
  local copies, waits for them, and re-layouts  25.6 us (4%)
    another operation x18, other arithmetic, apply_plan(): return jnp.stack(results)  213 us
    add x7, other arithmetic, taps_sum(): summed + taps[offset] * lax.slice_in_dim(padded, offset, offset + length,...  113 us
    all_to_all x2, blocking collectives, per_device(): lax.all_to_all(cross_out, 'gy', split_axis=1, concat_axis=2, tiled=True)  58.1 us
    all_to_all x2, blocking collectives, per_device(): lax.all_to_all(done, 'gx', split_axis=1, concat_axis=2, tiled=True)  53.6 us
    all_to_all x2, blocking collectives, per_device(): lax.all_to_all(depth_out, 'gx', split_axis=2, concat_axis=1, tiled=True)  48 us
    all_to_all x1, waiting for transfers between devices, per_device(): lax.all_to_all(along_done, 'gy', split_axis=2, concat_axis=1, tiled=True)  25.1 us
    all_to_all x1, blocking collectives, per_device(): lax.all_to_all(along_done, 'gy', split_axis=2, concat_axis=1, tiled=True)  24.2 us
    ppermute x4, starting transfers between devices, with_halo(): lax.ppermute(lax.slice_in_dim(block, block.shape[dim] - width, None, axis...  12.8 us
  transfers between devices with their start and end apart: 9, of which 5 were waited for; matrix products, arithmetic and copies ran while one was open for 1% of the time, Pallas kernels for 0%

commit v1 on v0

v1 whole, which is shorter than its diff:
```python
import functools

import jax
import jax.numpy as jnp
from jax import lax
from jax.experimental import pallas as pl
from jax.experimental.pallas import tpu as pltpu
from jax.sharding import PartitionSpec as P

UPDATES = 2
REACH = 13
SLAB = 16
SIDE = 32
RIM = 40
WIDE = 64
DEPTH = 128
TAPS = 25
SPAN = SIDE + 2 * REACH

IN_COORDS = list(range(SIDE + REACH)) + list(range(WIDE - REACH, WIDE))
OUT_ROWS = [RIM - 1] + list(range(SIDE + 1))


def split_rows(value):
    high = value.astype(jnp.bfloat16)
    low = (value - high.astype(jnp.float32)).astype(jnp.bfloat16)
    return high, low


def tap_select(index, taps):
    total = jnp.zeros(index.shape, jnp.float32)
    for k in range(TAPS):
        total = jnp.where(index == k, taps[k], total)
    return total


def side_matrix(low_open, high_open, smooth, slope):
    shape = (RIM, 3 * WIDE)
    row = lax.broadcasted_iota(jnp.int32, shape, 0)
    column = lax.broadcasted_iota(jnp.int32, shape, 1)
    place = column & (WIDE - 1)
    source = jnp.where(place < WIDE - SLAB, place, place - WIDE)
    target = jnp.where(row < RIM - 1, row, -1)
    index = source - target + TAPS // 2
    inside = (row < SIDE) | ((row == SIDE) & (high_open != 0)) | ((row == RIM - 1) & (low_open != 0))
    index = jnp.where(inside, index, -1)
    parts = []
    for taps in (smooth, slope):
        full = tap_select(index, taps)
        high = full.astype(jnp.bfloat16).astype(jnp.float32)
        parts.append(jnp.where(column < 2 * WIDE, high, full - high))
    return jnp.concatenate(parts, axis=0).astype(jnp.bfloat16)


def prepare_kernel(smooth, slope, band, step, edges, along_x, along_y, depth_s, depth_g, gain):
    along_x[...] = side_matrix(edges[0], edges[1], smooth, slope)
    along_y[...] = side_matrix(edges[2], edges[3], smooth, slope)
    shape = (DEPTH, DEPTH)
    index = (
        lax.broadcasted_iota(jnp.int32, shape, 0)
        - lax.broadcasted_iota(jnp.int32, shape, 1)
        + TAPS // 2
    )
    for taps, out in ((smooth, depth_s), (slope, depth_g)):
        high, low = split_rows(tap_select(index, taps))
        out[0:DEPTH, :] = high
        out[DEPTH : 2 * DEPTH, :] = high
        out[2 * DEPTH :, :] = low
    blocks_x, blocks_y, blocks_z = 2, 2, 4
    lane = lax.broadcasted_iota(jnp.int32, (SIDE // blocks_y, DEPTH), 1) // (DEPTH // blocks_z)
    for p in range(blocks_x):
        for q in range(blocks_y):
            value = jnp.zeros(lane.shape, jnp.float32)
            for r in range(blocks_z):
                entry = band[p, q, r].astype(jnp.float32) * step[0]
                value = jnp.where(lane == r, entry, value)
            gain[p, q * (SIDE // blocks_y) : (q + 1) * (SIDE // blocks_y), :] = value


def prepare(smooth, slope, band, step, edges):
    smem = pl.BlockSpec(memory_space=pltpu.SMEM)
    vmem = pl.BlockSpec(memory_space=pltpu.VMEM)
    return pl.pallas_call(
        prepare_kernel,
        out_shape=(
            jax.ShapeDtypeStruct((2 * RIM, 3 * WIDE), jnp.bfloat16),
            jax.ShapeDtypeStruct((2 * RIM, 3 * WIDE), jnp.bfloat16),
            jax.ShapeDtypeStruct((3 * DEPTH, DEPTH), jnp.bfloat16),
            jax.ShapeDtypeStruct((3 * DEPTH, DEPTH), jnp.bfloat16),
            jax.ShapeDtypeStruct((2, SIDE, DEPTH), jnp.float32),
        ),
        in_specs=[smem] * 5,
        out_specs=(vmem,) * 5,
    )(smooth, slope, band, step, edges)


def fill_extended(extended, own, x_next, x_prev, y_next, y_prev):
    low = WIDE - REACH
    high = SIDE + REACH
    extended[0:SIDE, 0:SIDE, :] = own
    extended[SIDE:high, 0:SIDE, :] = x_next
    extended[high:low, :, :] = jnp.zeros((low - high, WIDE, DEPTH), jnp.float32)
    extended[low:WIDE, 0:SIDE, :] = x_prev
    for start, slab in ((SIDE, y_next), (WIDE - SLAB, y_prev)):
        extended[0:high, start : start + SLAB, :] = slab[0:high]
        extended[low:WIDE, start : start + SLAB, :] = slab[high:SPAN]


def stacked_parts(value):
    high, low = split_rows(value)
    return jnp.concatenate([high, low, high], axis=0)


def lane_parts(value):
    high, low = split_rows(value)
    return jnp.concatenate([high, low, high], axis=1)


def take_place(block, place):
    outer, inner, depth = block.shape
    return block.reshape(outer * inner, depth)[pl.ds(place, outer, stride=inner), :]


def along_x_stage(extended, crossed, matrix):
    rows = matrix.shape[0]
    crossed[SIDE + REACH : WIDE - REACH, :, :] = jnp.zeros(
        (WIDE - 2 * REACH - SIDE, rows, DEPTH), jnp.float32
    )
    for pair in range(0, len(IN_COORDS), 2):
        places = IN_COORDS[pair : pair + 2]
        value = jnp.concatenate([take_place(extended, y) for y in places], axis=1)
        out = jnp.dot(matrix, stacked_parts(value), preferred_element_type=jnp.float32)
        for at, y in enumerate(places):
            crossed[y, :, :] = out[:, at * DEPTH : (at + 1) * DEPTH]


def gradient_kernel(
    own, x_next, x_prev, y_next, y_prev, along_x, along_y, depth_s, depth_g, speed, gain, out,
    extended, crossed, flat_s, flat_g, normals, lengths,
):
    fill_extended(extended, own[...], x_next[...], x_prev[...], y_next[...], y_prev[...])
    along_x_stage(extended, crossed, along_x[...])
    matrix = along_y[...]
    for at, row in enumerate(OUT_ROWS):
        value = jnp.concatenate(
            [take_place(crossed, row + kind * RIM) for kind in range(2)], axis=1
        )
        got = jnp.dot(matrix, stacked_parts(value), preferred_element_type=jnp.float32)
        flat_s[at, 0:RIM, :] = got[0:RIM, DEPTH:]
        flat_s[at, RIM:, :] = got[RIM:, :DEPTH]
        flat_g[at, :, :] = got[0:RIM, :DEPTH]
    weights_s = depth_s[...]
    weights_g = depth_g[...]
    for at in range(0, SIDE + 2, 2):
        cross = jnp.dot(
            lane_parts(flat_s[at : at + 2].reshape(4 * RIM, DEPTH)), weights_s,
            preferred_element_type=jnp.float32,
        )
        deep = jnp.dot(
            lane_parts(flat_g[at : at + 2].reshape(2 * RIM, DEPTH)), weights_g,
            preferred_element_type=jnp.float32,
        )
        for half in range(2):
            grad_x = cross[2 * half * RIM : (2 * half + 1) * RIM]
            grad_y = cross[(2 * half + 1) * RIM : (2 * half + 2) * RIM]
            grad_z = deep[half * RIM : (half + 1) * RIM]
            square = grad_x * grad_x + grad_y * grad_y + grad_z * grad_z + 1.0
            inverse = lax.rsqrt(square)
            normals[0, at + half, :, :] = grad_x * inverse
            normals[1, at + half, :, :] = grad_y * inverse
            normals[2, at + half, :, :] = grad_z * inverse
            lengths[at + half, :, :] = square * inverse
    lane = lax.broadcasted_iota(jnp.int32, (SIDE, DEPTH), 1)
    for x in range(SIDE):
        at = x + 1
        across = normals[1, at, :, :]
        deep = normals[2, at, 0:SIDE, :]
        bend = normals[0, at + 1, 0:SIDE, :] - normals[0, at - 1, 0:SIDE, :]
        bend += (pltpu.roll(across, RIM - 1, 0) - pltpu.roll(across, 1, 0))[0:SIDE]
        bend += jnp.where(lane < DEPTH - 1, pltpu.roll(deep, DEPTH - 1, 1), 0.0)
        bend -= jnp.where(lane > 0, pltpu.roll(deep, 1, 1), 0.0)
        push = gain[x // (SIDE // 2)] * lengths[at, 0:SIDE, :]
        out[x, :, :] = own[x, :, :] - push * (speed[x, :, :] - 0.25 * bend)


def speed_kernel(
    own, x_next, x_prev, y_next, y_prev, along_x, along_y, depth_s, out,
    extended, crossed, flat_s, velocity,
):
    fill_extended(extended, own[...], x_next[...], x_prev[...], y_next[...], y_prev[...])
    along_x_stage(extended, crossed, along_x[0:RIM + 8, :])
    matrix = along_y[0:RIM + 8, :]
    for pair in range(0, len(OUT_ROWS), 2):
        value = jnp.concatenate(
            [take_place(crossed, row) for row in OUT_ROWS[pair : pair + 2]], axis=1
        )
        got = jnp.dot(matrix, stacked_parts(value), preferred_element_type=jnp.float32)
        for half in range(2):
            flat_s[pair + half, :, :] = got[0:RIM, half * DEPTH : (half + 1) * DEPTH]
    weights = depth_s[...]
    for at in range(0, SIDE + 2, 2):
        got = jnp.dot(
            lane_parts(flat_s[at : at + 2].reshape(2 * RIM, DEPTH)), weights,
            preferred_element_type=jnp.float32,
        )
        velocity[at : at + 2, :, :] = got.reshape(2, RIM, DEPTH)
    lane = lax.broadcasted_iota(jnp.int32, (SIDE, DEPTH), 1)
    for x in range(SIDE):
        at = x + 1
        rim = velocity[at, :, :]
        centre = rim[0:SIDE]
        total = centre + velocity[at + 1, 0:SIDE, :] + velocity[at - 1, 0:SIDE, :]
        total += (pltpu.roll(rim, RIM - 1, 0) + pltpu.roll(rim, 1, 0))[0:SIDE]
        total += jnp.where(lane < DEPTH - 1, pltpu.roll(centre, DEPTH - 1, 1), 0.0)
        total += jnp.where(lane > 0, pltpu.roll(centre, 1, 1), 0.0)
        out[x, :, :] = total / 7.0


def neighbours(forward_block, backward_block, axis):
    count = lax.axis_size(axis)
    forward = [(i, i + 1) for i in range(count - 1)]
    backward = [(target, source) for source, target in forward]
    return lax.ppermute(backward_block, axis, backward), lax.ppermute(forward_block, axis, forward)


def gather_halos(block):
    x_next, x_prev = neighbours(block[..., SIDE - REACH :, :, :], block[..., :REACH, :, :], "gx")

    def slab(low, high):
        return jnp.concatenate(
            [part[..., low:high, :] for part in (block, x_next, x_prev)], axis=-3
        )

    y_next, y_prev = neighbours(slab(SIDE - SLAB, SIDE), slab(0, SLAB), "gy")
    return block, x_next, x_prev, y_next, y_prev


def call_kernel(body, fields, others, field, scratch):
    def whole(array):
        return pl.BlockSpec(array.shape, lambda i, rank=array.ndim: (0,) * rank)

    def one(array):
        if array.ndim == 3:
            return whole(array)
        return pl.BlockSpec((None,) + array.shape[1:], lambda i: (field, 0, 0, 0))

    return pl.pallas_call(
        body,
        grid=(1,),
        out_shape=jax.ShapeDtypeStruct((SIDE, SIDE, DEPTH), jnp.float32),
        in_specs=[one(f) for f in fields] + [whole(o) for o in others],
        out_specs=pl.BlockSpec((SIDE, SIDE, DEPTH), lambda i: (0, 0, 0)),
        scratch_shapes=[pltpu.VMEM(shape, jnp.float32) for shape in scratch],
        compiler_params=pltpu.CompilerParams(vmem_limit_bytes=48 * 1024 * 1024),
    )(*fields, *others)


def per_device(level_set, sensitivity, smooth_taps, slope_taps, band, time_step):
    edges = []
    for axis in ("gx", "gy"):
        at = lax.axis_index(axis)
        edges += [at > 0, at < lax.axis_size(axis) - 1]
    edges = jnp.stack(edges).astype(jnp.int32)
    along_x, along_y, depth_s, depth_g, gain = prepare(
        smooth_taps, slope_taps, band, time_step, edges
    )
    fields = gather_halos(jnp.stack([sensitivity, level_set]))
    rim = SIDE + 2
    speed = call_kernel(
        speed_kernel, fields, (along_x, along_y, depth_s), 0,
        [(WIDE, WIDE, DEPTH), (WIDE, RIM + 8, DEPTH), (rim, RIM, DEPTH), (rim, RIM, DEPTH)],
    )
    phi = level_set
    for update in range(UPDATES):
        if update > 0:
            fields = gather_halos(phi)
        phi = call_kernel(
            gradient_kernel, fields, (along_x, along_y, depth_s, depth_g, speed, gain), 1,
            [
                (WIDE, WIDE, DEPTH), (WIDE, 2 * RIM, DEPTH), (rim, 2 * RIM, DEPTH),
                (rim, RIM, DEPTH), (3, rim, RIM, DEPTH), (rim, RIM, DEPTH),
            ],
        )
    return phi


def solution(mesh):
    return jax.shard_map(
        per_device,
        mesh=mesh,
        in_specs=(P("gx", "gy", None), P("gx", "gy", None), P(), P(), P("gx", "gy", None), P()),
        out_specs=P("gx", "gy", None),
        check_vma=False,
    )
```

time: 619 us -> 75.4 us (0.12); the launches traced: 609 us -> 75.1 us
  other arithmetic: 335 us -> 5.37 us
  blocking collectives: 184 us -> 0 us
  local copies, waits for them, and re-layouts: 25.6 us -> 0.18 us
  Pallas kernels: 0 us -> 13 us
    another operation x20 -> x3, other arithmetic: 215 us -> 2.63 us  [per_device(): fields = gather_halos(jnp.stack([sensitivity, level_set]))]
    all_to_all x7 -> x0, blocking collectives: 184 us -> none  [the longest x2 58.1 us: per_device(): lax.all_to_all(cross_out, 'gy', split_axis=1, concat_axis=2, tiled=True)]
    add x7 -> x0, other arithmetic: 113 us -> none  [taps_sum(): summed + taps[offset] * lax.slice_in_dim(padded, offset, offset + length,...]
    all_to_all x1 -> x0, waiting for transfers between devices: 25.1 us -> none  [per_device(): lax.all_to_all(along_done, 'gy', split_axis=2, concat_axis=1, tiled=True)]
    ppermute x8, waiting for transfers between devices: 12.7 us -> 35.4 us  [the longest x4 18.5 us: neighbours(): lax.ppermute(forward_block, axis, forward)]
    pallas_call x0 -> x4, Pallas kernels: none -> 13 us  [the longest x3 10.9 us: call_kernel(): pl.pallas_call(body, grid=(1,), out_shape=jax.ShapeDtypeStruct((SIDE, SID...]
    another operation x6 -> x0, local copies, waits for them, and re-layouts: 8.07 us -> none  [apply_plan(): return jnp.stack(results)]
    slice x11 -> x6, local copies, waits for them, and re-layouts: 7.47 us -> 0.15 us  [the longest x5 0.12 us: slab(): part[..., low:high, :]]
  transfers between devices with their start and end apart: 9 -> 8, of which waited for: 5 -> 8; matrix products, arithmetic and copies ran while one was open for 1% -> 4% of each run, Pallas kernels for 0% -> 3%
where the time goes in v1:
time: 75.4 us; the launch traced here: 75.1 us
  waiting for transfers between devices  35.4 us (47%)
  starting transfers between devices  20.3 us (27%)
  Pallas kernels  13 us (17%)
  other arithmetic  5.37 us (7%)
  between operations  0.87 us (1%)
    ppermute x4, waiting for transfers between devices, neighbours(): lax.ppermute(forward_block, axis, forward)  18.5 us
    ppermute x4, waiting for transfers between devices, neighbours(): lax.ppermute(backward_block, axis, backward)  16.9 us
    pallas_call x3, Pallas kernels, call_kernel(): pl.pallas_call(body, grid=(1,), out_shape=jax.ShapeDtypeStruct((SIDE, SID...  10.9 us
    ppermute x4, starting transfers between devices, neighbours(): lax.ppermute(forward_block, axis, forward)  10.5 us
    ppermute x4, starting transfers between devices, neighbours(): lax.ppermute(backward_block, axis, backward)  9.85 us
    another operation x3, other arithmetic, per_device(): fields = gather_halos(jnp.stack([sensitivity, level_set]))  2.63 us
    concatenate x4, other arithmetic, slab(): jnp.concatenate([part[..., low:high, :] for part in (block, x_next, x_pre...  2.13 us
    pallas_call x1, Pallas kernels, prepare(): pl.pallas_call(prepare_kernel, out_shape=(jax.ShapeDtypeStruct((2 * RIM,...  2.09 us
  transfers between devices with their start and end apart: 8, of which 8 were waited for; matrix products, arithmetic and copies ran while one was open for 4% of the time, Pallas kernels for 3%

profile of v1, /device:TPU:14, one launch (start us, length us, event | category | flops | bytes accessed | tf_op | source)
XLA Modules:
  0.0 75.1 jit_solution(2025502494440332199)
XLA Ops:
  0.0 1.4 %fusion.3 = (f32[2,13,32,128]{3,2,1,0:T(8,128)S(1)}, f32[2,13,32,128]{3,2,1,0:T(8,128)S(1)}) fusion(f32[1,32,32,128]{3,2,1,0:T(8,128)} %bitcast.9, f32[1,32,32,128]{3,2,1,0:T(8,128)} %bitcast.6), kind=kLoop, calls=%fused_computation.16 | loop fusion | flops 212992 | bytes 1900544 | tf_op jit(solution)/shard_map/stack | solution.py:267
  1.4 3.7 %collective-permute-start.1 = (f32[2,13,32,128]{3,2,1,0:T(8,128)S(1)}, f32[2,13,32,128]{3,2,1,0:T(8,128)S(1)}, u32[]{:S(2)}, u32[]{:S(2)}) collective-permute-start(f32[2,13,32,128]{3,2,1,0:T(8,128)S(1)} %get-tuple-element.17), channel_id=1, source_target_pairs={{0,8},{8,16},{16,24},{24,32},{32,40},{40,48},{48,56},{56,64},{64,7... | collective-permute-start | bytes 1277960 | tf_op jit(solution)/shard_map/ppermute | solution.py:223
  5.1 2.1 %collective-permute-start = (f32[2,13,32,128]{3,2,1,0:T(8,128)S(1)}, f32[2,13,32,128]{3,2,1,0:T(8,128)S(1)}, u32[]{:S(2)}, u32[]{:S(2)}) collective-permute-start(f32[2,13,32,128]{3,2,1,0:T(8,128)S(1)} %get-tuple-element.18), channel_id=1, source_target_pairs={{8,0},{16,8},{24,16},{32,24},{40,32},{48,40},{56,48},{64,56},{72,6... | collective-permute-start | bytes 1277960 | tf_op jit(solution)/shard_map/ppermute | solution.py:223
  7.4 7.5 %collective-permute-done.1.x_prev = f32[2,13,32,128]{3,2,1,0:T(8,128)S(1)} collective-permute-done((f32[2,13,32,128]{3,2,1,0:T(8,128)S(1)}, f32[2,13,32,128]{3,2,1,0:T(8,128)S(1)}, u32[]{:S(2)}, u32[]{:S(2)}) %collective-permute-start.1) | collective-permute-done | bytes 426016 | tf_op jit(solution)/shard_map/ppermute | solution.py:223
  14.9 5.5 %collective-permute-done.x_next = f32[2,13,32,128]{3,2,1,0:T(8,128)S(1)} collective-permute-done((f32[2,13,32,128]{3,2,1,0:T(8,128)S(1)}, f32[2,13,32,128]{3,2,1,0:T(8,128)S(1)}, u32[]{:S(2)}, u32[]{:S(2)}) %collective-permute-start) | collective-permute-done | bytes 426016 | tf_op jit(solution)/shard_map/ppermute | solution.py:223
  20.5 1.0 %pad_maximum_fusion.1 = f32[2,58,16,128]{3,2,1,0:T(8,128)} fusion(f32[2,13,16,128]{3,2,1,0:T(8,128)S(1)} %get-tuple-element.26, f32[2,13,16,128]{3,2,1,0:T(8,128)S(1)} %get-tuple-element.24, f32[2,32,16,128]{3,2,1,0:T(8,128)S(1)} %get-tuple-element.16), kind=kLoop, calls=%fused_computation.9 | loop fusion | flops 475136 | bytes 1900544 | tf_op jit(solution)/shard_map/concatenate | solution.py:230
  21.5 1.9 %collective-permute-start.2 = (f32[2,58,16,128]{3,2,1,0:T(8,128)}, f32[2,58,16,128]{3,2,1,0:T(8,128)S(1)}, u32[]{:S(2)}, u32[]{:S(2)}) collective-permute-start(f32[2,58,16,128]{3,2,1,0:T(8,128)} %pad_maximum_fusion.1), channel_id=1, source_target_pairs={{1,0},{2,1},{3,2},{4,3},{5,4},{6,5},{7,6},{9,8},{10,9},{11,10},{12... | collective-permute-start | bytes 2850824 | tf_op jit(solution)/shard_map/ppermute | solution.py:223
  23.4 1.0 %pad_maximum_fusion.2 = f32[2,58,16,128]{3,2,1,0:T(8,128)} fusion(f32[2,13,16,128]{3,2,1,0:T(8,128)S(1)} %get-tuple-element.25, f32[2,13,16,128]{3,2,1,0:T(8,128)S(1)} %get-tuple-element.23, f32[2,32,16,128]{3,2,1,0:T(8,128)S(1)} %get-tuple-element.15), kind=kLoop, calls=%fused_computation.10 | loop fusion | flops 475136 | bytes 1900544 | tf_op jit(solution)/shard_map/concatenate | solution.py:230
  24.4 2.4 %collective-permute-start.3 = (f32[2,58,16,128]{3,2,1,0:T(8,128)}, f32[2,58,16,128]{3,2,1,0:T(8,128)S(1)}, u32[]{:S(2)}, u32[]{:S(2)}) collective-permute-start(f32[2,58,16,128]{3,2,1,0:T(8,128)} %pad_maximum_fusion.2), channel_id=1, source_target_pairs={{0,1},{1,2},{2,3},{3,4},{4,5},{5,6},{6,7},{8,9},{9,10},{10,11},{11... | collective-permute-start | bytes 2850824 | tf_op jit(solution)/shard_map/ppermute | solution.py:223
  28.1 2.1 %shard_map.64 = (bf16[80,192]{1,0:T(8,128)(2,1)}, bf16[80,192]{1,0:T(8,128)(2,1)}, bf16[384,128]{1,0:T(8,128)(2,1)}, bf16[384,128]{1,0:T(8,128)(2,1)}, f32[2,32,128]{2,1,0:T(8,128)}) custom-call(f32[25]{0:T(128)} %smooth.1, f32[25]{0:T(128)} %slope.1, s32[2,2,4]{2,1,0:T(2,128)} %band.1, f32[1]{0:T(128)S(6)} %copy.7.step, s32[4]{0:T(128)} %add_convert_fusion.edges), custom_call_target="tpu_custom_call" | custom-call | tf_op jit(solution)/shard_map/pallas_call | solution.py:83
  30.2 1.1 %pad_maximum_fusion.own = f32[2,32,32,128]{3,2,1,0:T(8,128)S(1)} fusion(f32[1,32,32,128]{3,2,1,0:T(8,128)S(1)} %bitcast.8, f32[1,32,32,128]{3,2,1,0:T(8,128)} %bitcast.10), kind=kLoop, calls=%fused_computation.4 | loop fusion | flops 262144 | bytes 2097152 | tf_op jit(solution)/shard_map/stack | solution.py:267
  31.4 3.6 %collective-permute-done.2.y_next = f32[2,58,16,128]{3,2,1,0:T(8,128)S(1)} collective-permute-done((f32[2,58,16,128]{3,2,1,0:T(8,128)}, f32[2,58,16,128]{3,2,1,0:T(8,128)S(1)}, u32[]{:S(2)}, u32[]{:S(2)}) %collective-permute-start.2) | collective-permute-done | bytes 950304 | tf_op jit(solution)/shard_map/ppermute | solution.py:223
  35.0 4.7 %collective-permute-done.3.y_prev = f32[2,58,16,128]{3,2,1,0:T(8,128)S(1)} collective-permute-done((f32[2,58,16,128]{3,2,1,0:T(8,128)}, f32[2,58,16,128]{3,2,1,0:T(8,128)S(1)}, u32[]{:S(2)}, u32[]{:S(2)}) %collective-permute-start.3) | collective-permute-done | bytes 950304 | tf_op jit(solution)/shard_map/ppermute | solution.py:223
  39.7 2.6 %shard_map.65.speed = f32[32,32,128]{2,1,0:T(8,128)S(1)} custom-call(f32[2,32,32,128]{3,2,1,0:T(8,128)S(1)} %pad_maximum_fusion.own, f32[2,13,32,128]{3,2,1,0:T(8,128)S(1)} %collective-permute-done.x_next, f32[2,13,32,128]{3,2,1,0:T(8,128)S(1)} %collective-permute-done.1.x_prev, f32[2,58,16,128]{3,2,1,0:T(8,128)S(1)} %collective-permute-done.2.y_next, ...), custom_call_target="tpu_custom_call" | custom-call | tf_op jit(solution)/shard_map/pallas_call | solution.py:247
  42.4 3.7 %shard_map.66.own = f32[32,32,128]{2,1,0:T(8,128)S(1)} custom-call(f32[2,32,32,128]{3,2,1,0:T(8,128)S(1)} %pad_maximum_fusion.own, f32[2,13,32,128]{3,2,1,0:T(8,128)S(1)} %collective-permute-done.x_next, f32[2,13,32,128]{3,2,1,0:T(8,128)S(1)} %collective-permute-done.1.x_prev, f32[2,58,16,128]{3,2,1,0:T(8,128)S(1)} %collective-permute-done.2.y_next, ...), custom_call_target="tpu_custom_call" | custom-call | tf_op jit(solution)/shard_map/pallas_call | solution.py:247
  46.2 1.9 %collective-permute-start.5 = (f32[13,32,128]{2,1,0:T(8,128)S(1)}, f32[13,32,128]{2,1,0:T(8,128)S(1)}, u32[]{:S(2)}, u32[]{:S(2)}) collective-permute-start(f32[13,32,128]{2,1,0:T(8,128)S(1)} %get-tuple-element.21), channel_id=1, source_target_pairs={{0,8},{8,16},{16,24},{24,32},{32,40},{40,48},{48,56},{56,64},{64,7... | collective-permute-start | bytes 638984 | tf_op jit(solution)/shard_map/ppermute | solution.py:223
  48.1 3.9 %collective-permute-start.4 = (f32[13,32,128]{2,1,0:T(8,128)S(1)}, f32[13,32,128]{2,1,0:T(8,128)S(1)}, u32[]{:S(2)}, u32[]{:S(2)}) collective-permute-start(f32[13,32,128]{2,1,0:T(8,128)S(1)} %get-tuple-element.22), channel_id=1, source_target_pairs={{8,0},{16,8},{24,16},{32,24},{40,32},{48,40},{56,48},{64,56},{72,6... | collective-permute-start | bytes 638984 | tf_op jit(solution)/shard_map/ppermute | solution.py:223
  52.1 2.5 %collective-permute-done.5.x_prev = f32[13,32,128]{2,1,0:T(8,128)S(1)} collective-permute-done((f32[13,32,128]{2,1,0:T(8,128)S(1)}, f32[13,32,128]{2,1,0:T(8,128)S(1)}, u32[]{:S(2)}, u32[]{:S(2)}) %collective-permute-start.5) | collective-permute-done | bytes 213024 | tf_op jit(solution)/shard_map/ppermute | solution.py:223
  54.5 4.0 %collective-permute-done.4.x_next = f32[13,32,128]{2,1,0:T(8,128)S(1)} collective-permute-done((f32[13,32,128]{2,1,0:T(8,128)S(1)}, f32[13,32,128]{2,1,0:T(8,128)S(1)}, u32[]{:S(2)}, u32[]{:S(2)}) %collective-permute-start.4) | collective-permute-done | bytes 213024 | tf_op jit(solution)/shard_map/ppermute | solution.py:223
  58.6 1.9 %collective-permute-start.6 = (f32[58,16,128]{2,1,0:T(8,128)S(1)}, f32[58,16,128]{2,1,0:T(8,128)S(1)}, u32[]{:S(2)}, u32[]{:S(2)}) collective-permute-start(f32[58,16,128]{2,1,0:T(8,128)S(1)} %pad_maximum_fusion.3), channel_id=1, source_target_pairs={{1,0},{2,1},{3,2},{4,3},{5,4},{6,5},{7,6},{9,8},{10,9},{11,10},{12... | collective-permute-start | bytes 1425416 | tf_op jit(solution)/shard_map/ppermute | solution.py:223
  60.6 2.4 %collective-permute-start.7 = (f32[58,16,128]{2,1,0:T(8,128)S(1)}, f32[58,16,128]{2,1,0:T(8,128)S(1)}, u32[]{:S(2)}, u32[]{:S(2)}) collective-permute-start(f32[58,16,128]{2,1,0:T(8,128)S(1)} %pad_maximum_fusion.4), channel_id=1, source_target_pairs={{0,1},{1,2},{2,3},{3,4},{4,5},{5,6},{6,7},{8,9},{9,10},{10,11},{11... | collective-permute-start | bytes 1425416 | tf_op jit(solution)/shard_map/ppermute | solution.py:223
  63.0 3.7 %collective-permute-done.6.y_next = f32[58,16,128]{2,1,0:T(8,128)S(1)} collective-permute-done((f32[58,16,128]{2,1,0:T(8,128)S(1)}, f32[58,16,128]{2,1,0:T(8,128)S(1)}, u32[]{:S(2)}, u32[]{:S(2)}) %collective-permute-start.6) | collective-permute-done | bytes 475168 | tf_op jit(solution)/shard_map/ppermute | solution.py:223
  66.7 3.9 %collective-permute-done.7.y_prev = f32[58,16,128]{2,1,0:T(8,128)S(1)} collective-permute-done((f32[58,16,128]{2,1,0:T(8,128)S(1)}, f32[58,16,128]{2,1,0:T(8,128)S(1)}, u32[]{:S(2)}, u32[]{:S(2)}) %collective-permute-start.7) | collective-permute-done | bytes 475168 | tf_op jit(solution)/shard_map/ppermute | solution.py:223
  70.6 4.5 %shard_map.67 = f32[32,32,128]{2,1,0:T(8,128)} custom-call(f32[32,32,128]{2,1,0:T(8,128)S(1)} %shard_map.66.own, f32[13,32,128]{2,1,0:T(8,128)S(1)} %collective-permute-done.4.x_next, f32[13,32,128]{2,1,0:T(8,128)S(1)} %collective-permute-done.5.x_prev, f32[58,16,128]{2,1,0:T(8,128)S(1)} %collective-permute-done.6.y_next, ...), custom_call_target="tpu_custom_call" | custom-call | tf_op jit(solution)/shard_map/pallas_call | solution.py:247
  (24 shorter events, 1.0 us)
Async XLA Ops:
  0.0 7.3 %copy-start.5 = (f32[32,32,128]{2,1,0:T(8,128)S(1)}, f32[32,32,128]{2,1,0:T(8,128)}, u32[]{:S(2)}) copy-start(f32[32,32,128]{2,1,0:T(8,128)} %param.6) | copy-start | bytes 1572868
  0.0 7.3 %copy-start.6 = (f32[32,32,128]{2,1,0:T(8,128)S(1)}, f32[32,32,128]{2,1,0:T(8,128)}, u32[]{:S(2)}) copy-start(f32[32,32,128]{2,1,0:T(8,128)} %param.7) | copy-start | bytes 1572868
  1.4 13.5 %collective-permute-start.1 = (f32[2,13,32,128]{3,2,1,0:T(8,128)S(1)}, f32[2,13,32,128]{3,2,1,0:T(8,128)S(1)}, u32[]{:S(2)}, u32[]{:S(2)}) collective-permute-start(f32[2,13,32,128]{3,2,1,0:T(8,128)S(1)} %get-tuple-element.17), channel_id=1, source_target_pairs={{0,8},{8,16},{16,24},{24,32},{32,40},{40,48},{48,56},{56,64},{64,7... | collective-permute-start | bytes 1277960 | tf_op jit(solution)/shard_map/ppermute | solution.py:223
  5.1 15.3 %collective-permute-start = (f32[2,13,32,128]{3,2,1,0:T(8,128)S(1)}, f32[2,13,32,128]{3,2,1,0:T(8,128)S(1)}, u32[]{:S(2)}, u32[]{:S(2)}) collective-permute-start(f32[2,13,32,128]{3,2,1,0:T(8,128)S(1)} %get-tuple-element.18), channel_id=1, source_target_pairs={{8,0},{16,8},{24,16},{32,24},{40,32},{48,40},{56,48},{64,56},{72,6... | collective-permute-start | bytes 1277960 | tf_op jit(solution)/shard_map/ppermute | solution.py:223
  21.5 13.5 %collective-permute-start.2 = (f32[2,58,16,128]{3,2,1,0:T(8,128)}, f32[2,58,16,128]{3,2,1,0:T(8,128)S(1)}, u32[]{:S(2)}, u32[]{:S(2)}) collective-permute-start(f32[2,58,16,128]{3,2,1,0:T(8,128)} %pad_maximum_fusion.1), channel_id=1, source_target_pairs={{1,0},{2,1},{3,2},{4,3},{5,4},{6,5},{7,6},{9,8},{10,9},{11,10},{12... | collective-permute-start | bytes 2850824 | tf_op jit(solution)/shard_map/ppermute | solution.py:223
  24.4 15.3 %collective-permute-start.3 = (f32[2,58,16,128]{3,2,1,0:T(8,128)}, f32[2,58,16,128]{3,2,1,0:T(8,128)S(1)}, u32[]{:S(2)}, u32[]{:S(2)}) collective-permute-start(f32[2,58,16,128]{3,2,1,0:T(8,128)} %pad_maximum_fusion.2), channel_id=1, source_target_pairs={{0,1},{1,2},{2,3},{3,4},{4,5},{5,6},{6,7},{8,9},{9,10},{10,11},{11... | collective-permute-start | bytes 2850824 | tf_op jit(solution)/shard_map/ppermute | solution.py:223
  30.2 9.5 %copy-start = (bf16[384,128]{1,0:T(8,128)(2,1)S(1)}, bf16[384,128]{1,0:T(8,128)(2,1)}, u32[]{:S(2)}) copy-start(bf16[384,128]{1,0:T(8,128)(2,1)} %get-tuple-element.12.depth_s) | copy-start | bytes 294916
  30.2 9.5 %copy-start.2 = (bf16[80,192]{1,0:T(8,128)(2,1)S(1)}, bf16[80,192]{1,0:T(8,128)(2,1)}, u32[]{:S(2)}) copy-start(bf16[80,192]{1,0:T(8,128)(2,1)} %get-tuple-element.10.along_x) | copy-start | bytes 92164
  30.2 9.5 %copy-start.3 = (bf16[80,192]{1,0:T(8,128)(2,1)S(1)}, bf16[80,192]{1,0:T(8,128)(2,1)}, u32[]{:S(2)}) copy-start(bf16[80,192]{1,0:T(8,128)(2,1)} %get-tuple-element.11.along_y) | copy-start | bytes 92164
  39.7 2.7 %copy-start.1 = (bf16[384,128]{1,0:T(8,128)(2,1)S(1)}, bf16[384,128]{1,0:T(8,128)(2,1)}, u32[]{:S(2)}) copy-start(bf16[384,128]{1,0:T(8,128)(2,1)} %get-tuple-element.13.depth_g) | copy-start | bytes 294916
  39.7 2.7 %copy-start.4 = (f32[2,32,128]{2,1,0:T(8,128)S(1)}, f32[2,32,128]{2,1,0:T(8,128)}, u32[]{:S(2)}) copy-start(f32[2,32,128]{2,1,0:T(8,128)} %get-tuple-element.14.gain) | copy-start | bytes 98308
  46.2 8.4 %collective-permute-start.5 = (f32[13,32,128]{2,1,0:T(8,128)S(1)}, f32[13,32,128]{2,1,0:T(8,128)S(1)}, u32[]{:S(2)}, u32[]{:S(2)}) collective-permute-start(f32[13,32,128]{2,1,0:T(8,128)S(1)} %get-tuple-element.21), channel_id=1, source_target_pairs={{0,8},{8,16},{16,24},{24,32},{32,40},{40,48},{48,56},{56,64},{64,7... | collective-permute-start | bytes 638984 | tf_op jit(solution)/shard_map/ppermute | solution.py:223
  48.1 10.5 %collective-permute-start.4 = (f32[13,32,128]{2,1,0:T(8,128)S(1)}, f32[13,32,128]{2,1,0:T(8,128)S(1)}, u32[]{:S(2)}, u32[]{:S(2)}) collective-permute-start(f32[13,32,128]{2,1,0:T(8,128)S(1)} %get-tuple-element.22), channel_id=1, source_target_pairs={{8,0},{16,8},{24,16},{32,24},{40,32},{48,40},{56,48},{64,56},{72,6... | collective-permute-start | bytes 638984 | tf_op jit(solution)/shard_map/ppermute | solution.py:223
  58.6 8.1 %collective-permute-start.6 = (f32[58,16,128]{2,1,0:T(8,128)S(1)}, f32[58,16,128]{2,1,0:T(8,128)S(1)}, u32[]{:S(2)}, u32[]{:S(2)}) collective-permute-start(f32[58,16,128]{2,1,0:T(8,128)S(1)} %pad_maximum_fusion.3), channel_id=1, source_target_pairs={{1,0},{2,1},{3,2},{4,3},{5,4},{6,5},{7,6},{9,8},{10,9},{11,10},{12... | collective-permute-start | bytes 1425416 | tf_op jit(solution)/shard_map/ppermute | solution.py:223
  60.6 10.0 %collective-permute-start.7 = (f32[58,16,128]{2,1,0:T(8,128)S(1)}, f32[58,16,128]{2,1,0:T(8,128)S(1)}, u32[]{:S(2)}, u32[]{:S(2)}) collective-permute-start(f32[58,16,128]{2,1,0:T(8,128)S(1)} %pad_maximum_fusion.4), channel_id=1, source_target_pairs={{0,1},{1,2},{2,3},{3,4},{4,5},{5,6},{6,7},{8,9},{9,10},{10,11},{11... | collective-permute-start | bytes 1425416 | tf_op jit(solution)/shard_map/ppermute | solution.py:223

commit v2 on v1

--- a/solution.py
+++ b/solution.py
@@ -91,19 +91,26 @@
         ),
         in_specs=[smem] * 5,
         out_specs=(vmem,) * 5,
+        cost_estimate=pl.CostEstimate(flops=1000000, bytes_accessed=1000000, transcendentals=0),
     )(smooth, slope, band, step, edges)
 
 
-def fill_extended(extended, own, x_next, x_prev, y_next, y_prev):
+def fill_extended(extended, edges, own, x_even, x_odd, y_even, y_odd, c_even, c_odd):
+    high = SIDE + REACH
     low = WIDE - REACH
-    high = SIDE + REACH
+    x_places = (jnp.where(edges[4] == 0, SIDE, low), jnp.where(edges[4] == 0, low, SIDE))
+    y_places = (
+        jnp.where(edges[5] == 0, SIDE, WIDE - SLAB), jnp.where(edges[5] == 0, WIDE - SLAB, SIDE)
+    )
     extended[0:SIDE, 0:SIDE, :] = own
-    extended[SIDE:high, 0:SIDE, :] = x_next
     extended[high:low, :, :] = jnp.zeros((low - high, WIDE, DEPTH), jnp.float32)
-    extended[low:WIDE, 0:SIDE, :] = x_prev
-    for start, slab in ((SIDE, y_next), (WIDE - SLAB, y_prev)):
-        extended[0:high, start : start + SLAB, :] = slab[0:high]
-        extended[low:WIDE, start : start + SLAB, :] = slab[high:SPAN]
+    for place, part in zip(x_places, (x_even, x_odd)):
+        extended[pl.ds(place, REACH), 0:SIDE, :] = part
+    for place, part, corner in zip(y_places, (y_even, y_odd), (c_even, c_odd)):
+        columns = pl.ds(pl.multiple_of(place, SLAB), SLAB)
+        extended[0:SIDE, columns, :] = part
+        for at, row in enumerate(x_places):
+            extended[pl.ds(row, REACH), columns, :] = corner[at * REACH : (at + 1) * REACH]
 
 
 def stacked_parts(value):
@@ -134,11 +141,7 @@
             crossed[y, :, :] = out[:, at * DEPTH : (at + 1) * DEPTH]
 
 
-def gradient_kernel(
-    own, x_next, x_prev, y_next, y_prev, along_x, along_y, depth_s, depth_g, speed, gain, out,
-    extended, crossed, flat_s, flat_g, normals, lengths,
-):
-    fill_extended(extended, own[...], x_next[...], x_prev[...], y_next[...], y_prev[...])
+def gradient_stages(extended, along_x, along_y, depth_s, depth_g, crossed, flat_s, flat_g, normals, lengths):
     along_x_stage(extended, crossed, along_x[...])
     matrix = along_y[...]
     for at, row in enumerate(OUT_ROWS):
@@ -170,6 +173,9 @@
             normals[1, at + half, :, :] = grad_y * inverse
             normals[2, at + half, :, :] = grad_z * inverse
             lengths[at + half, :, :] = square * inverse
+
+
+def advance(own, speed, gain, normals, lengths, out):
     lane = lax.broadcasted_iota(jnp.int32, (SIDE, DEPTH), 1)
     for x in range(SIDE):
         at = x + 1
@@ -183,13 +189,9 @@
         out[x, :, :] = own[x, :, :] - push * (speed[x, :, :] - 0.25 * bend)
 
 
-def speed_kernel(
-    own, x_next, x_prev, y_next, y_prev, along_x, along_y, depth_s, out,
-    extended, crossed, flat_s, velocity,
-):
-    fill_extended(extended, own[...], x_next[...], x_prev[...], y_next[...], y_prev[...])
-    along_x_stage(extended, crossed, along_x[0:RIM + 8, :])
-    matrix = along_y[0:RIM + 8, :]
+def speed_stages(extended, along_x, along_y, depth_s, crossed, flat_s, velocity, out):
+    along_x_stage(extended, crossed, along_x[0 : RIM + 8, :])
+    matrix = along_y[0 : RIM + 8, :]
     for pair in range(0, len(OUT_ROWS), 2):
         value = jnp.concatenate(
             [take_place(crossed, row) for row in OUT_ROWS[pair : pair + 2]], axis=1
@@ -216,70 +218,110 @@
         out[x, :, :] = total / 7.0
 
 
-def neighbours(forward_block, backward_block, axis):
-    count = lax.axis_size(axis)
-    forward = [(i, i + 1) for i in range(count - 1)]
-    backward = [(target, source) for source, target in forward]
-    return lax.ppermute(backward_block, axis, backward), lax.ppermute(forward_block, axis, forward)
-
-
-def gather_halos(block):
-    x_next, x_prev = neighbours(block[..., SIDE - REACH :, :, :], block[..., :REACH, :, :], "gx")
-
-    def slab(low, high):
-        return jnp.concatenate(
-            [part[..., low:high, :] for part in (block, x_next, x_prev)], axis=-3
-        )
-
-    y_next, y_prev = neighbours(slab(SIDE - SLAB, SIDE), slab(0, SLAB), "gy")
-    return block, x_next, x_prev, y_next, y_prev
-
-
-def call_kernel(body, fields, others, field, scratch):
-    def whole(array):
-        return pl.BlockSpec(array.shape, lambda i, rank=array.ndim: (0,) * rank)
-
-    def one(array):
-        if array.ndim == 3:
-            return whole(array)
-        return pl.BlockSpec((None,) + array.shape[1:], lambda i: (field, 0, 0, 0))
-
+HALOS = 6
+
+
+def first_kernel(edges, own_s, own, *refs):
+    halos = refs[:HALOS]
+    along_x, along_y, depth_s, depth_g, gain, out, speed = refs[HALOS : HALOS + 7]
+    extended_s, crossed_s, flat_v, velocity = refs[HALOS + 7 : HALOS + 11]
+    extended, crossed, flat_s, flat_g, normals, lengths = refs[HALOS + 11 :]
+    fill_extended(extended_s, edges, own_s[...], *[halo[0] for halo in halos])
+    fill_extended(extended, edges, own[...], *[halo[1] for halo in halos])
+    speed_stages(extended_s, along_x, along_y, depth_s, crossed_s, flat_v, velocity, speed)
+    gradient_stages(
+        extended, along_x, along_y, depth_s, depth_g, crossed, flat_s, flat_g, normals, lengths
+    )
+    advance(own, speed, gain, normals, lengths, out)
+
+
+def later_kernel(edges, own, *refs):
+    halos = refs[:HALOS]
+    along_x, along_y, depth_s, depth_g, gain, speed, out = refs[HALOS : HALOS + 7]
+    extended, crossed, flat_s, flat_g, normals, lengths = refs[HALOS + 7 :]
+    fill_extended(extended, edges, own[...], *[halo[...] for halo in halos])
+    gradient_stages(
+        extended, along_x, along_y, depth_s, depth_g, crossed, flat_s, flat_g, normals, lengths
+    )
+    advance(own, speed, gain, normals, lengths, out)
+
+
+def call_kernel(body, edges, arrays, outputs, scratch):
+    smem = pl.BlockSpec(memory_space=pltpu.SMEM)
+    vmem = pl.BlockSpec(memory_space=pltpu.VMEM)
+    shape = jax.ShapeDtypeStruct((SIDE, SIDE, DEPTH), jnp.float32)
     return pl.pallas_call(
         body,
-        grid=(1,),
-        out_shape=jax.ShapeDtypeStruct((SIDE, SIDE, DEPTH), jnp.float32),
-        in_specs=[one(f) for f in fields] + [whole(o) for o in others],
-        out_specs=pl.BlockSpec((SIDE, SIDE, DEPTH), lambda i: (0, 0, 0)),
+        out_shape=(shape,) * outputs,
+        in_specs=[smem] + [vmem] * len(arrays),
+        out_specs=(vmem,) * outputs,
         scratch_shapes=[pltpu.VMEM(shape, jnp.float32) for shape in scratch],
         compiler_params=pltpu.CompilerParams(vmem_limit_bytes=48 * 1024 * 1024),
-    )(*fields, *others)
+    )(edges, *arrays)
+
+
+def swap(block, axis, first):
+    pairs = []
+    for low in range(first, lax.axis_size(axis) - 1, 2):
+        pairs += [(low, low + 1), (low + 1, low)]
+    return lax.ppermute(block, axis, pairs)
+
+
+def side_pieces(blocks, dim, width, parity):
+    even, odd = [], []
+    for block in blocks:
+        length = block.shape[dim]
+        even.append(
+            lax.dynamic_slice_in_dim(block, jnp.where(parity == 0, length - width, 0), width, dim)
+        )
+        odd.append(
+            lax.dynamic_slice_in_dim(block, jnp.where(parity == 0, 0, length - width), width, dim)
+        )
+    if len(blocks) == 1:
+        return even[0], odd[0]
+    return jnp.stack(even), jnp.stack(odd)
+
+
+def gather_halos(blocks, parity_x, parity_y):
+    even, odd = side_pieces(blocks, 0, REACH, parity_x)
+    x_even = swap(even, "gx", 0)
+    x_odd = swap(odd, "gx", 1)
+    even, odd = side_pieces(blocks, 1, SLAB, parity_y)
+    y_even = swap(even, "gy", 0)
+    y_odd = swap(odd, "gy", 1)
+    edge = jnp.concatenate([x_even, x_odd], axis=-3)
+    even, odd = side_pieces([edge], edge.ndim - 2, SLAB, parity_y)
+    return x_even, x_odd, y_even, y_odd, swap(even, "gy", 0), swap(odd, "gy", 1)
 
 
 def per_device(level_set, sensitivity, smooth_taps, slope_taps, band, time_step):
-    edges = []
+    edges, parity = [], []
     for axis in ("gx", "gy"):
         at = lax.axis_index(axis)
         edges += [at > 0, at < lax.axis_size(axis) - 1]
-    edges = jnp.stack(edges).astype(jnp.int32)
+        parity.append(at & 1)
+    edges = jnp.stack([jnp.int32(e) for e in edges] + parity)
     along_x, along_y, depth_s, depth_g, gain = prepare(
         smooth_taps, slope_taps, band, time_step, edges
     )
-    fields = gather_halos(jnp.stack([sensitivity, level_set]))
+    matrices = (along_x, along_y, depth_s, depth_g, gain)
     rim = SIDE + 2
-    speed = call_kernel(
-        speed_kernel, fields, (along_x, along_y, depth_s), 0,
-        [(WIDE, WIDE, DEPTH), (WIDE, RIM + 8, DEPTH), (rim, RIM, DEPTH), (rim, RIM, DEPTH)],
-    )
-    phi = level_set
-    for update in range(UPDATES):
-        if update > 0:
-            fields = gather_halos(phi)
-        phi = call_kernel(
-            gradient_kernel, fields, (along_x, along_y, depth_s, depth_g, speed, gain), 1,
-            [
-                (WIDE, WIDE, DEPTH), (WIDE, 2 * RIM, DEPTH), (rim, 2 * RIM, DEPTH),
-                (rim, RIM, DEPTH), (3, rim, RIM, DEPTH), (rim, RIM, DEPTH),
-            ],
+    gradient_scratch = [
+        (WIDE, WIDE, DEPTH), (WIDE, 2 * RIM, DEPTH), (rim, 2 * RIM, DEPTH),
+        (rim, RIM, DEPTH), (3, rim, RIM, DEPTH), (rim, RIM, DEPTH),
+    ]
+    speed_scratch = [
+        (WIDE, WIDE, DEPTH), (WIDE, RIM + 8, DEPTH), (rim, RIM, DEPTH), (rim, RIM, DEPTH)
+    ]
+    halos = gather_halos([sensitivity, level_set], *parity)
+    phi, speed = call_kernel(
+        first_kernel, edges, (sensitivity, level_set, *halos, *matrices), 2,
+        speed_scratch + gradient_scratch,
+    )
+    for _ in range(1, UPDATES):
+        halos = gather_halos([phi], *parity)
+        (phi,) = call_kernel(
+            later_kernel, edges, (phi, *halos, *matrices, speed), 1, gradient_scratch
         )
     return phi
 

time: 75.4 us -> 66.5 us (0.88)
  the two profiles are of different devices: /device:TPU:14 before, /device:TPU:41 now
where the time goes in v2:
time: 66.5 us; the launch traced here: 65.9 us
  starting transfers between devices  25.5 us (38%)
  waiting for transfers between devices  14.6 us (22%)
  Pallas kernels  14.5 us (22%)
  local copies, waits for them, and re-layouts  7.94 us (12%)
  other arithmetic  2.49 us (4%)
  between operations  0.91 us (1%)
    ppermute x12, starting transfers between devices, swap(): return lax.ppermute(block, axis, pairs)  25.5 us
    ppermute x12, waiting for transfers between devices, swap(): return lax.ppermute(block, axis, pairs)  14.6 us
    pallas_call x2, Pallas kernels, call_kernel(): pl.pallas_call(body, out_shape=(shape,) * outputs, in_specs=[smem] + [vme...  12.4 us
    unnamed x18, local copies, waits for them, and re-layouts  4.75 us
    another operation x4, other arithmetic, side_pieces(): return (jnp.stack(even), jnp.stack(odd))  2.49 us
    pallas_call x1, Pallas kernels, prepare(): pl.pallas_call(prepare_kernel, out_shape=(jax.ShapeDtypeStruct((2 * RIM,...  2.1 us
    another operation x2, local copies, waits for them, and re-layouts, side_pieces(): return (jnp.stack(even), jnp.stack(odd))  1.42 us
  transfers between devices with their start and end apart: 12, of which 4 were waited for; matrix products, arithmetic and copies ran while one was open for 7% of the time, Pallas kernels for 3%

profile of v2, /device:TPU:41, one launch (start us, length us, event | category | flops | bytes accessed | tf_op | source)
XLA Modules:
  0.0 65.9 jit_solution(16146518949132084965)
XLA Ops:
  0.0 1.3 %dynamic-slice_bitcast_fusion.4 = (f32[1,13,32,128]{3,2,1,0:T(8,128)S(1)}, f32[1,13,32,128]{3,2,1,0:T(8,128)S(1)}, f32[1,13,32,128]{3,2,1,0:T(8,128)S(1)}, f32[1,13,32,128]{3,2,1,0:T(8,128)S(1)}) fusion(f32[32,32,128]{2,1,0:T(8,128)} %own.1, s32[]{:T(128)S(6)} %select_n.42, s32[]{:T(128)S(6)} %select_n.41, f32[32,32,128]{2,1,0:T(8,128)} %own_s.1), kind=kLoop, calls=%fused_computation.8 | loop fusion | bytes 1703944 | tf_op jit(solution)/shard_map/stack | solution.py:282
  1.4 1.3 %collective-permute-start = (f32[2,13,32,128]{3,2,1,0:T(8,128)S(1)}, f32[2,13,32,128]{3,2,1,0:T(8,128)S(1)}, u32[]{:S(2)}, u32[]{:S(2)}) collective-permute-start(f32[2,13,32,128]{3,2,1,0:T(8,128)S(1)} %pad_maximum_fusion.2), channel_id=1, source_target_pairs={{0,8},{8,0},{16,24},{24,16},{32,40},{40,32},{48,56},{56,48},{64,72... | collective-permute-start | bytes 1277960 | tf_op jit(solution)/shard_map/ppermute | solution.py:267
  2.7 0.8 %pad_maximum_fusion.3 = f32[2,13,32,128]{3,2,1,0:T(8,128)} fusion(f32[1,13,32,128]{3,2,1,0:T(8,128)S(1)} %get-tuple-element.31, f32[1,13,32,128]{3,2,1,0:T(8,128)S(1)} %get-tuple-element.36), kind=kLoop, calls=%fused_computation.3 | loop fusion | flops 106496 | bytes 851968 | tf_op jit(solution)/shard_map/stack | solution.py:282
  3.5 3.3 %collective-permute-start.1 = (f32[2,13,32,128]{3,2,1,0:T(8,128)}, f32[2,13,32,128]{3,2,1,0:T(8,128)S(1)}, u32[]{:S(2)}, u32[]{:S(2)}) collective-permute-start(f32[2,13,32,128]{3,2,1,0:T(8,128)} %pad_maximum_fusion.3), channel_id=1, source_target_pairs={{8,16},{16,8},{24,32},{32,24},{40,48},{48,40},{56,64},{64,56},{72,... | collective-permute-start | bytes 1277960 | tf_op jit(solution)/shard_map/ppermute | solution.py:267
  6.9 0.8 %pad_maximum_fusion = f32[2,32,16,128]{3,2,1,0:T(8,128)} fusion(f32[1,32,16,128]{3,2,1,0:T(8,128)S(1)} %get-tuple-element.28, f32[1,32,16,128]{3,2,1,0:T(8,128)S(1)} %get-tuple-element.37), kind=kLoop, calls=%fused_computation | loop fusion | flops 131072 | bytes 1048576 | tf_op jit(solution)/shard_map/stack | solution.py:282
  7.7 1.2 %collective-permute-start.2 = (f32[2,32,16,128]{3,2,1,0:T(8,128)}, f32[2,32,16,128]{3,2,1,0:T(8,128)S(1)}, u32[]{:S(2)}, u32[]{:S(2)}) collective-permute-start(f32[2,32,16,128]{3,2,1,0:T(8,128)} %pad_maximum_fusion), channel_id=1, source_target_pairs={{0,1},{1,0},{2,3},{3,2},{4,5},{5,4},{6,7},{7,6},{8,9},{9,8},{10,11... | collective-permute-start | bytes 1572872 | tf_op jit(solution)/shard_map/ppermute | solution.py:267
  8.9 0.8 %pad_maximum_fusion.1 = f32[2,32,16,128]{3,2,1,0:T(8,128)} fusion(f32[1,32,16,128]{3,2,1,0:T(8,128)S(1)} %get-tuple-element.27, f32[1,32,16,128]{3,2,1,0:T(8,128)S(1)} %get-tuple-element.38), kind=kLoop, calls=%fused_computation.1 | loop fusion | flops 131072 | bytes 1048576 | tf_op jit(solution)/shard_map/stack | solution.py:282
  9.8 3.1 %collective-permute-start.3 = (f32[2,32,16,128]{3,2,1,0:T(8,128)}, f32[2,32,16,128]{3,2,1,0:T(8,128)S(1)}, u32[]{:S(2)}, u32[]{:S(2)}) collective-permute-start(f32[2,32,16,128]{3,2,1,0:T(8,128)} %pad_maximum_fusion.1), channel_id=1, source_target_pairs={{1,2},{2,1},{3,4},{4,3},{5,6},{6,5},{9,10},{10,9},{11,12},{12,11},... | collective-permute-start | bytes 1572872 | tf_op jit(solution)/shard_map/ppermute | solution.py:267
  12.9 5.1 %collective-permute-done.1.refs_1_ = f32[2,13,32,128]{3,2,1,0:T(8,128)S(1)} collective-permute-done((f32[2,13,32,128]{3,2,1,0:T(8,128)}, f32[2,13,32,128]{3,2,1,0:T(8,128)S(1)}, u32[]{:S(2)}, u32[]{:S(2)}) %collective-permute-start.1) | collective-permute-done | bytes 426016 | tf_op jit(solution)/shard_map/ppermute | solution.py:267
  18.1 1.0 %constant_dynamic-slice_fusion.6 = (f32[2,26,16,128]{3,2,1,0:T(8,128)}, f32[2,26,16,128]{3,2,1,0:T(8,128)}) fusion(f32[2,26,32,128]{3,2,1,0:T(8,128)S(1)} %constant_dynamic-update-slice_fusion, s32[]{:T(128)S(6)} %select_n.44, s32[]{:T(128)S(6)} %select_n.43), kind=kLoop, calls=%fused_computation.22 | loop fusion | bytes 1703944 | tf_op jit(solution)/shard_map/dynamic_slice | solution.py:278
  19.1 4.9 %collective-permute-start.5 = (f32[2,26,16,128]{3,2,1,0:T(8,128)}, f32[2,26,16,128]{3,2,1,0:T(8,128)S(1)}, u32[]{:S(2)}, u32[]{:S(2)}) collective-permute-start(f32[2,26,16,128]{3,2,1,0:T(8,128)} %get-tuple-element.19), channel_id=1, source_target_pairs={{1,2},{2,1},{3,4},{4,3},{5,6},{6,5},{9,10},{10,9},{11,12},{12,11},... | collective-permute-start | bytes 1277960 | tf_op jit(solution)/shard_map/ppermute | solution.py:267
  25.4 2.1 %shard_map.64 = (bf16[80,192]{1,0:T(8,128)(2,1)}, bf16[80,192]{1,0:T(8,128)(2,1)}, bf16[384,128]{1,0:T(8,128)(2,1)}, bf16[384,128]{1,0:T(8,128)(2,1)}, f32[2,32,128]{2,1,0:T(8,128)}) custom-call(f32[25]{0:T(128)} %smooth.1, f32[25]{0:T(128)} %slope.1, s32[2,2,4]{2,1,0:T(2,128)} %band.1, f32[1]{0:T(128)S(6)} %copy.9.step, s32[6]{0:T(128)} %stack.79.edges), custom_call_target="tpu_custom_call" | custom-call | flops 1000000 | bytes 1000000 | tf_op jit(solution)/shard_map/pallas_call | solution.py:83
  27.5 2.7 %collective-permute-done.5.refs_5_ = f32[2,26,16,128]{3,2,1,0:T(8,128)S(1)} collective-permute-done((f32[2,26,16,128]{3,2,1,0:T(8,128)}, f32[2,26,16,128]{3,2,1,0:T(8,128)S(1)}, u32[]{:S(2)}, u32[]{:S(2)}) %collective-permute-start.5) | collective-permute-done | bytes 426016 | tf_op jit(solution)/shard_map/ppermute | solution.py:267
  30.8 0.9 %copy-done.2 = bf16[384,128]{1,0:T(8,128)(2,1)S(1)} copy-done((bf16[384,128]{1,0:T(8,128)(2,1)S(1)}, bf16[384,128]{1,0:T(8,128)(2,1)}, u32[]{:S(2)}) %copy-start.2) | copy-done | bytes 98328
  31.7 0.9 %copy-done.3 = bf16[384,128]{1,0:T(8,128)(2,1)S(1)} copy-done((bf16[384,128]{1,0:T(8,128)(2,1)S(1)}, bf16[384,128]{1,0:T(8,128)(2,1)}, u32[]{:S(2)}) %copy-start.3) | copy-done | bytes 98328
  32.6 0.8 %copy-done.4 = bf16[80,192]{1,0:T(8,128)(2,1)S(1)} copy-done((bf16[80,192]{1,0:T(8,128)(2,1)S(1)}, bf16[80,192]{1,0:T(8,128)(2,1)}, u32[]{:S(2)}) %copy-start.4) | copy-done | bytes 30744
  33.4 0.8 %copy-done.5 = bf16[80,192]{1,0:T(8,128)(2,1)S(1)} copy-done((bf16[80,192]{1,0:T(8,128)(2,1)S(1)}, bf16[80,192]{1,0:T(8,128)(2,1)}, u32[]{:S(2)}) %copy-start.5) | copy-done | bytes 30744
  34.9 7.2 %shard_map.65 = (f32[32,32,128]{2,1,0:T(8,128)S(1)}, f32[32,32,128]{2,1,0:T(8,128)S(1)}) custom-call(s32[6]{0:T(128)S(1)} %copy-done.7, f32[32,32,128]{2,1,0:T(8,128)S(1)} %copy-done, f32[32,32,128]{2,1,0:T(8,128)S(1)} %copy-done.1, f32[2,13,32,128]{3,2,1,0:T(8,128)S(1)} %collective-permute-done.refs_0_, ...), custom_call_target="tpu_custom_call" | custom-call | tf_op jit(solution)/shard_map/pallas_call | solution.py:253
  42.3 3.3 %collective-permute-start.7 = (f32[13,32,128]{2,1,0:T(8,128)S(1)}, f32[13,32,128]{2,1,0:T(8,128)S(1)}, u32[]{:S(2)}, u32[]{:S(2)}) collective-permute-start(f32[13,32,128]{2,1,0:T(8,128)S(1)} %get-tuple-element.23), channel_id=1, source_target_pairs={{8,16},{16,8},{24,32},{32,24},{40,48},{48,40},{56,64},{64,56},{72,... | collective-permute-start | bytes 638984 | tf_op jit(solution)/shard_map/ppermute | solution.py:267
  45.6 3.7 %collective-permute-start.9 = (f32[32,16,128]{2,1,0:T(8,128)S(1)}, f32[32,16,128]{2,1,0:T(8,128)S(1)}, u32[]{:S(2)}, u32[]{:S(2)}) collective-permute-start(f32[32,16,128]{2,1,0:T(8,128)S(1)} %get-tuple-element.21), channel_id=1, source_target_pairs={{1,2},{2,1},{3,4},{4,3},{5,6},{6,5},{9,10},{10,9},{11,12},{12,11},... | collective-permute-start | bytes 786440 | tf_op jit(solution)/shard_map/ppermute | solution.py:267
  49.5 3.2 %collective-permute-done.7.refs_1_ = f32[13,32,128]{2,1,0:T(8,128)S(1)} collective-permute-done((f32[13,32,128]{2,1,0:T(8,128)S(1)}, f32[13,32,128]{2,1,0:T(8,128)S(1)}, u32[]{:S(2)}, u32[]{:S(2)}) %collective-permute-start.7) | collective-permute-done | bytes 213024 | tf_op jit(solution)/shard_map/ppermute | solution.py:267
  52.8 4.1 %collective-permute-start.11 = (f32[26,16,128]{2,1,0:T(8,128)S(1)}, f32[26,16,128]{2,1,0:T(8,128)S(1)}, u32[]{:S(2)}, u32[]{:S(2)}) collective-permute-start(f32[26,16,128]{2,1,0:T(8,128)S(1)} %get-tuple-element.33), channel_id=1, source_target_pairs={{1,2},{2,1},{3,4},{4,3},{5,6},{6,5},{9,10},{10,9},{11,12},{12,11},... | collective-permute-start | bytes 638984 | tf_op jit(solution)/shard_map/ppermute | solution.py:267
  57.2 3.5 %collective-permute-done.11.refs_5_ = f32[26,16,128]{2,1,0:T(8,128)S(1)} collective-permute-done((f32[26,16,128]{2,1,0:T(8,128)S(1)}, f32[26,16,128]{2,1,0:T(8,128)S(1)}, u32[]{:S(2)}, u32[]{:S(2)}) %collective-permute-start.11) | collective-permute-done | bytes 213024 | tf_op jit(solution)/shard_map/ppermute | solution.py:267
  60.8 5.2 %shard_map.66 = f32[32,32,128]{2,1,0:T(8,128)} custom-call(s32[6]{0:T(128)S(1)} %copy-done.7, f32[32,32,128]{2,1,0:T(8,128)S(1)} %get-tuple-element.17.own, f32[13,32,128]{2,1,0:T(8,128)S(1)} %collective-permute-done.6.refs_0_, f32[13,32,128]{2,1,0:T(8,128)S(1)} %collective-permute-done.7.refs_1_, f32[32,16,128]{2,1,0:T(8,128)S(1)} %collective-permute-done.8.refs_2_, ...), custom_call_target="tpu_custom_call" | custom-call | tf_op jit(solution)/shard_map/pallas_call | solution.py:253
  (34 shorter events, 2.9 us)
Async XLA Ops:
  1.3 5.4 %copy-start.1 = (f32[32,32,128]{2,1,0:T(8,128)S(1)}, f32[32,32,128]{2,1,0:T(8,128)}, u32[]{:S(2)}) copy-start(f32[32,32,128]{2,1,0:T(8,128)} %own.1) | copy-start | bytes 1572868
  1.4 5.4 %copy-start = (f32[32,32,128]{2,1,0:T(8,128)S(1)}, f32[32,32,128]{2,1,0:T(8,128)}, u32[]{:S(2)}) copy-start(f32[32,32,128]{2,1,0:T(8,128)} %own_s.1) | copy-start | bytes 1572868
  1.4 11.5 %collective-permute-start = (f32[2,13,32,128]{3,2,1,0:T(8,128)S(1)}, f32[2,13,32,128]{3,2,1,0:T(8,128)S(1)}, u32[]{:S(2)}, u32[]{:S(2)}) collective-permute-start(f32[2,13,32,128]{3,2,1,0:T(8,128)S(1)} %pad_maximum_fusion.2), channel_id=1, source_target_pairs={{0,8},{8,0},{16,24},{24,16},{32,40},{40,32},{48,56},{56,48},{64,72... | collective-permute-start | bytes 1277960 | tf_op jit(solution)/shard_map/ppermute | solution.py:267
  3.5 14.6 %collective-permute-start.1 = (f32[2,13,32,128]{3,2,1,0:T(8,128)}, f32[2,13,32,128]{3,2,1,0:T(8,128)S(1)}, u32[]{:S(2)}, u32[]{:S(2)}) collective-permute-start(f32[2,13,32,128]{3,2,1,0:T(8,128)} %pad_maximum_fusion.3), channel_id=1, source_target_pairs={{8,16},{16,8},{24,32},{32,24},{40,48},{48,40},{56,64},{64,56},{72,... | collective-permute-start | bytes 1277960 | tf_op jit(solution)/shard_map/ppermute | solution.py:267
  7.7 19.8 %collective-permute-start.2 = (f32[2,32,16,128]{3,2,1,0:T(8,128)}, f32[2,32,16,128]{3,2,1,0:T(8,128)S(1)}, u32[]{:S(2)}, u32[]{:S(2)}) collective-permute-start(f32[2,32,16,128]{3,2,1,0:T(8,128)} %pad_maximum_fusion), channel_id=1, source_target_pairs={{0,1},{1,0},{2,3},{3,2},{4,5},{5,4},{6,7},{7,6},{8,9},{9,8},{10,11... | collective-permute-start | bytes 1572872 | tf_op jit(solution)/shard_map/ppermute | solution.py:267
  9.8 17.7 %collective-permute-start.3 = (f32[2,32,16,128]{3,2,1,0:T(8,128)}, f32[2,32,16,128]{3,2,1,0:T(8,128)S(1)}, u32[]{:S(2)}, u32[]{:S(2)}) collective-permute-start(f32[2,32,16,128]{3,2,1,0:T(8,128)} %pad_maximum_fusion.1), channel_id=1, source_target_pairs={{1,2},{2,1},{3,4},{4,3},{5,6},{6,5},{9,10},{10,9},{11,12},{12,11},... | collective-permute-start | bytes 1572872 | tf_op jit(solution)/shard_map/ppermute | solution.py:267
  19.1 11.1 %collective-permute-start.5 = (f32[2,26,16,128]{3,2,1,0:T(8,128)}, f32[2,26,16,128]{3,2,1,0:T(8,128)S(1)}, u32[]{:S(2)}, u32[]{:S(2)}) collective-permute-start(f32[2,26,16,128]{3,2,1,0:T(8,128)} %get-tuple-element.19), channel_id=1, source_target_pairs={{1,2},{2,1},{3,4},{4,3},{5,6},{6,5},{9,10},{10,9},{11,12},{12,11},... | collective-permute-start | bytes 1277960 | tf_op jit(solution)/shard_map/ppermute | solution.py:267
  24.0 6.2 %collective-permute-start.4 = (f32[2,26,16,128]{3,2,1,0:T(8,128)}, f32[2,26,16,128]{3,2,1,0:T(8,128)}, u32[]{:S(2)}, u32[]{:S(2)}) collective-permute-start(f32[2,26,16,128]{3,2,1,0:T(8,128)} %get-tuple-element.20), channel_id=1, source_target_pairs={{0,1},{1,0},{2,3},{3,2},{4,5},{5,4},{6,7},{7,6},{8,9},{9,8},{10,11... | collective-permute-start | bytes 1277960 | tf_op jit(solution)/shard_map/ppermute | solution.py:267
  30.2 0.6 copy-start.7
  30.8 0.9 %copy-start.2 = (bf16[384,128]{1,0:T(8,128)(2,1)S(1)}, bf16[384,128]{1,0:T(8,128)(2,1)}, u32[]{:S(2)}) copy-start(bf16[384,128]{1,0:T(8,128)(2,1)} %get-tuple-element.14.refs_8_) | copy-start | bytes 294916
  31.7 0.9 %copy-start.3 = (bf16[384,128]{1,0:T(8,128)(2,1)S(1)}, bf16[384,128]{1,0:T(8,128)(2,1)}, u32[]{:S(2)}) copy-start(bf16[384,128]{1,0:T(8,128)(2,1)} %get-tuple-element.15.refs_9_) | copy-start | bytes 294916
  32.6 0.8 %copy-start.4 = (bf16[80,192]{1,0:T(8,128)(2,1)S(1)}, bf16[80,192]{1,0:T(8,128)(2,1)}, u32[]{:S(2)}) copy-start(bf16[80,192]{1,0:T(8,128)(2,1)} %get-tuple-element.12.refs_6_) | copy-start | bytes 92164
  33.4 0.8 %copy-start.5 = (bf16[80,192]{1,0:T(8,128)(2,1)S(1)}, bf16[80,192]{1,0:T(8,128)(2,1)}, u32[]{:S(2)}) copy-start(bf16[80,192]{1,0:T(8,128)(2,1)} %get-tuple-element.13.refs_7_) | copy-start | bytes 92164
  34.1 0.8 %copy-start.6 = (f32[2,32,128]{2,1,0:T(8,128)S(1)}, f32[2,32,128]{2,1,0:T(8,128)}, u32[]{:S(2)}) copy-start(f32[2,32,128]{2,1,0:T(8,128)} %get-tuple-element.16.refs_10_) | copy-start | bytes 98308
  42.2 7.3 %collective-permute-start.6 = (f32[13,32,128]{2,1,0:T(8,128)S(1)}, f32[13,32,128]{2,1,0:T(8,128)S(1)}, u32[]{:S(2)}, u32[]{:S(2)}) collective-permute-start(f32[13,32,128]{2,1,0:T(8,128)S(1)} %get-tuple-element.24), channel_id=1, source_target_pairs={{0,8},{8,0},{16,24},{24,16},{32,40},{40,32},{48,56},{56,48},{64,72... | collective-permute-start | bytes 638984 | tf_op jit(solution)/shard_map/ppermute | solution.py:267
  42.3 10.5 %collective-permute-start.7 = (f32[13,32,128]{2,1,0:T(8,128)S(1)}, f32[13,32,128]{2,1,0:T(8,128)S(1)}, u32[]{:S(2)}, u32[]{:S(2)}) collective-permute-start(f32[13,32,128]{2,1,0:T(8,128)S(1)} %get-tuple-element.23), channel_id=1, source_target_pairs={{8,16},{16,8},{24,32},{32,24},{40,48},{48,40},{56,64},{64,56},{72,... | collective-permute-start | bytes 638984 | tf_op jit(solution)/shard_map/ppermute | solution.py:267
  45.6 11.6 %collective-permute-start.9 = (f32[32,16,128]{2,1,0:T(8,128)S(1)}, f32[32,16,128]{2,1,0:T(8,128)S(1)}, u32[]{:S(2)}, u32[]{:S(2)}) collective-permute-start(f32[32,16,128]{2,1,0:T(8,128)S(1)} %get-tuple-element.21), channel_id=1, source_target_pairs={{1,2},{2,1},{3,4},{4,3},{5,6},{6,5},{9,10},{10,9},{11,12},{12,11},... | collective-permute-start | bytes 786440 | tf_op jit(solution)/shard_map/ppermute | solution.py:267
  49.4 7.9 %collective-permute-start.8 = (f32[32,16,128]{2,1,0:T(8,128)S(1)}, f32[32,16,128]{2,1,0:T(8,128)S(1)}, u32[]{:S(2)}, u32[]{:S(2)}) collective-permute-start(f32[32,16,128]{2,1,0:T(8,128)S(1)} %get-tuple-element.22), channel_id=1, source_target_pairs={{0,1},{1,0},{2,3},{3,2},{4,5},{5,4},{6,7},{7,6},{8,9},{9,8},{10,11... | collective-permute-start | bytes 786440 | tf_op jit(solution)/shard_map/ppermute | solution.py:267
  52.8 8.0 %collective-permute-start.11 = (f32[26,16,128]{2,1,0:T(8,128)S(1)}, f32[26,16,128]{2,1,0:T(8,128)S(1)}, u32[]{:S(2)}, u32[]{:S(2)}) collective-permute-start(f32[26,16,128]{2,1,0:T(8,128)S(1)} %get-tuple-element.33), channel_id=1, source_target_pairs={{1,2},{2,1},{3,4},{4,3},{5,6},{6,5},{9,10},{10,9},{11,12},{12,11},... | collective-permute-start | bytes 638984 | tf_op jit(solution)/shard_map/ppermute | solution.py:267
  56.9 3.8 %collective-permute-start.10 = (f32[26,16,128]{2,1,0:T(8,128)S(1)}, f32[26,16,128]{2,1,0:T(8,128)S(1)}, u32[]{:S(2)}, u32[]{:S(2)}) collective-permute-start(f32[26,16,128]{2,1,0:T(8,128)S(1)} %get-tuple-element.34), channel_id=1, source_target_pairs={{0,1},{1,0},{2,3},{3,2},{4,5},{5,4},{6,7},{7,6},{8,9},{9,8},{10,11... | collective-permute-start | bytes 638984 | tf_op jit(solution)/shard_map/ppermute | solution.py:267

commit v3 on v2

v3 whole, which is shorter than its diff:
```python
import functools

import jax
import jax.numpy as jnp
from jax import lax
from jax.experimental import pallas as pl
from jax.experimental.pallas import tpu as pltpu
from jax.sharding import PartitionSpec as P

UPDATES = 2
REACH = 13
SLAB = 16
SIDE = 32
RIM = 40
WIDE = 64
DEPTH = 128
TAPS = 25

OUT_ROWS = [RIM - 1] + list(range(SIDE + 1))


def split_rows(value):
    high = value.astype(jnp.bfloat16)
    low = (value - high.astype(jnp.float32)).astype(jnp.bfloat16)
    return high, low


def tap_select(index, taps):
    total = jnp.zeros(index.shape, jnp.float32)
    for k in range(TAPS):
        total = jnp.where(index == k, taps[k], total)
    return total


def side_matrix(axis, smooth, slope):
    at = lax.axis_index(axis)
    last = lax.axis_size(axis) - 1
    shape = (RIM, 3 * WIDE)
    row = lax.broadcasted_iota(jnp.int32, shape, 0)
    column = lax.broadcasted_iota(jnp.int32, shape, 1)
    place = column & (WIDE - 1)
    width = REACH if axis == "gx" else SLAB
    source = place
    for slot, side in ((0, at & 1), (1, 1 - (at & 1))):
        start = SIDE + slot * SLAB
        moved = place - start + jnp.where(side == 0, SIDE, -width)
        source = jnp.where((place >= start) & (place < start + SLAB), moved, source)
        source = jnp.where((place >= start + width) & (place < start + SLAB), -WIDE, source)
    target = jnp.where(row < RIM - 1, row, -1)
    index = source - target + TAPS // 2
    inside = (row < SIDE) | ((row == SIDE) & (at < last)) | ((row == RIM - 1) & (at > 0))
    index = jnp.where(inside, index, -1)
    parts = []
    for taps in (smooth, slope):
        full = tap_select(index, taps)
        high = full.astype(jnp.bfloat16).astype(jnp.float32)
        parts.append(jnp.where(column < 2 * WIDE, high, full - high))
    return jnp.concatenate(parts, axis=0).astype(jnp.bfloat16)


def block_gain(band, step, p):
    blocks_y, blocks_z = 2, 4
    rows = SIDE // blocks_y
    lane = lax.broadcasted_iota(jnp.int32, (rows, DEPTH), 1) // (DEPTH // blocks_z)
    parts = []
    for q in range(blocks_y):
        value = jnp.zeros(lane.shape, jnp.float32)
        for r in range(blocks_z):
            entry = band[p, q, r].astype(jnp.float32) * step[0]
            value = jnp.where(lane == r, entry, value)
        parts.append(value)
    return jnp.concatenate(parts, axis=0)


def prepare_kernel(smooth, slope, band, step, out, gain):
    for p in range(2):
        gain[p, :, :] = block_gain(band, step, p)
    for at, axis in enumerate(("gx", "gy")):
        out[2 * at * RIM : 2 * (at + 1) * RIM, 0 : 3 * WIDE] = side_matrix(axis, smooth, slope)
        out[2 * at * RIM : 2 * (at + 1) * RIM, 3 * WIDE :] = jnp.zeros((2 * RIM, WIDE), jnp.bfloat16)
    shape = (DEPTH, DEPTH)
    index = (
        lax.broadcasted_iota(jnp.int32, shape, 0)
        - lax.broadcasted_iota(jnp.int32, shape, 1)
        + TAPS // 2
    )
    for at, taps in enumerate((smooth, slope)):
        columns = slice(at * DEPTH, (at + 1) * DEPTH)
        high, low = split_rows(tap_select(index, taps))
        out[4 * RIM : 4 * RIM + DEPTH, columns] = high
        out[4 * RIM + DEPTH : 4 * RIM + 2 * DEPTH, columns] = high
        out[4 * RIM + 2 * DEPTH :, columns] = low


SMEM = pl.BlockSpec(memory_space=pltpu.SMEM)
VMEM = pl.BlockSpec(memory_space=pltpu.VMEM)
SMALL = pltpu.CompilerParams(vmem_limit_bytes=4 * 1024 * 1024)


def prepare(smooth, slope, band, step):
    return pl.pallas_call(
        prepare_kernel,
        out_shape=(
            jax.ShapeDtypeStruct((4 * RIM + 3 * DEPTH, 2 * DEPTH), jnp.bfloat16),
            jax.ShapeDtypeStruct((2, SIDE, DEPTH), jnp.float32),
        ),
        in_specs=[SMEM] * 4,
        out_specs=(VMEM, VMEM),
        compiler_params=SMALL,
        cost_estimate=pl.CostEstimate(flops=1000000, bytes_accessed=1000000, transcendentals=0),
    )(smooth, slope, band, step)


def along_matrix(matrices, axis, rows):
    return matrices[2 * axis * RIM : 2 * axis * RIM + rows, 0 : 3 * WIDE]


def depth_matrix(matrices, kind):
    return matrices[4 * RIM :, kind * DEPTH : (kind + 1) * DEPTH]


def fill_extended(extended, own, x_even, x_odd, y_even, y_odd, c_even, c_odd):
    extended[0:SIDE, 0:SIDE, :] = own
    gap = jnp.zeros((SLAB - REACH, WIDE, DEPTH), jnp.float32)
    for at, part in enumerate((x_even, x_odd)):
        start = SIDE + at * SLAB
        extended[start : start + REACH, 0:SIDE, :] = part
        extended[start + REACH : start + SLAB, :, :] = gap
    for at, (part, corner) in enumerate(((y_even, c_even), (y_odd, c_odd))):
        columns = slice(SIDE + at * SLAB, SIDE + (at + 1) * SLAB)
        extended[0:SIDE, columns, :] = part
        for side in range(2):
            start = SIDE + side * SLAB
            extended[start : start + REACH, columns, :] = corner[side * REACH : (side + 1) * REACH]


def stacked_parts(value):
    high, low = split_rows(value)
    return jnp.concatenate([high, low, high], axis=0)


def lane_parts(value):
    high, low = split_rows(value)
    return jnp.concatenate([high, low, high], axis=1)


def take_place(block, place):
    outer, inner, depth = block.shape
    return block.reshape(outer * inner, depth)[pl.ds(place, outer, stride=inner), :]


def along_x_stage(extended, crossed, matrix):
    for pair in range(0, WIDE, 2):
        places = (pair, pair + 1)
        value = jnp.concatenate([take_place(extended, y) for y in places], axis=1)
        out = jnp.dot(matrix, stacked_parts(value), preferred_element_type=jnp.float32)
        for at, y in enumerate(places):
            crossed[y, :, :] = out[:, at * DEPTH : (at + 1) * DEPTH]


def gradient_stages(extended, matrices, crossed, flat_s, flat_g, normals, lengths):
    along_x_stage(extended, crossed, along_matrix(matrices, 0, 2 * RIM))
    matrix = along_matrix(matrices, 1, 2 * RIM)
    for at, row in enumerate(OUT_ROWS):
        value = jnp.concatenate(
            [take_place(crossed, row + kind * RIM) for kind in range(2)], axis=1
        )
        got = jnp.dot(matrix, stacked_parts(value), preferred_element_type=jnp.float32)
        flat_s[at, 0:RIM, :] = got[0:RIM, DEPTH:]
        flat_s[at, RIM:, :] = got[RIM:, :DEPTH]
        flat_g[at, :, :] = got[0:RIM, :DEPTH]
    weights_s = depth_matrix(matrices, 0)
    weights_g = depth_matrix(matrices, 1)
    for at in range(0, SIDE + 2, 2):
        cross = jnp.dot(
            lane_parts(flat_s[at : at + 2].reshape(4 * RIM, DEPTH)), weights_s,
            preferred_element_type=jnp.float32,
        )
        deep = jnp.dot(
            lane_parts(flat_g[at : at + 2].reshape(2 * RIM, DEPTH)), weights_g,
            preferred_element_type=jnp.float32,
        )
        for half in range(2):
            grad_x = cross[2 * half * RIM : (2 * half + 1) * RIM]
            grad_y = cross[(2 * half + 1) * RIM : (2 * half + 2) * RIM]
            grad_z = deep[half * RIM : (half + 1) * RIM]
            square = grad_x * grad_x + grad_y * grad_y + grad_z * grad_z + 1.0
            inverse = lax.rsqrt(square)
            normals[0, at + half, :, :] = grad_x * inverse
            normals[1, at + half, :, :] = grad_y * inverse
            normals[2, at + half, :, :] = grad_z * inverse
            lengths[at + half, :, :] = square * inverse


def advance(own, speed, gain, normals, lengths, out):
    lane = lax.broadcasted_iota(jnp.int32, (SIDE, DEPTH), 1)
    for x in range(SIDE):
        at = x + 1
        across = normals[1, at, :, :]
        deep = normals[2, at, 0:SIDE, :]
        bend = normals[0, at + 1, 0:SIDE, :] - normals[0, at - 1, 0:SIDE, :]
        bend += (pltpu.roll(across, RIM - 1, 0) - pltpu.roll(across, 1, 0))[0:SIDE]
        bend += jnp.where(lane < DEPTH - 1, pltpu.roll(deep, DEPTH - 1, 1), 0.0)
        bend -= jnp.where(lane > 0, pltpu.roll(deep, 1, 1), 0.0)
        push = gain[x // (SIDE // 2), :, :] * lengths[at, 0:SIDE, :]
        out[x, :, :] = own[x, :, :] - push * (speed[x, :, :] - 0.25 * bend)


def speed_stages(extended, matrices, crossed, flat_s, velocity, out):
    along_x_stage(extended, crossed, along_matrix(matrices, 0, RIM + 8))
    matrix = along_matrix(matrices, 1, RIM + 8)
    for pair in range(0, len(OUT_ROWS), 2):
        value = jnp.concatenate(
            [take_place(crossed, row) for row in OUT_ROWS[pair : pair + 2]], axis=1
        )
        got = jnp.dot(matrix, stacked_parts(value), preferred_element_type=jnp.float32)
        for half in range(2):
            flat_s[pair + half, :, :] = got[0:RIM, half * DEPTH : (half + 1) * DEPTH]
    weights = depth_matrix(matrices, 0)
    for at in range(0, SIDE + 2, 2):
        got = jnp.dot(
            lane_parts(flat_s[at : at + 2].reshape(2 * RIM, DEPTH)), weights,
            preferred_element_type=jnp.float32,
        )
        velocity[at : at + 2, :, :] = got.reshape(2, RIM, DEPTH)
    lane = lax.broadcasted_iota(jnp.int32, (SIDE, DEPTH), 1)
    for x in range(SIDE):
        at = x + 1
        rim = velocity[at, :, :]
        centre = rim[0:SIDE]
        total = centre + velocity[at + 1, 0:SIDE, :] + velocity[at - 1, 0:SIDE, :]
        total += (pltpu.roll(rim, RIM - 1, 0) + pltpu.roll(rim, 1, 0))[0:SIDE]
        total += jnp.where(lane < DEPTH - 1, pltpu.roll(centre, DEPTH - 1, 1), 0.0)
        total += jnp.where(lane > 0, pltpu.roll(centre, 1, 1), 0.0)
        out[x, :, :] = total / 7.0


HALOS = 6


def first_kernel(own_s, own, *refs):
    halos = refs[:HALOS]
    matrices, gain, out, speed = refs[HALOS : HALOS + 4]
    extended_s, crossed_s, flat_v, velocity = refs[HALOS + 4 : HALOS + 8]
    extended, crossed, flat_s, flat_g, normals, lengths = refs[HALOS + 8 :]
    fill_extended(extended_s, own_s[...], *[halo[0] for halo in halos])
    fill_extended(extended, own[...], *[halo[1] for halo in halos])
    speed_stages(extended_s, matrices, crossed_s, flat_v, velocity, speed)
    gradient_stages(extended, matrices, crossed, flat_s, flat_g, normals, lengths)
    advance(own, speed, gain, normals, lengths, out)


def later_kernel(own, *refs):
    halos = refs[:HALOS]
    matrices, gain, speed, out = refs[HALOS : HALOS + 4]
    extended, crossed, flat_s, flat_g, normals, lengths = refs[HALOS + 4 :]
    fill_extended(extended, own[...], *[halo[...] for halo in halos])
    gradient_stages(extended, matrices, crossed, flat_s, flat_g, normals, lengths)
    advance(own, speed, gain, normals, lengths, out)


def call_kernel(body, arrays, outputs, scratch):
    shape = jax.ShapeDtypeStruct((SIDE, SIDE, DEPTH), jnp.float32)
    return pl.pallas_call(
        body,
        out_shape=(shape,) * outputs,
        in_specs=[VMEM] * len(arrays),
        out_specs=(VMEM,) * outputs,
        scratch_shapes=[pltpu.VMEM(shape, jnp.float32) for shape in scratch],
        compiler_params=pltpu.CompilerParams(vmem_limit_bytes=20 * 1024 * 1024),
    )(*arrays)


def corner_kernel(x_even, x_odd, even, odd):
    parity = lax.axis_index("gy") & 1
    for side, target in enumerate((even, odd)):
        start = pl.multiple_of(jnp.where(parity == side, SIDE - SLAB, 0), SLAB)
        for at, source in enumerate((x_even, x_odd)):
            target[..., at * REACH : (at + 1) * REACH, :, :] = source[..., pl.ds(start, SLAB), :]


def corner_sides(x_halos):
    shape = x_halos[0].shape[:-3] + (2 * REACH, SLAB, DEPTH)
    out = jax.ShapeDtypeStruct(shape, jnp.float32)
    return pl.pallas_call(
        corner_kernel,
        out_shape=(out, out),
        in_specs=[VMEM] * 2,
        out_specs=(VMEM, VMEM),
        compiler_params=SMALL,
    )(*x_halos)


def swap(block, axis, first):
    pairs = []
    for low in range(first, lax.axis_size(axis) - 1, 2):
        pairs += [(low, low + 1), (low + 1, low)]
    return lax.ppermute(block, axis, pairs)


def both_sides(block, dim, width, parity):
    length = block.shape[dim]
    high = jnp.where(parity == 0, length - width, 0)
    return (
        lax.dynamic_slice_in_dim(block, high, width, dim),
        lax.dynamic_slice_in_dim(block, length - width - high, width, dim),
    )


def stacked_sides(blocks, dim, width, parity):
    return [jnp.stack(side) for side in zip(*[both_sides(b, dim, width, parity) for b in blocks])]


def swap_sides(pieces, axis):
    return swap(pieces[0], axis, 0), swap(pieces[1], axis, 1)


def per_device(level_set, sensitivity, smooth_taps, slope_taps, band, time_step):
    parity = [lax.axis_index(axis) & 1 for axis in ("gx", "gy")]
    fields = [sensitivity, level_set]
    x_halos = swap_sides(stacked_sides(fields, 0, REACH, parity[0]), "gx")
    y_halos = swap_sides(stacked_sides(fields, 1, SLAB, parity[1]), "gy")
    matrices = prepare(smooth_taps, slope_taps, band, time_step)
    x_halos, matrices = lax.optimization_barrier((x_halos, matrices))
    corners = swap_sides(corner_sides(x_halos), "gy")
    rim = SIDE + 2
    gradient_scratch = [
        (WIDE, WIDE, DEPTH), (WIDE, 2 * RIM, DEPTH), (rim, 2 * RIM, DEPTH),
        (rim, RIM, DEPTH), (3, rim, RIM, DEPTH), (rim, RIM, DEPTH),
    ]
    speed_scratch = [
        (WIDE, WIDE, DEPTH), (WIDE, RIM + 8, DEPTH), (rim, RIM, DEPTH), (rim, RIM, DEPTH)
    ]
    phi, speed = call_kernel(
        first_kernel, (*fields, *x_halos, *y_halos, *corners, *matrices), 2,
        speed_scratch + gradient_scratch,
    )
    for _ in range(1, UPDATES):
        x_halos = swap_sides(both_sides(phi, 0, REACH, parity[0]), "gx")
        y_halos = swap_sides(both_sides(phi, 1, SLAB, parity[1]), "gy")
        corners = swap_sides(corner_sides(x_halos), "gy")
        (phi,) = call_kernel(
            later_kernel, (phi, *x_halos, *y_halos, *corners, *matrices, speed), 1, gradient_scratch,
        )
    return phi


def solution(mesh):
    return jax.shard_map(
        per_device,
        mesh=mesh,
        in_specs=(P("gx", "gy", None), P("gx", "gy", None), P(), P(), P("gx", "gy", None), P()),
        out_specs=P("gx", "gy", None),
        check_vma=False,
    )
```

time: 66.5 us -> 58.7 us (0.88)
  local copies, waits for them, and re-layouts: 7.94 us -> 1.53 us
  waiting for transfers between devices: 14.6 us -> 18.4 us
  other arithmetic: 2.49 us -> 0.13 us
  Pallas kernels: 14.5 us -> 12.4 us
    unnamed x18 -> x10, local copies, waits for them, and re-layouts: 4.75 us -> 0.03 us
    ppermute x12, waiting for transfers between devices: 14.6 us -> 18.4 us  [swap(): return lax.ppermute(block, axis, pairs)]
    another operation x4, other arithmetic: 2.49 us -> 0.13 us  [stacked_sides(): jnp.stack(side)]
    pallas_call x3 -> x5, Pallas kernels: 14.5 us -> 12.4 us  [the longest x2 10.9 us: call_kernel(): pl.pallas_call(body, out_shape=(shape,) * outputs, in_specs=[VMEM] * len(...]
    dynamic_slice x4 -> x2, local copies, waits for them, and re-layouts: 1.13 us -> 0.08 us  [both_sides(): lax.dynamic_slice_in_dim(block, length - width - high, width, dim)]
    another operation x3 -> x2, local copies, waits for them, and re-layouts: 2.01 us -> 1.42 us  [stacked_sides(): jnp.stack(side)]
  transfers between devices with their start and end apart: 12 -> 12, of which waited for: 4 -> 4; matrix products, arithmetic and copies ran while one was open for 7% -> 0% of each run, Pallas kernels for 3% -> 2%
where the time goes in v3:
time: 58.7 us; the launch traced here: 58.4 us
  starting transfers between devices  25 us (43%)
  waiting for transfers between devices  18.4 us (31%)
  Pallas kernels  12.4 us (21%)
  local copies, waits for them, and re-layouts  1.53 us (3%)
  between operations  0.93 us (2%)
    ppermute x12, starting transfers between devices, swap(): return lax.ppermute(block, axis, pairs)  25 us
    ppermute x12, waiting for transfers between devices, swap(): return lax.ppermute(block, axis, pairs)  18.4 us
    pallas_call x2, Pallas kernels, call_kernel(): pl.pallas_call(body, out_shape=(shape,) * outputs, in_specs=[VMEM] * len(...  10.9 us
    another operation x2, local copies, waits for them, and re-layouts, stacked_sides(): jnp.stack(side)  1.42 us
    pallas_call x1, Pallas kernels, prepare(): pl.pallas_call(prepare_kernel, out_shape=(jax.ShapeDtypeStruct((4 * RIM +...  1.36 us
  transfers between devices with their start and end apart: 12, of which 4 were waited for; matrix products, arithmetic and copies ran while one was open for 0% of the time, Pallas kernels for 2%

profile of v3, /device:TPU:41, one launch (start us, length us, event | category | flops | bytes accessed | tf_op | source)
XLA Modules:
  0.0 58.4 jit_solution(17264078672064825017)
XLA Ops:
  0.0 1.3 %dynamic-slice_bitcast_fusion.4 = (f32[1,13,32,128]{3,2,1,0:T(8,128)S(1)}, f32[1,13,32,128]{3,2,1,0:T(8,128)S(1)}, f32[1,13,32,128]{3,2,1,0:T(8,128)S(1)}, f32[1,13,32,128]{3,2,1,0:T(8,128)S(1)}) fusion(f32[32,32,128]{2,1,0:T(8,128)} %own.1, s32[]{:T(128)S(6)} %select_n.28, s32[]{:T(128)S(6)} %select_n.27, f32[32,32,128]{2,1,0:T(8,128)} %own_s.1), kind=kLoop, calls=%fused_computation.8 | loop fusion | bytes 1703944 | tf_op jit(solution)/shard_map/stack | solution.py:311
  1.3 0.0 copy-start.1
  1.4 0.0 copy-start
  1.4 1.3 %collective-permute-start = (f32[2,13,32,128]{3,2,1,0:T(8,128)S(1)}, f32[2,13,32,128]{3,2,1,0:T(8,128)S(1)}, u32[]{:S(2)}, u32[]{:S(2)}) collective-permute-start(f32[2,13,32,128]{3,2,1,0:T(8,128)S(1)} %pad_maximum_fusion.2), channel_id=1, source_target_pairs={{0,8},{8,0},{16,24},{24,16},{32,40},{40,32},{48,56},{56,48},{64,72... | collective-permute-start | bytes 1277960 | tf_op jit(solution)/shard_map/ppermute | solution.py:298
  2.7 3.3 %collective-permute-start.1 = (f32[2,13,32,128]{3,2,1,0:T(8,128)S(1)}, f32[2,13,32,128]{3,2,1,0:T(8,128)S(1)}, u32[]{:S(2)}, u32[]{:S(2)}) collective-permute-start(f32[2,13,32,128]{3,2,1,0:T(8,128)S(1)} %pad_maximum_fusion.3), channel_id=1, source_target_pairs={{8,16},{16,8},{24,32},{32,24},{40,48},{48,40},{56,64},{64,56},{72,... | collective-permute-start | bytes 1277960 | tf_op jit(solution)/shard_map/ppermute | solution.py:298
  6.0 0.1 dynamic-slice_bitcast_fusion
  6.2 1.3 %collective-permute-start.2 = (f32[2,32,16,128]{3,2,1,0:T(8,128)S(1)}, f32[2,32,16,128]{3,2,1,0:T(8,128)S(1)}, u32[]{:S(2)}, u32[]{:S(2)}) collective-permute-start(f32[2,32,16,128]{3,2,1,0:T(8,128)S(1)} %pad_maximum_fusion), channel_id=1, source_target_pairs={{0,1},{1,0},{2,3},{3,2},{4,5},{5,4},{6,7},{7,6},{8,9},{9,8},{10,11... | collective-permute-start | bytes 1572872 | tf_op jit(solution)/shard_map/ppermute | solution.py:298
  7.5 3.1 %collective-permute-start.3 = (f32[2,32,16,128]{3,2,1,0:T(8,128)S(1)}, f32[2,32,16,128]{3,2,1,0:T(8,128)S(1)}, u32[]{:S(2)}, u32[]{:S(2)}) collective-permute-start(f32[2,32,16,128]{3,2,1,0:T(8,128)S(1)} %pad_maximum_fusion.1), channel_id=1, source_target_pairs={{1,2},{2,1},{3,4},{4,3},{5,6},{6,5},{9,10},{10,9},{11,12},{12,11},... | collective-permute-start | bytes 1572872 | tf_op jit(solution)/shard_map/ppermute | solution.py:298
  11.4 1.4 %shard_map.64 = (bf16[544,256]{1,0:T(8,128)(2,1)S(1)}, f32[2,32,128]{2,1,0:T(8,128)S(1)}) custom-call(f32[25]{0:T(128)S(1)} %copy-done.3, f32[25]{0:T(128)S(1)} %copy-done.4, s32[2,2,4]{2,1,0:T(2,128)S(1)} %copy-done.2, f32[1]{0:T(128)S(6)} %copy.7.step), custom_call_target="tpu_custom_call" | custom-call | flops 1000000 | bytes 1000000 | tf_op jit(solution)/shard_map/pallas_call | solution.py:101
  12.7 4.3 %collective-permute-done.1.x_odd.refs_1_ = f32[2,13,32,128]{3,2,1,0:T(8,128)S(1)} collective-permute-done((f32[2,13,32,128]{3,2,1,0:T(8,128)S(1)}, f32[2,13,32,128]{3,2,1,0:T(8,128)S(1)}, u32[]{:S(2)}, u32[]{:S(2)}) %collective-permute-start.1) | collective-permute-done | bytes 426016 | tf_op jit(solution)/shard_map/ppermute | solution.py:298
  17.1 0.1 shard_map.65
  17.1 1.9 %collective-permute-start.4 = (f32[2,26,16,128]{3,2,1,0:T(8,128)S(1)}, f32[2,26,16,128]{3,2,1,0:T(8,128)S(1)}, u32[]{:S(2)}, u32[]{:S(2)}) collective-permute-start(f32[2,26,16,128]{3,2,1,0:T(8,128)S(1)} %get-tuple-element.21), channel_id=1, source_target_pairs={{0,1},{1,0},{2,3},{3,2},{4,5},{5,4},{6,7},{7,6},{8,9},{9,8},{10,11... | collective-permute-start | bytes 1277960 | tf_op jit(solution)/shard_map/ppermute | solution.py:298
  19.1 3.1 %collective-permute-start.5 = (f32[2,26,16,128]{3,2,1,0:T(8,128)S(1)}, f32[2,26,16,128]{3,2,1,0:T(8,128)S(1)}, u32[]{:S(2)}, u32[]{:S(2)}) collective-permute-start(f32[2,26,16,128]{3,2,1,0:T(8,128)S(1)} %get-tuple-element.22), channel_id=1, source_target_pairs={{1,2},{2,1},{3,4},{4,3},{5,6},{6,5},{9,10},{10,9},{11,12},{12,11},... | collective-permute-start | bytes 1277960 | tf_op jit(solution)/shard_map/ppermute | solution.py:298
  22.2 6.3 %collective-permute-done.5.refs_5_ = f32[2,26,16,128]{3,2,1,0:T(8,128)S(1)} collective-permute-done((f32[2,26,16,128]{3,2,1,0:T(8,128)S(1)}, f32[2,26,16,128]{3,2,1,0:T(8,128)S(1)}, u32[]{:S(2)}, u32[]{:S(2)}) %collective-permute-start.5) | collective-permute-done | bytes 426016 | tf_op jit(solution)/shard_map/ppermute | solution.py:298
  28.5 6.3 %shard_map.66 = (f32[32,32,128]{2,1,0:T(8,128)S(1)}, f32[32,32,128]{2,1,0:T(8,128)S(1)}) custom-call(f32[32,32,128]{2,1,0:T(8,128)S(1)} %copy-done, f32[32,32,128]{2,1,0:T(8,128)S(1)} %copy-done.1, f32[2,13,32,128]{3,2,1,0:T(8,128)S(1)} %collective-permute-done.x_even.refs_0_, f32[2,13,32,128]{3,2,1,0:T(8,128)S(1)} %collective-permute-done.1.x_odd.refs_1_, ...), custom_call_target="tpu_custom_call" | custom-call | tf_op jit(solution)/shard_map/pallas_call | solution.py:264
  34.9 3.3 %collective-permute-start.7 = (f32[13,32,128]{2,1,0:T(8,128)S(1)}, f32[13,32,128]{2,1,0:T(8,128)S(1)}, u32[]{:S(2)}, u32[]{:S(2)}) collective-permute-start(f32[13,32,128]{2,1,0:T(8,128)S(1)} %get-tuple-element.31), channel_id=1, source_target_pairs={{8,16},{16,8},{24,32},{32,24},{40,48},{48,40},{56,64},{64,56},{72,... | collective-permute-start | bytes 638984 | tf_op jit(solution)/shard_map/ppermute | solution.py:298
  38.1 0.1 collective-permute-start.6
  38.3 3.4 %collective-permute-start.9 = (f32[32,16,128]{2,1,0:T(8,128)S(1)}, f32[32,16,128]{2,1,0:T(8,128)S(1)}, u32[]{:S(2)}, u32[]{:S(2)}) collective-permute-start(f32[32,16,128]{2,1,0:T(8,128)S(1)} %get-tuple-element.29), channel_id=1, source_target_pairs={{1,2},{2,1},{3,4},{4,3},{5,6},{6,5},{9,10},{10,9},{11,12},{12,11},... | collective-permute-start | bytes 786440 | tf_op jit(solution)/shard_map/ppermute | solution.py:298
  41.7 0.1 collective-permute-start.8
  41.8 4.0 %collective-permute-done.7.x_odd.refs_1_ = f32[13,32,128]{2,1,0:T(8,128)S(1)} collective-permute-done((f32[13,32,128]{2,1,0:T(8,128)S(1)}, f32[13,32,128]{2,1,0:T(8,128)S(1)}, u32[]{:S(2)}, u32[]{:S(2)}) %collective-permute-start.7) | collective-permute-done | bytes 213024 | tf_op jit(solution)/shard_map/ppermute | solution.py:298
  45.8 0.9 %collective-permute-start.10 = (f32[26,16,128]{2,1,0:T(8,128)S(1)}, f32[26,16,128]{2,1,0:T(8,128)S(1)}, u32[]{:S(2)}, u32[]{:S(2)}) collective-permute-start(f32[26,16,128]{2,1,0:T(8,128)S(1)} %get-tuple-element.26), channel_id=1, source_target_pairs={{0,1},{1,0},{2,3},{3,2},{4,5},{5,4},{6,7},{7,6},{8,9},{9,8},{10,11... | collective-permute-start | bytes 638984 | tf_op jit(solution)/shard_map/ppermute | solution.py:298
  46.7 3.3 %collective-permute-start.11 = (f32[26,16,128]{2,1,0:T(8,128)S(1)}, f32[26,16,128]{2,1,0:T(8,128)S(1)}, u32[]{:S(2)}, u32[]{:S(2)}) collective-permute-start(f32[26,16,128]{2,1,0:T(8,128)S(1)} %get-tuple-element.27), channel_id=1, source_target_pairs={{1,2},{2,1},{3,4},{4,3},{5,6},{6,5},{9,10},{10,9},{11,12},{12,11},... | collective-permute-start | bytes 638984 | tf_op jit(solution)/shard_map/ppermute | solution.py:298
  50.0 3.8 %collective-permute-done.11.refs_5_ = f32[26,16,128]{2,1,0:T(8,128)S(1)} collective-permute-done((f32[26,16,128]{2,1,0:T(8,128)S(1)}, f32[26,16,128]{2,1,0:T(8,128)S(1)}, u32[]{:S(2)}, u32[]{:S(2)}) %collective-permute-start.11) | collective-permute-done | bytes 213024 | tf_op jit(solution)/shard_map/ppermute | solution.py:298
  53.8 4.6 %shard_map.68 = f32[32,32,128]{2,1,0:T(8,128)} custom-call(f32[32,32,128]{2,1,0:T(8,128)S(1)} %get-tuple-element.25.own, f32[13,32,128]{2,1,0:T(8,128)S(1)} %collective-permute-done.6.x_even.refs_0_, f32[13,32,128]{2,1,0:T(8,128)S(1)} %collective-permute-done.7.x_odd.refs_1_, f32[32,16,128]{2,1,0:T(8,128)S(1)} %collective-permute-done.8.refs_2_, ...), custom_call_target="tpu_custom_call" | custom-call | tf_op jit(solution)/shard_map/pallas_call | solution.py:264
  (23 shorter events, 0.3 us)
Async XLA Ops:
  1.3 4.7 %copy-start.1 = (f32[32,32,128]{2,1,0:T(8,128)S(1)}, f32[32,32,128]{2,1,0:T(8,128)}, u32[]{:S(2)}) copy-start(f32[32,32,128]{2,1,0:T(8,128)} %own.1) | copy-start | bytes 1572868
  1.4 4.6 %copy-start = (f32[32,32,128]{2,1,0:T(8,128)S(1)}, f32[32,32,128]{2,1,0:T(8,128)}, u32[]{:S(2)}) copy-start(f32[32,32,128]{2,1,0:T(8,128)} %own_s.1) | copy-start | bytes 1572868
  1.4 11.3 %collective-permute-start = (f32[2,13,32,128]{3,2,1,0:T(8,128)S(1)}, f32[2,13,32,128]{3,2,1,0:T(8,128)S(1)}, u32[]{:S(2)}, u32[]{:S(2)}) collective-permute-start(f32[2,13,32,128]{3,2,1,0:T(8,128)S(1)} %pad_maximum_fusion.2), channel_id=1, source_target_pairs={{0,8},{8,0},{16,24},{24,16},{32,40},{40,32},{48,56},{56,48},{64,72... | collective-permute-start | bytes 1277960 | tf_op jit(solution)/shard_map/ppermute | solution.py:298
  2.7 14.4 %collective-permute-start.1 = (f32[2,13,32,128]{3,2,1,0:T(8,128)S(1)}, f32[2,13,32,128]{3,2,1,0:T(8,128)S(1)}, u32[]{:S(2)}, u32[]{:S(2)}) collective-permute-start(f32[2,13,32,128]{3,2,1,0:T(8,128)S(1)} %pad_maximum_fusion.3), channel_id=1, source_target_pairs={{8,16},{16,8},{24,32},{32,24},{40,48},{48,40},{56,64},{64,56},{72,... | collective-permute-start | bytes 1277960 | tf_op jit(solution)/shard_map/ppermute | solution.py:298
  6.2 16.0 %collective-permute-start.2 = (f32[2,32,16,128]{3,2,1,0:T(8,128)S(1)}, f32[2,32,16,128]{3,2,1,0:T(8,128)S(1)}, u32[]{:S(2)}, u32[]{:S(2)}) collective-permute-start(f32[2,32,16,128]{3,2,1,0:T(8,128)S(1)} %pad_maximum_fusion), channel_id=1, source_target_pairs={{0,1},{1,0},{2,3},{3,2},{4,5},{5,4},{6,7},{7,6},{8,9},{9,8},{10,11... | collective-permute-start | bytes 1572872 | tf_op jit(solution)/shard_map/ppermute | solution.py:298
  7.5 3.8 %copy-start.2 = (s32[2,2,4]{2,1,0:T(2,128)S(1)}, s32[2,2,4]{2,1,0:T(2,128)}, u32[]{:S(2)}) copy-start(s32[2,2,4]{2,1,0:T(2,128)} %band.1) | copy-start | bytes 196
  7.5 3.8 %copy-start.3 = (f32[25]{0:T(128)S(1)}, f32[25]{0:T(128)}, u32[]{:S(2)}) copy-start(f32[25]{0:T(128)} %smooth.1) | copy-start | bytes 304
  7.5 3.8 %copy-start.4 = (f32[25]{0:T(128)S(1)}, f32[25]{0:T(128)}, u32[]{:S(2)}) copy-start(f32[25]{0:T(128)} %slope.1) | copy-start | bytes 304
  7.5 14.7 %collective-permute-start.3 = (f32[2,32,16,128]{3,2,1,0:T(8,128)S(1)}, f32[2,32,16,128]{3,2,1,0:T(8,128)S(1)}, u32[]{:S(2)}, u32[]{:S(2)}) collective-permute-start(f32[2,32,16,128]{3,2,1,0:T(8,128)S(1)} %pad_maximum_fusion.1), channel_id=1, source_target_pairs={{1,2},{2,1},{3,4},{4,3},{5,6},{6,5},{9,10},{10,9},{11,12},{12,11},... | collective-permute-start | bytes 1572872 | tf_op jit(solution)/shard_map/ppermute | solution.py:298
  17.1 5.1 %collective-permute-start.4 = (f32[2,26,16,128]{3,2,1,0:T(8,128)S(1)}, f32[2,26,16,128]{3,2,1,0:T(8,128)S(1)}, u32[]{:S(2)}, u32[]{:S(2)}) collective-permute-start(f32[2,26,16,128]{3,2,1,0:T(8,128)S(1)} %get-tuple-element.21), channel_id=1, source_target_pairs={{0,1},{1,0},{2,3},{3,2},{4,5},{5,4},{6,7},{7,6},{8,9},{9,8},{10,11... | collective-permute-start | bytes 1277960 | tf_op jit(solution)/shard_map/ppermute | solution.py:298
  19.1 9.4 %collective-permute-start.5 = (f32[2,26,16,128]{3,2,1,0:T(8,128)S(1)}, f32[2,26,16,128]{3,2,1,0:T(8,128)S(1)}, u32[]{:S(2)}, u32[]{:S(2)}) collective-permute-start(f32[2,26,16,128]{3,2,1,0:T(8,128)S(1)} %get-tuple-element.22), channel_id=1, source_target_pairs={{1,2},{2,1},{3,4},{4,3},{5,6},{6,5},{9,10},{10,9},{11,12},{12,11},... | collective-permute-start | bytes 1277960 | tf_op jit(solution)/shard_map/ppermute | solution.py:298
  34.9 10.9 %collective-permute-start.7 = (f32[13,32,128]{2,1,0:T(8,128)S(1)}, f32[13,32,128]{2,1,0:T(8,128)S(1)}, u32[]{:S(2)}, u32[]{:S(2)}) collective-permute-start(f32[13,32,128]{2,1,0:T(8,128)S(1)} %get-tuple-element.31), channel_id=1, source_target_pairs={{8,16},{16,8},{24,32},{32,24},{40,48},{48,40},{56,64},{64,56},{72,... | collective-permute-start | bytes 638984 | tf_op jit(solution)/shard_map/ppermute | solution.py:298
  38.1 7.6 %collective-permute-start.6 = (f32[13,32,128]{2,1,0:T(8,128)S(1)}, f32[13,32,128]{2,1,0:T(8,128)S(1)}, u32[]{:S(2)}, u32[]{:S(2)}) collective-permute-start(f32[13,32,128]{2,1,0:T(8,128)S(1)} %get-tuple-element.32), channel_id=1, source_target_pairs={{0,8},{8,0},{16,24},{24,16},{32,40},{40,32},{48,56},{56,48},{64,72... | collective-permute-start | bytes 638984 | tf_op jit(solution)/shard_map/ppermute | solution.py:298
  38.3 11.7 %collective-permute-start.9 = (f32[32,16,128]{2,1,0:T(8,128)S(1)}, f32[32,16,128]{2,1,0:T(8,128)S(1)}, u32[]{:S(2)}, u32[]{:S(2)}) collective-permute-start(f32[32,16,128]{2,1,0:T(8,128)S(1)} %get-tuple-element.29), channel_id=1, source_target_pairs={{1,2},{2,1},{3,4},{4,3},{5,6},{6,5},{9,10},{10,9},{11,12},{12,11},... | collective-permute-start | bytes 786440 | tf_op jit(solution)/shard_map/ppermute | solution.py:298
  41.7 8.3 %collective-permute-start.8 = (f32[32,16,128]{2,1,0:T(8,128)S(1)}, f32[32,16,128]{2,1,0:T(8,128)S(1)}, u32[]{:S(2)}, u32[]{:S(2)}) collective-permute-start(f32[32,16,128]{2,1,0:T(8,128)S(1)} %get-tuple-element.30), channel_id=1, source_target_pairs={{0,1},{1,0},{2,3},{3,2},{4,5},{5,4},{6,7},{7,6},{8,9},{9,8},{10,11... | collective-permute-start | bytes 786440 | tf_op jit(solution)/shard_map/ppermute | solution.py:298
  45.8 4.2 %collective-permute-start.10 = (f32[26,16,128]{2,1,0:T(8,128)S(1)}, f32[26,16,128]{2,1,0:T(8,128)S(1)}, u32[]{:S(2)}, u32[]{:S(2)}) collective-permute-start(f32[26,16,128]{2,1,0:T(8,128)S(1)} %get-tuple-element.26), channel_id=1, source_target_pairs={{0,1},{1,0},{2,3},{3,2},{4,5},{5,4},{6,7},{7,6},{8,9},{9,8},{10,11... | collective-permute-start | bytes 638984 | tf_op jit(solution)/shard_map/ppermute | solution.py:298
  46.7 7.2 %collective-permute-start.11 = (f32[26,16,128]{2,1,0:T(8,128)S(1)}, f32[26,16,128]{2,1,0:T(8,128)S(1)}, u32[]{:S(2)}, u32[]{:S(2)}) collective-permute-start(f32[26,16,128]{2,1,0:T(8,128)S(1)} %get-tuple-element.27), channel_id=1, source_target_pairs={{1,2},{2,1},{3,4},{4,3},{5,6},{6,5},{9,10},{10,9},{11,12},{12,11},... | collective-permute-start | bytes 638984 | tf_op jit(solution)/shard_map/ppermute | solution.py:298

commit v4 on v3

--- a/solution.py
+++ b/solution.py
@@ -125,7 +125,7 @@
     for at, part in enumerate((x_even, x_odd)):
         start = SIDE + at * SLAB
         extended[start : start + REACH, 0:SIDE, :] = part
-        extended[start + REACH : start + SLAB, :, :] = gap
+        extended[start + REACH : start + SLAB, 0:WIDE, :] = gap
     for at, (part, corner) in enumerate(((y_even, c_even), (y_odd, c_odd))):
         columns = slice(SIDE + at * SLAB, SIDE + (at + 1) * SLAB)
         extended[0:SIDE, columns, :] = part
@@ -155,10 +155,10 @@
         value = jnp.concatenate([take_place(extended, y) for y in places], axis=1)
         out = jnp.dot(matrix, stacked_parts(value), preferred_element_type=jnp.float32)
         for at, y in enumerate(places):
-            crossed[y, :, :] = out[:, at * DEPTH : (at + 1) * DEPTH]
-
-
-def gradient_stages(extended, matrices, crossed, flat_s, flat_g, normals, lengths):
+            crossed[y, 0 : out.shape[0], :] = out[:, at * DEPTH : (at + 1) * DEPTH]
+
+
+def gradient_stages(extended, matrices, crossed, flat_s, flat_g, normals, lengths, finish):
     along_x_stage(extended, crossed, along_matrix(matrices, 0, 2 * RIM))
     matrix = along_matrix(matrices, 1, 2 * RIM)
     for at, row in enumerate(OUT_ROWS):
@@ -190,20 +190,22 @@
             normals[1, at + half, :, :] = grad_y * inverse
             normals[2, at + half, :, :] = grad_z * inverse
             lengths[at + half, :, :] = square * inverse
-
-
-def advance(own, speed, gain, normals, lengths, out):
+        if at > 0:
+            finish(at - 2)
+            finish(at - 1)
+
+
+def advance(x, own, speed, gain, normals, lengths):
     lane = lax.broadcasted_iota(jnp.int32, (SIDE, DEPTH), 1)
-    for x in range(SIDE):
-        at = x + 1
-        across = normals[1, at, :, :]
-        deep = normals[2, at, 0:SIDE, :]
-        bend = normals[0, at + 1, 0:SIDE, :] - normals[0, at - 1, 0:SIDE, :]
-        bend += (pltpu.roll(across, RIM - 1, 0) - pltpu.roll(across, 1, 0))[0:SIDE]
-        bend += jnp.where(lane < DEPTH - 1, pltpu.roll(deep, DEPTH - 1, 1), 0.0)
-        bend -= jnp.where(lane > 0, pltpu.roll(deep, 1, 1), 0.0)
-        push = gain[x // (SIDE // 2), :, :] * lengths[at, 0:SIDE, :]
-        out[x, :, :] = own[x, :, :] - push * (speed[x, :, :] - 0.25 * bend)
+    at = x + 1
+    across = normals[1, at, :, :]
+    deep = normals[2, at, 0:SIDE, :]
+    bend = normals[0, at + 1, 0:SIDE, :] - normals[0, at - 1, 0:SIDE, :]
+    bend += (pltpu.roll(across, RIM - 1, 0) - pltpu.roll(across, 1, 0))[0:SIDE]
+    bend += jnp.where(lane < DEPTH - 1, pltpu.roll(deep, DEPTH - 1, 1), 0.0)
+    bend -= jnp.where(lane > 0, pltpu.roll(deep, 1, 1), 0.0)
+    push = gain[x // (SIDE // 2), :, :] * lengths[at, 0:SIDE, :]
+    return own[x, :, :] - push * (speed[x, :, :] - 0.25 * bend)
 
 
 def speed_stages(extended, matrices, crossed, flat_s, velocity, out):
@@ -246,8 +248,11 @@
     fill_extended(extended_s, own_s[...], *[halo[0] for halo in halos])
     fill_extended(extended, own[...], *[halo[1] for halo in halos])
     speed_stages(extended_s, matrices, crossed_s, flat_v, velocity, speed)
-    gradient_stages(extended, matrices, crossed, flat_s, flat_g, normals, lengths)
-    advance(own, speed, gain, normals, lengths, out)
+
+    def finish(x):
+        out[x, :, :] = advance(x, own, speed, gain, normals, lengths)
+
+    gradient_stages(extended, matrices, crossed, flat_s, flat_g, normals, lengths, finish)
 
 
 def later_kernel(own, *refs):
@@ -255,8 +260,11 @@
     matrices, gain, speed, out = refs[HALOS : HALOS + 4]
     extended, crossed, flat_s, flat_g, normals, lengths = refs[HALOS + 4 :]
     fill_extended(extended, own[...], *[halo[...] for halo in halos])
-    gradient_stages(extended, matrices, crossed, flat_s, flat_g, normals, lengths)
-    advance(own, speed, gain, normals, lengths, out)
+
+    def finish(x):
+        out[x, :, :] = advance(x, own, speed, gain, normals, lengths)
+
+    gradient_stages(extended, matrices, crossed, flat_s, flat_g, normals, lengths, finish)
 
 
 def call_kernel(body, arrays, outputs, scratch):
@@ -325,11 +333,11 @@
     corners = swap_sides(corner_sides(x_halos), "gy")
     rim = SIDE + 2
     gradient_scratch = [
-        (WIDE, WIDE, DEPTH), (WIDE, 2 * RIM, DEPTH), (rim, 2 * RIM, DEPTH),
+        (WIDE, WIDE + 8, DEPTH), (WIDE, 2 * RIM + 8, DEPTH), (rim, 2 * RIM, DEPTH),
         (rim, RIM, DEPTH), (3, rim, RIM, DEPTH), (rim, RIM, DEPTH),
     ]
     speed_scratch = [
-        (WIDE, WIDE, DEPTH), (WIDE, RIM + 8, DEPTH), (rim, RIM, DEPTH), (rim, RIM, DEPTH)
+        (WIDE, WIDE + 8, DEPTH), (WIDE, RIM + 16, DEPTH), (rim, RIM, DEPTH), (rim, RIM, DEPTH)
     ]
     phi, speed = call_kernel(
         first_kernel, (*fields, *x_halos, *y_halos, *corners, *matrices), 2,

time: 58.7 us -> 55.2 us (0.940)
  Pallas kernels: 12.4 us -> 8.89 us
    pallas_call x2, Pallas kernels: 10.9 us -> 7.45 us  [call_kernel(): pl.pallas_call(body, out_shape=(shape,) * outputs, in_specs=[VMEM] * len(...]
  transfers between devices with their start and end apart: 12 -> 12, of which waited for: 4 -> 4; matrix products, arithmetic and copies ran while one was open for 0% -> 0% of each run, Pallas kernels for 2% -> 3%
where the time goes in v4:
time: 55.2 us; the launch traced here: 55 us
  starting transfers between devices  24.8 us (45%)
  waiting for transfers between devices  18.6 us (34%)
  Pallas kernels  8.89 us (16%)
  local copies, waits for them, and re-layouts  1.53 us (3%)
  between operations  0.93 us (2%)
    ppermute x12, starting transfers between devices, swap(): return lax.ppermute(block, axis, pairs)  24.8 us
    ppermute x12, waiting for transfers between devices, swap(): return lax.ppermute(block, axis, pairs)  18.6 us
    pallas_call x2, Pallas kernels, call_kernel(): pl.pallas_call(body, out_shape=(shape,) * outputs, in_specs=[VMEM] * len(...  7.45 us
    another operation x2, local copies, waits for them, and re-layouts, stacked_sides(): jnp.stack(side)  1.42 us
    pallas_call x1, Pallas kernels, prepare(): pl.pallas_call(prepare_kernel, out_shape=(jax.ShapeDtypeStruct((4 * RIM +...  1.36 us
  transfers between devices with their start and end apart: 12, of which 4 were waited for; matrix products, arithmetic and copies ran while one was open for 0% of the time, Pallas kernels for 3%

profile of v4, /device:TPU:41, one launch (start us, length us, event | category | flops | bytes accessed | tf_op | source)
XLA Modules:
  0.0 55.0 jit_solution(893525410550010327)
XLA Ops:
  0.0 1.3 %dynamic-slice_bitcast_fusion.4 = (f32[1,13,32,128]{3,2,1,0:T(8,128)S(1)}, f32[1,13,32,128]{3,2,1,0:T(8,128)S(1)}, f32[1,13,32,128]{3,2,1,0:T(8,128)S(1)}, f32[1,13,32,128]{3,2,1,0:T(8,128)S(1)}) fusion(f32[32,32,128]{2,1,0:T(8,128)} %own.1, s32[]{:T(128)S(6)} %select_n.28, s32[]{:T(128)S(6)} %select_n.27, f32[32,32,128]{2,1,0:T(8,128)} %own_s.1), kind=kLoop, calls=%fused_computation.8 | loop fusion | bytes 1703944 | tf_op jit(solution)/shard_map/stack | solution.py:319
  1.3 0.0 copy-start.1
  1.4 0.0 copy-start
  1.4 1.3 %collective-permute-start = (f32[2,13,32,128]{3,2,1,0:T(8,128)S(1)}, f32[2,13,32,128]{3,2,1,0:T(8,128)S(1)}, u32[]{:S(2)}, u32[]{:S(2)}) collective-permute-start(f32[2,13,32,128]{3,2,1,0:T(8,128)S(1)} %pad_maximum_fusion.2), channel_id=1, source_target_pairs={{0,8},{8,0},{16,24},{24,16},{32,40},{40,32},{48,56},{56,48},{64,72... | collective-permute-start | bytes 1277960 | tf_op jit(solution)/shard_map/ppermute | solution.py:306
  2.7 3.3 %collective-permute-start.1 = (f32[2,13,32,128]{3,2,1,0:T(8,128)S(1)}, f32[2,13,32,128]{3,2,1,0:T(8,128)S(1)}, u32[]{:S(2)}, u32[]{:S(2)}) collective-permute-start(f32[2,13,32,128]{3,2,1,0:T(8,128)S(1)} %pad_maximum_fusion.3), channel_id=1, source_target_pairs={{8,16},{16,8},{24,32},{32,24},{40,48},{48,40},{56,64},{64,56},{72,... | collective-permute-start | bytes 1277960 | tf_op jit(solution)/shard_map/ppermute | solution.py:306
  6.0 0.1 dynamic-slice_bitcast_fusion
  6.2 1.3 %collective-permute-start.2 = (f32[2,32,16,128]{3,2,1,0:T(8,128)S(1)}, f32[2,32,16,128]{3,2,1,0:T(8,128)S(1)}, u32[]{:S(2)}, u32[]{:S(2)}) collective-permute-start(f32[2,32,16,128]{3,2,1,0:T(8,128)S(1)} %pad_maximum_fusion), channel_id=1, source_target_pairs={{0,1},{1,0},{2,3},{3,2},{4,5},{5,4},{6,7},{7,6},{8,9},{9,8},{10,11... | collective-permute-start | bytes 1572872 | tf_op jit(solution)/shard_map/ppermute | solution.py:306
  7.5 3.1 %collective-permute-start.3 = (f32[2,32,16,128]{3,2,1,0:T(8,128)S(1)}, f32[2,32,16,128]{3,2,1,0:T(8,128)S(1)}, u32[]{:S(2)}, u32[]{:S(2)}) collective-permute-start(f32[2,32,16,128]{3,2,1,0:T(8,128)S(1)} %pad_maximum_fusion.1), channel_id=1, source_target_pairs={{1,2},{2,1},{3,4},{4,3},{5,6},{6,5},{9,10},{10,9},{11,12},{12,11},... | collective-permute-start | bytes 1572872 | tf_op jit(solution)/shard_map/ppermute | solution.py:306
  11.4 1.4 %shard_map.64 = (bf16[544,256]{1,0:T(8,128)(2,1)S(1)}, f32[2,32,128]{2,1,0:T(8,128)S(1)}) custom-call(f32[25]{0:T(128)S(1)} %copy-done.3, f32[25]{0:T(128)S(1)} %copy-done.4, s32[2,2,4]{2,1,0:T(2,128)S(1)} %copy-done.2, f32[1]{0:T(128)S(6)} %copy.7.step), custom_call_target="tpu_custom_call" | custom-call | flops 1000000 | bytes 1000000 | tf_op jit(solution)/shard_map/pallas_call | solution.py:101
  12.7 4.3 %collective-permute-done.1.x_odd.refs_1_ = f32[2,13,32,128]{3,2,1,0:T(8,128)S(1)} collective-permute-done((f32[2,13,32,128]{3,2,1,0:T(8,128)S(1)}, f32[2,13,32,128]{3,2,1,0:T(8,128)S(1)}, u32[]{:S(2)}, u32[]{:S(2)}) %collective-permute-start.1) | collective-permute-done | bytes 426016 | tf_op jit(solution)/shard_map/ppermute | solution.py:306
  17.1 0.1 shard_map.65
  17.1 1.9 %collective-permute-start.4 = (f32[2,26,16,128]{3,2,1,0:T(8,128)S(1)}, f32[2,26,16,128]{3,2,1,0:T(8,128)S(1)}, u32[]{:S(2)}, u32[]{:S(2)}) collective-permute-start(f32[2,26,16,128]{3,2,1,0:T(8,128)S(1)} %get-tuple-element.21), channel_id=1, source_target_pairs={{0,1},{1,0},{2,3},{3,2},{4,5},{5,4},{6,7},{7,6},{8,9},{9,8},{10,11... | collective-permute-start | bytes 1277960 | tf_op jit(solution)/shard_map/ppermute | solution.py:306
  19.1 3.1 %collective-permute-start.5 = (f32[2,26,16,128]{3,2,1,0:T(8,128)S(1)}, f32[2,26,16,128]{3,2,1,0:T(8,128)S(1)}, u32[]{:S(2)}, u32[]{:S(2)}) collective-permute-start(f32[2,26,16,128]{3,2,1,0:T(8,128)S(1)} %get-tuple-element.22), channel_id=1, source_target_pairs={{1,2},{2,1},{3,4},{4,3},{5,6},{6,5},{9,10},{10,9},{11,12},{12,11},... | collective-permute-start | bytes 1277960 | tf_op jit(solution)/shard_map/ppermute | solution.py:306
  22.2 6.3 %collective-permute-done.5.refs_5_ = f32[2,26,16,128]{3,2,1,0:T(8,128)S(1)} collective-permute-done((f32[2,26,16,128]{3,2,1,0:T(8,128)S(1)}, f32[2,26,16,128]{3,2,1,0:T(8,128)S(1)}, u32[]{:S(2)}, u32[]{:S(2)}) %collective-permute-start.5) | collective-permute-done | bytes 426016 | tf_op jit(solution)/shard_map/ppermute | solution.py:306
  28.5 4.0 %shard_map.66 = (f32[32,32,128]{2,1,0:T(8,128)S(1)}, f32[32,32,128]{2,1,0:T(8,128)S(1)}) custom-call(f32[32,32,128]{2,1,0:T(8,128)S(1)} %copy-done, f32[32,32,128]{2,1,0:T(8,128)S(1)} %copy-done.1, f32[2,13,32,128]{3,2,1,0:T(8,128)S(1)} %collective-permute-done.x_even.refs_0_, f32[2,13,32,128]{3,2,1,0:T(8,128)S(1)} %collective-permute-done.1.x_odd.refs_1_, ...), custom_call_target="tpu_custom_call" | custom-call | tf_op jit(solution)/shard_map/pallas_call | solution.py:272
  32.6 3.3 %collective-permute-start.7 = (f32[13,32,128]{2,1,0:T(8,128)S(1)}, f32[13,32,128]{2,1,0:T(8,128)S(1)}, u32[]{:S(2)}, u32[]{:S(2)}) collective-permute-start(f32[13,32,128]{2,1,0:T(8,128)S(1)} %get-tuple-element.31), channel_id=1, source_target_pairs={{8,16},{16,8},{24,32},{32,24},{40,48},{48,40},{56,64},{64,56},{72,... | collective-permute-start | bytes 638984 | tf_op jit(solution)/shard_map/ppermute | solution.py:306
  35.8 0.1 collective-permute-start.6
  36.0 3.4 %collective-permute-start.9 = (f32[32,16,128]{2,1,0:T(8,128)S(1)}, f32[32,16,128]{2,1,0:T(8,128)S(1)}, u32[]{:S(2)}, u32[]{:S(2)}) collective-permute-start(f32[32,16,128]{2,1,0:T(8,128)S(1)} %get-tuple-element.29), channel_id=1, source_target_pairs={{1,2},{2,1},{3,4},{4,3},{5,6},{6,5},{9,10},{10,9},{11,12},{12,11},... | collective-permute-start | bytes 786440 | tf_op jit(solution)/shard_map/ppermute | solution.py:306
  39.4 0.1 collective-permute-start.8
  39.5 4.0 %collective-permute-done.7.x_odd.refs_1_ = f32[13,32,128]{2,1,0:T(8,128)S(1)} collective-permute-done((f32[13,32,128]{2,1,0:T(8,128)S(1)}, f32[13,32,128]{2,1,0:T(8,128)S(1)}, u32[]{:S(2)}, u32[]{:S(2)}) %collective-permute-start.7) | collective-permute-done | bytes 213024 | tf_op jit(solution)/shard_map/ppermute | solution.py:306
  43.5 0.9 %collective-permute-start.10 = (f32[26,16,128]{2,1,0:T(8,128)S(1)}, f32[26,16,128]{2,1,0:T(8,128)S(1)}, u32[]{:S(2)}, u32[]{:S(2)}) collective-permute-start(f32[26,16,128]{2,1,0:T(8,128)S(1)} %get-tuple-element.26), channel_id=1, source_target_pairs={{0,1},{1,0},{2,3},{3,2},{4,5},{5,4},{6,7},{7,6},{8,9},{9,8},{10,11... | collective-permute-start | bytes 638984 | tf_op jit(solution)/shard_map/ppermute | solution.py:306
  44.4 3.1 %collective-permute-start.11 = (f32[26,16,128]{2,1,0:T(8,128)S(1)}, f32[26,16,128]{2,1,0:T(8,128)S(1)}, u32[]{:S(2)}, u32[]{:S(2)}) collective-permute-start(f32[26,16,128]{2,1,0:T(8,128)S(1)} %get-tuple-element.27), channel_id=1, source_target_pairs={{1,2},{2,1},{3,4},{4,3},{5,6},{6,5},{9,10},{10,9},{11,12},{12,11},... | collective-permute-start | bytes 638984 | tf_op jit(solution)/shard_map/ppermute | solution.py:306
  47.5 4.0 %collective-permute-done.11.refs_5_ = f32[26,16,128]{2,1,0:T(8,128)S(1)} collective-permute-done((f32[26,16,128]{2,1,0:T(8,128)S(1)}, f32[26,16,128]{2,1,0:T(8,128)S(1)}, u32[]{:S(2)}, u32[]{:S(2)}) %collective-permute-start.11) | collective-permute-done | bytes 213024 | tf_op jit(solution)/shard_map/ppermute | solution.py:306
  51.5 3.4 %shard_map.68 = f32[32,32,128]{2,1,0:T(8,128)} custom-call(f32[32,32,128]{2,1,0:T(8,128)S(1)} %get-tuple-element.25.own, f32[13,32,128]{2,1,0:T(8,128)S(1)} %collective-permute-done.6.x_even.refs_0_, f32[13,32,128]{2,1,0:T(8,128)S(1)} %collective-permute-done.7.x_odd.refs_1_, f32[32,16,128]{2,1,0:T(8,128)S(1)} %collective-permute-done.8.refs_2_, ...), custom_call_target="tpu_custom_call" | custom-call | tf_op jit(solution)/shard_map/pallas_call | solution.py:272
  (23 shorter events, 0.3 us)
Async XLA Ops:
  1.3 4.7 %copy-start.1 = (f32[32,32,128]{2,1,0:T(8,128)S(1)}, f32[32,32,128]{2,1,0:T(8,128)}, u32[]{:S(2)}) copy-start(f32[32,32,128]{2,1,0:T(8,128)} %own.1) | copy-start | bytes 1572868
  1.4 4.6 %copy-start = (f32[32,32,128]{2,1,0:T(8,128)S(1)}, f32[32,32,128]{2,1,0:T(8,128)}, u32[]{:S(2)}) copy-start(f32[32,32,128]{2,1,0:T(8,128)} %own_s.1) | copy-start | bytes 1572868
  1.4 11.3 %collective-permute-start = (f32[2,13,32,128]{3,2,1,0:T(8,128)S(1)}, f32[2,13,32,128]{3,2,1,0:T(8,128)S(1)}, u32[]{:S(2)}, u32[]{:S(2)}) collective-permute-start(f32[2,13,32,128]{3,2,1,0:T(8,128)S(1)} %pad_maximum_fusion.2), channel_id=1, source_target_pairs={{0,8},{8,0},{16,24},{24,16},{32,40},{40,32},{48,56},{56,48},{64,72... | collective-permute-start | bytes 1277960 | tf_op jit(solution)/shard_map/ppermute | solution.py:306
  2.7 14.4 %collective-permute-start.1 = (f32[2,13,32,128]{3,2,1,0:T(8,128)S(1)}, f32[2,13,32,128]{3,2,1,0:T(8,128)S(1)}, u32[]{:S(2)}, u32[]{:S(2)}) collective-permute-start(f32[2,13,32,128]{3,2,1,0:T(8,128)S(1)} %pad_maximum_fusion.3), channel_id=1, source_target_pairs={{8,16},{16,8},{24,32},{32,24},{40,48},{48,40},{56,64},{64,56},{72,... | collective-permute-start | bytes 1277960 | tf_op jit(solution)/shard_map/ppermute | solution.py:306
  6.2 16.0 %collective-permute-start.2 = (f32[2,32,16,128]{3,2,1,0:T(8,128)S(1)}, f32[2,32,16,128]{3,2,1,0:T(8,128)S(1)}, u32[]{:S(2)}, u32[]{:S(2)}) collective-permute-start(f32[2,32,16,128]{3,2,1,0:T(8,128)S(1)} %pad_maximum_fusion), channel_id=1, source_target_pairs={{0,1},{1,0},{2,3},{3,2},{4,5},{5,4},{6,7},{7,6},{8,9},{9,8},{10,11... | collective-permute-start | bytes 1572872 | tf_op jit(solution)/shard_map/ppermute | solution.py:306
  7.5 3.8 %copy-start.2 = (s32[2,2,4]{2,1,0:T(2,128)S(1)}, s32[2,2,4]{2,1,0:T(2,128)}, u32[]{:S(2)}) copy-start(s32[2,2,4]{2,1,0:T(2,128)} %band.1) | copy-start | bytes 196
  7.5 3.8 %copy-start.3 = (f32[25]{0:T(128)S(1)}, f32[25]{0:T(128)}, u32[]{:S(2)}) copy-start(f32[25]{0:T(128)} %smooth.1) | copy-start | bytes 304
  7.5 3.8 %copy-start.4 = (f32[25]{0:T(128)S(1)}, f32[25]{0:T(128)}, u32[]{:S(2)}) copy-start(f32[25]{0:T(128)} %slope.1) | copy-start | bytes 304
  7.5 14.7 %collective-permute-start.3 = (f32[2,32,16,128]{3,2,1,0:T(8,128)S(1)}, f32[2,32,16,128]{3,2,1,0:T(8,128)S(1)}, u32[]{:S(2)}, u32[]{:S(2)}) collective-permute-start(f32[2,32,16,128]{3,2,1,0:T(8,128)S(1)} %pad_maximum_fusion.1), channel_id=1, source_target_pairs={{1,2},{2,1},{3,4},{4,3},{5,6},{6,5},{9,10},{10,9},{11,12},{12,11},... | collective-permute-start | bytes 1572872 | tf_op jit(solution)/shard_map/ppermute | solution.py:306
  17.1 5.1 %collective-permute-start.4 = (f32[2,26,16,128]{3,2,1,0:T(8,128)S(1)}, f32[2,26,16,128]{3,2,1,0:T(8,128)S(1)}, u32[]{:S(2)}, u32[]{:S(2)}) collective-permute-start(f32[2,26,16,128]{3,2,1,0:T(8,128)S(1)} %get-tuple-element.21), channel_id=1, source_target_pairs={{0,1},{1,0},{2,3},{3,2},{4,5},{5,4},{6,7},{7,6},{8,9},{9,8},{10,11... | collective-permute-start | bytes 1277960 | tf_op jit(solution)/shard_map/ppermute | solution.py:306
  19.1 9.4 %collective-permute-start.5 = (f32[2,26,16,128]{3,2,1,0:T(8,128)S(1)}, f32[2,26,16,128]{3,2,1,0:T(8,128)S(1)}, u32[]{:S(2)}, u32[]{:S(2)}) collective-permute-start(f32[2,26,16,128]{3,2,1,0:T(8,128)S(1)} %get-tuple-element.22), channel_id=1, source_target_pairs={{1,2},{2,1},{3,4},{4,3},{5,6},{6,5},{9,10},{10,9},{11,12},{12,11},... | collective-permute-start | bytes 1277960 | tf_op jit(solution)/shard_map/ppermute | solution.py:306
  32.6 10.9 %collective-permute-start.7 = (f32[13,32,128]{2,1,0:T(8,128)S(1)}, f32[13,32,128]{2,1,0:T(8,128)S(1)}, u32[]{:S(2)}, u32[]{:S(2)}) collective-permute-start(f32[13,32,128]{2,1,0:T(8,128)S(1)} %get-tuple-element.31), channel_id=1, source_target_pairs={{8,16},{16,8},{24,32},{32,24},{40,48},{48,40},{56,64},{64,56},{72,... | collective-permute-start | bytes 638984 | tf_op jit(solution)/shard_map/ppermute | solution.py:306
  35.8 7.6 %collective-permute-start.6 = (f32[13,32,128]{2,1,0:T(8,128)S(1)}, f32[13,32,128]{2,1,0:T(8,128)S(1)}, u32[]{:S(2)}, u32[]{:S(2)}) collective-permute-start(f32[13,32,128]{2,1,0:T(8,128)S(1)} %get-tuple-element.32), channel_id=1, source_target_pairs={{0,8},{8,0},{16,24},{24,16},{32,40},{40,32},{48,56},{56,48},{64,72... | collective-permute-start | bytes 638984 | tf_op jit(solution)/shard_map/ppermute | solution.py:306
  36.0 11.5 %collective-permute-start.9 = (f32[32,16,128]{2,1,0:T(8,128)S(1)}, f32[32,16,128]{2,1,0:T(8,128)S(1)}, u32[]{:S(2)}, u32[]{:S(2)}) collective-permute-start(f32[32,16,128]{2,1,0:T(8,128)S(1)} %get-tuple-element.29), channel_id=1, source_target_pairs={{1,2},{2,1},{3,4},{4,3},{5,6},{6,5},{9,10},{10,9},{11,12},{12,11},... | collective-permute-start | bytes 786440 | tf_op jit(solution)/shard_map/ppermute | solution.py:306
  39.4 8.1 %collective-permute-start.8 = (f32[32,16,128]{2,1,0:T(8,128)S(1)}, f32[32,16,128]{2,1,0:T(8,128)S(1)}, u32[]{:S(2)}, u32[]{:S(2)}) collective-permute-start(f32[32,16,128]{2,1,0:T(8,128)S(1)} %get-tuple-element.30), channel_id=1, source_target_pairs={{0,1},{1,0},{2,3},{3,2},{4,5},{5,4},{6,7},{7,6},{8,9},{9,8},{10,11... | collective-permute-start | bytes 786440 | tf_op jit(solution)/shard_map/ppermute | solution.py:306
  43.5 4.0 %collective-permute-start.10 = (f32[26,16,128]{2,1,0:T(8,128)S(1)}, f32[26,16,128]{2,1,0:T(8,128)S(1)}, u32[]{:S(2)}, u32[]{:S(2)}) collective-permute-start(f32[26,16,128]{2,1,0:T(8,128)S(1)} %get-tuple-element.26), channel_id=1, source_target_pairs={{0,1},{1,0},{2,3},{3,2},{4,5},{5,4},{6,7},{7,6},{8,9},{9,8},{10,11... | collective-permute-start | bytes 638984 | tf_op jit(solution)/shard_map/ppermute | solution.py:306
  44.4 7.2 %collective-permute-start.11 = (f32[26,16,128]{2,1,0:T(8,128)S(1)}, f32[26,16,128]{2,1,0:T(8,128)S(1)}, u32[]{:S(2)}, u32[]{:S(2)}) collective-permute-start(f32[26,16,128]{2,1,0:T(8,128)S(1)} %get-tuple-element.27), channel_id=1, source_target_pairs={{1,2},{2,1},{3,4},{4,3},{5,6},{6,5},{9,10},{10,9},{11,12},{12,11},... | collective-permute-start | bytes 638984 | tf_op jit(solution)/shard_map/ppermute | solution.py:306

commit v5 on v4

--- a/solution.py
+++ b/solution.py
@@ -119,19 +119,18 @@
     return matrices[4 * RIM :, kind * DEPTH : (kind + 1) * DEPTH]
 
 
-def fill_extended(extended, own, x_even, x_odd, y_even, y_odd, c_even, c_odd):
+def fill_extended(extended, own, x_even, x_odd, y_even, y_odd, even_corner, odd_corner):
     extended[0:SIDE, 0:SIDE, :] = own
     gap = jnp.zeros((SLAB - REACH, WIDE, DEPTH), jnp.float32)
+    columns = (slice(SIDE, SIDE + SLAB), slice(SIDE + SLAB, WIDE))
+    extended[0:SIDE, columns[0], :] = y_even
+    extended[0:SIDE, columns[1], :] = y_odd
     for at, part in enumerate((x_even, x_odd)):
-        start = SIDE + at * SLAB
-        extended[start : start + REACH, 0:SIDE, :] = part
-        extended[start + REACH : start + SLAB, 0:WIDE, :] = gap
-    for at, (part, corner) in enumerate(((y_even, c_even), (y_odd, c_odd))):
-        columns = slice(SIDE + at * SLAB, SIDE + (at + 1) * SLAB)
-        extended[0:SIDE, columns, :] = part
-        for side in range(2):
-            start = SIDE + side * SLAB
-            extended[start : start + REACH, columns, :] = corner[side * REACH : (side + 1) * REACH]
+        rows = slice(SIDE + at * SLAB, SIDE + at * SLAB + REACH)
+        extended[rows, 0:SIDE, :] = part
+        extended[rows.stop : SIDE + (at + 1) * SLAB, 0:WIDE, :] = gap
+        extended[rows, columns[0], :] = even_corner[at * REACH : (at + 1) * REACH]
+        extended[rows, columns[1], :] = odd_corner[at * REACH : (at + 1) * REACH]
 
 
 def stacked_parts(value):
@@ -195,7 +194,7 @@
             finish(at - 1)
 
 
-def advance(x, own, speed, gain, normals, lengths):
+def bending(normals, x):
     lane = lax.broadcasted_iota(jnp.int32, (SIDE, DEPTH), 1)
     at = x + 1
     across = normals[1, at, :, :]
@@ -204,11 +203,10 @@
     bend += (pltpu.roll(across, RIM - 1, 0) - pltpu.roll(across, 1, 0))[0:SIDE]
     bend += jnp.where(lane < DEPTH - 1, pltpu.roll(deep, DEPTH - 1, 1), 0.0)
     bend -= jnp.where(lane > 0, pltpu.roll(deep, 1, 1), 0.0)
-    push = gain[x // (SIDE // 2), :, :] * lengths[at, 0:SIDE, :]
-    return own[x, :, :] - push * (speed[x, :, :] - 0.25 * bend)
-
-
-def speed_stages(extended, matrices, crossed, flat_s, velocity, out):
+    return 0.25 * bend
+
+
+def speed_stages(extended, matrices, crossed, flat_s, velocity, finish):
     along_x_stage(extended, crossed, along_matrix(matrices, 0, RIM + 8))
     matrix = along_matrix(matrices, 1, RIM + 8)
     for pair in range(0, len(OUT_ROWS), 2):
@@ -225,44 +223,69 @@
             preferred_element_type=jnp.float32,
         )
         velocity[at : at + 2, :, :] = got.reshape(2, RIM, DEPTH)
+        if at > 0:
+            finish(at - 2)
+            finish(at - 1)
+
+
+def face_mean(velocity, x):
     lane = lax.broadcasted_iota(jnp.int32, (SIDE, DEPTH), 1)
-    for x in range(SIDE):
-        at = x + 1
-        rim = velocity[at, :, :]
-        centre = rim[0:SIDE]
-        total = centre + velocity[at + 1, 0:SIDE, :] + velocity[at - 1, 0:SIDE, :]
-        total += (pltpu.roll(rim, RIM - 1, 0) + pltpu.roll(rim, 1, 0))[0:SIDE]
-        total += jnp.where(lane < DEPTH - 1, pltpu.roll(centre, DEPTH - 1, 1), 0.0)
-        total += jnp.where(lane > 0, pltpu.roll(centre, 1, 1), 0.0)
-        out[x, :, :] = total / 7.0
-
-
-HALOS = 6
-
-
-def first_kernel(own_s, own, *refs):
+    at = x + 1
+    rim = velocity[at, :, :]
+    centre = rim[0:SIDE]
+    total = centre + velocity[at + 1, 0:SIDE, :] + velocity[at - 1, 0:SIDE, :]
+    total += (pltpu.roll(rim, RIM - 1, 0) + pltpu.roll(rim, 1, 0))[0:SIDE]
+    total += jnp.where(lane < DEPTH - 1, pltpu.roll(centre, DEPTH - 1, 1), 0.0)
+    total += jnp.where(lane > 0, pltpu.roll(centre, 1, 1), 0.0)
+    return total / 7.0
+
+
+HALOS = 5
+
+
+def stacked_halos(halos, part):
+    x_even, x_odd, y_odd = [halo[part] for halo in halos[:3]]
+    even_slab, odd_corner = [halo[...] for halo in halos[3:]]
+    return x_even, x_odd, even_slab[0:SIDE], y_odd, even_slab[SIDE:], odd_corner
+
+
+def bend_kernel(own, *refs):
     halos = refs[:HALOS]
-    matrices, gain, out, speed = refs[HALOS : HALOS + 4]
-    extended_s, crossed_s, flat_v, velocity = refs[HALOS + 4 : HALOS + 8]
-    extended, crossed, flat_s, flat_g, normals, lengths = refs[HALOS + 8 :]
-    fill_extended(extended_s, own_s[...], *[halo[0] for halo in halos])
-    fill_extended(extended, own[...], *[halo[1] for halo in halos])
-    speed_stages(extended_s, matrices, crossed_s, flat_v, velocity, speed)
+    matrices, gain, base, push = refs[HALOS : HALOS + 4]
+    extended, crossed, flat_s, flat_g, normals, lengths = refs[HALOS + 4 :]
+    fill_extended(extended, own[...], *stacked_halos(halos, 1))
 
     def finish(x):
-        out[x, :, :] = advance(x, own, speed, gain, normals, lengths)
+        factor = gain[x // (SIDE // 2), :, :] * lengths[x + 1, 0:SIDE, :]
+        push[x, :, :] = factor
+        base[x, :, :] = own[x, :, :] + factor * bending(normals, x)
 
     gradient_stages(extended, matrices, crossed, flat_s, flat_g, normals, lengths, finish)
 
 
+def speed_kernel(own, *refs):
+    halos = refs[:HALOS]
+    matrices, base, push, out, speed = refs[HALOS : HALOS + 5]
+    extended, crossed, flat_s, velocity = refs[HALOS + 5 :]
+    fill_extended(extended, own[...], *stacked_halos(halos, 0))
+
+    def finish(x):
+        value = face_mean(velocity, x)
+        speed[x, :, :] = value
+        out[x, :, :] = base[x, :, :] - push[x, :, :] * value
+
+    speed_stages(extended, matrices, crossed, flat_s, velocity, finish)
+
+
 def later_kernel(own, *refs):
-    halos = refs[:HALOS]
-    matrices, gain, speed, out = refs[HALOS : HALOS + 4]
-    extended, crossed, flat_s, flat_g, normals, lengths = refs[HALOS + 4 :]
+    halos = refs[: HALOS + 1]
+    matrices, gain, speed, out = refs[HALOS + 1 : HALOS + 5]
+    extended, crossed, flat_s, flat_g, normals, lengths = refs[HALOS + 5 :]
     fill_extended(extended, own[...], *[halo[...] for halo in halos])
 
     def finish(x):
-        out[x, :, :] = advance(x, own, speed, gain, normals, lengths)
+        factor = gain[x // (SIDE // 2), :, :] * lengths[x + 1, 0:SIDE, :]
+        out[x, :, :] = own[x, :, :] - factor * (speed[x, :, :] - bending(normals, x))
 
     gradient_stages(extended, matrices, crossed, flat_s, flat_g, normals, lengths, finish)
 
@@ -279,24 +302,47 @@
     )(*arrays)
 
 
-def corner_kernel(x_even, x_odd, even, odd):
+def corner_kernel(part, own, x_even, x_odd, even, odd):
     parity = lax.axis_index("gy") & 1
-    for side, target in enumerate((even, odd)):
-        start = pl.multiple_of(jnp.where(parity == side, SIDE - SLAB, 0), SLAB)
-        for at, source in enumerate((x_even, x_odd)):
-            target[..., at * REACH : (at + 1) * REACH, :, :] = source[..., pl.ds(start, SLAB), :]
-
-
-def corner_sides(x_halos):
-    shape = x_halos[0].shape[:-3] + (2 * REACH, SLAB, DEPTH)
-    out = jax.ShapeDtypeStruct(shape, jnp.float32)
+    starts = [
+        pl.multiple_of(jnp.where(parity == side, SIDE - SLAB, 0), SLAB) for side in range(2)
+    ]
+    offset = even.shape[0] - 2 * REACH
+    if offset:
+        even[0:SIDE, :, :] = own[:, pl.ds(starts[0], SLAB), :]
+    for at, x_halo in enumerate((x_even, x_odd)):
+        source = x_halo if part is None else x_halo.at[part]
+        rows = slice(at * REACH, (at + 1) * REACH)
+        even[offset + rows.start : offset + rows.stop, :, :] = source[:, pl.ds(starts[0], SLAB), :]
+        odd[rows, :, :] = source[:, pl.ds(starts[1], SLAB), :]
+
+
+def corner_sides(own, x_halos, part=None):
+    offset = 0 if part is None else SIDE
     return pl.pallas_call(
-        corner_kernel,
-        out_shape=(out, out),
-        in_specs=[VMEM] * 2,
+        functools.partial(corner_kernel, part),
+        out_shape=(
+            jax.ShapeDtypeStruct((offset + 2 * REACH, SLAB, DEPTH), jnp.float32),
+            jax.ShapeDtypeStruct((2 * REACH, SLAB, DEPTH), jnp.float32),
+        ),
+        in_specs=[VMEM] * 3,
         out_specs=(VMEM, VMEM),
         compiler_params=SMALL,
-    )(*x_halos)
+    )(own, *x_halos)
+
+
+def copy_kernel(source, target):
+    target[...] = source[...]
+
+
+def settle(block):
+    return pl.pallas_call(
+        copy_kernel,
+        out_shape=jax.ShapeDtypeStruct(block.shape, block.dtype),
+        in_specs=[VMEM],
+        out_specs=VMEM,
+        compiler_params=SMALL,
+    )(block)
 
 
 def swap(block, axis, first):
@@ -315,22 +361,42 @@
     )
 
 
+def stack_kernel(*refs):
+    count = (len(refs) - 2) // 2
+    for at in range(count):
+        for side in range(2):
+            refs[2 * count + side][at] = refs[2 * at + side][...]
+
+
 def stacked_sides(blocks, dim, width, parity):
-    return [jnp.stack(side) for side in zip(*[both_sides(b, dim, width, parity) for b in blocks])]
+    pieces = [piece for block in blocks for piece in both_sides(block, dim, width, parity)]
+    out = jax.ShapeDtypeStruct((len(blocks), *pieces[0].shape), jnp.float32)
+    return pl.pallas_call(
+        stack_kernel,
+        out_shape=(out, out),
+        in_specs=[VMEM] * len(pieces),
+        out_specs=(VMEM, VMEM),
+        compiler_params=SMALL,
+    )(*pieces)
 
 
 def swap_sides(pieces, axis):
-    return swap(pieces[0], axis, 0), swap(pieces[1], axis, 1)
+    odd = swap(pieces[1], axis, 1)
+    even = swap(pieces[0], axis, 0)
+    return even, odd
 
 
 def per_device(level_set, sensitivity, smooth_taps, slope_taps, band, time_step):
     parity = [lax.axis_index(axis) & 1 for axis in ("gx", "gy")]
     fields = [sensitivity, level_set]
     x_halos = swap_sides(stacked_sides(fields, 0, REACH, parity[0]), "gx")
-    y_halos = swap_sides(stacked_sides(fields, 1, SLAB, parity[1]), "gy")
+    y_odd = swap(jnp.stack([both_sides(f, 1, SLAB, parity[1])[1] for f in fields]), "gy", 1)
     matrices = prepare(smooth_taps, slope_taps, band, time_step)
+    x_halos = (x_halos[0], settle(x_halos[1]))
     x_halos, matrices = lax.optimization_barrier((x_halos, matrices))
-    corners = swap_sides(corner_sides(x_halos), "gy")
+    matrices, gain = matrices
+    corners = swap_sides(corner_sides(level_set, x_halos, 1), "gy")
+    corners_s = swap_sides(corner_sides(sensitivity, x_halos, 0), "gy")
     rim = SIDE + 2
     gradient_scratch = [
         (WIDE, WIDE + 8, DEPTH), (WIDE, 2 * RIM + 8, DEPTH), (rim, 2 * RIM, DEPTH),
@@ -339,16 +405,19 @@
     speed_scratch = [
         (WIDE, WIDE + 8, DEPTH), (WIDE, RIM + 16, DEPTH), (rim, RIM, DEPTH), (rim, RIM, DEPTH)
     ]
+    base, push = call_kernel(
+        bend_kernel, (level_set, *x_halos, y_odd, *corners, matrices, gain), 2, gradient_scratch
+    )
     phi, speed = call_kernel(
-        first_kernel, (*fields, *x_halos, *y_halos, *corners, *matrices), 2,
-        speed_scratch + gradient_scratch,
+        speed_kernel, (sensitivity, *x_halos, y_odd, *corners_s, matrices, base, push), 2,
+        speed_scratch,
     )
     for _ in range(1, UPDATES):
         x_halos = swap_sides(both_sides(phi, 0, REACH, parity[0]), "gx")
         y_halos = swap_sides(both_sides(phi, 1, SLAB, parity[1]), "gy")
-        corners = swap_sides(corner_sides(x_halos), "gy")
+        corners = swap_sides(corner_sides(phi, x_halos), "gy")
         (phi,) = call_kernel(
-            later_kernel, (phi, *x_halos, *y_halos, *corners, *matrices, speed), 1, gradient_scratch,
+            later_kernel, (phi, *x_halos, *y_halos, *corners, matrices, gain, speed), 1, gradient_scratch,
         )
     return phi
 

time: 55.2 us -> 53.5 us (0.969)
  waiting for transfers between devices: 18.6 us -> 14.7 us
  starting transfers between devices: 24.8 us -> 26.6 us
    ppermute x12 -> x13, waiting for transfers between devices: 18.6 us -> 14.7 us  [swap(): return lax.ppermute(block, axis, pairs)]
    ppermute x12 -> x13, starting transfers between devices: 24.8 us -> 26.6 us  [swap(): return lax.ppermute(block, axis, pairs)]
    another operation x2, local copies, waits for them, and re-layouts: 1.42 us -> 0.04 us  [per_device(): jnp.stack([both_sides(f, 1, SLAB, parity[1])[1] for f in fields])]
    dynamic_slice x2 -> x3, local copies, waits for them, and re-layouts: 0.08 us -> 1.39 us  [both_sides(): lax.dynamic_slice_in_dim(block, length - width - high, width, dim)]
    pallas_call x2 -> x3, Pallas kernels: 7.45 us -> 7.69 us  [call_kernel(): pl.pallas_call(body, out_shape=(shape,) * outputs, in_specs=[VMEM] * len(...]
  transfers between devices with their start and end apart: 12 -> 13, of which waited for: 4 -> 5; matrix products, arithmetic and copies ran while one was open for 0% -> 0% of each run, Pallas kernels for 3% -> 8%
where the time goes in v5:
time: 53.5 us; the launch traced here: 52.9 us
  starting transfers between devices  26.6 us (50%)
  waiting for transfers between devices  14.7 us (27%)
  Pallas kernels  9.27 us (17%)
  local copies, waits for them, and re-layouts  1.46 us (3%)
  between operations  0.92 us (2%)
    ppermute x13, starting transfers between devices, swap(): return lax.ppermute(block, axis, pairs)  26.6 us
    ppermute x13, waiting for transfers between devices, swap(): return lax.ppermute(block, axis, pairs)  14.7 us
    pallas_call x3, Pallas kernels, call_kernel(): pl.pallas_call(body, out_shape=(shape,) * outputs, in_specs=[VMEM] * len(...  7.69 us
    dynamic_slice x3, local copies, waits for them, and re-layouts, both_sides(): lax.dynamic_slice_in_dim(block, length - width - high, width, dim)  1.39 us
    pallas_call x1, Pallas kernels, prepare(): pl.pallas_call(prepare_kernel, out_shape=(jax.ShapeDtypeStruct((4 * RIM +...  1.36 us
  transfers between devices with their start and end apart: 13, of which 5 were waited for; matrix products, arithmetic and copies ran while one was open for 0% of the time, Pallas kernels for 8%

profile of v5, /device:TPU:41, one launch (start us, length us, event | category | flops | bytes accessed | tf_op | source)
XLA Modules:
  0.0 52.9 jit_solution(15353055716340536388)
XLA Ops:
  0.0 1.3 %constant_dynamic-slice_fusion.4 = (f32[13,32,128]{2,1,0:T(8,128)S(1)}, f32[13,32,128]{2,1,0:T(8,128)S(1)}, f32[13,32,128]{2,1,0:T(8,128)S(1)}, f32[13,32,128]{2,1,0:T(8,128)S(1)}) fusion(f32[32,32,128]{2,1,0:T(8,128)} %own.6, s32[]{:T(128)S(6)} %select_n.26, s32[]{:T(128)S(6)} %select_n.25, f32[32,32,128]{2,1,0:T(8,128)} %own.7), kind=kLoop, calls=%fused_computation.7 | loop fusion | bytes 1703944 | tf_op jit(solution)/shard_map/dynamic_slice | solution.py:360
  1.3 0.1 shard_map.64
  1.4 4.1 %collective-permute-start.1 = (f32[2,13,32,128]{3,2,1,0:T(8,128)S(1)}, f32[2,13,32,128]{3,2,1,0:T(8,128)S(1)}, u32[]{:S(2)}, u32[]{:S(2)}) collective-permute-start(f32[2,13,32,128]{3,2,1,0:T(8,128)S(1)} %get-tuple-element.24), channel_id=1, source_target_pairs={{8,16},{16,8},{24,32},{32,24},{40,48},{48,40},{56,64},{64,56},{72,... | collective-permute-start | bytes 1277960 | tf_op jit(solution)/shard_map/ppermute | solution.py:352
  5.5 0.5 collective-permute-start
  6.1 4.3 %collective-permute-start.2 = (f32[2,32,16,128]{3,2,1,0:T(8,128)S(1)}, f32[2,32,16,128]{3,2,1,0:T(8,128)S(1)}, u32[]{:S(2)}, u32[]{:S(2)}) collective-permute-start(f32[2,32,16,128]{3,2,1,0:T(8,128)S(1)} %pad_maximum_fusion), channel_id=1, source_target_pairs={{1,2},{2,1},{3,4},{4,3},{5,6},{6,5},{9,10},{10,9},{11,12},{12,11},... | collective-permute-start | bytes 1572872 | tf_op jit(solution)/shard_map/ppermute | solution.py:352
  11.1 1.4 %shard_map.66 = (bf16[544,256]{1,0:T(8,128)(2,1)S(1)}, f32[2,32,128]{2,1,0:T(8,128)S(1)}) custom-call(f32[25]{0:T(128)S(1)} %copy-done.3, f32[25]{0:T(128)S(1)} %copy-done.4, s32[2,2,4]{2,1,0:T(2,128)S(1)} %copy-done.2, f32[1]{0:T(128)S(6)} %copy.7.step), custom_call_target="tpu_custom_call" | custom-call | flops 1000000 | bytes 1000000 | tf_op jit(solution)/shard_map/pallas_call | solution.py:101
  12.5 3.7 %collective-permute-done.1.source = f32[2,13,32,128]{3,2,1,0:T(8,128)S(1)} collective-permute-done((f32[2,13,32,128]{3,2,1,0:T(8,128)S(1)}, f32[2,13,32,128]{3,2,1,0:T(8,128)S(1)}, u32[]{:S(2)}, u32[]{:S(2)}) %collective-permute-start.1) | collective-permute-done | bytes 426016 | tf_op jit(solution)/shard_map/ppermute | solution.py:352
  16.3 1.6 %collective-permute-start.5 = (f32[58,16,128]{2,1,0:T(8,128)S(1)}, f32[58,16,128]{2,1,0:T(8,128)S(1)}, u32[]{:S(2)}, u32[]{:S(2)}) collective-permute-start(f32[58,16,128]{2,1,0:T(8,128)S(1)} %get-tuple-element.32), channel_id=1, source_target_pairs={{0,1},{1,0},{2,3},{3,2},{4,5},{5,4},{6,7},{7,6},{8,9},{9,8},{10,11... | collective-permute-start | bytes 1425416 | tf_op jit(solution)/shard_map/ppermute | solution.py:352
  18.0 0.1 collective-permute-start.3
  18.1 3.6 %collective-permute-start.6 = (f32[26,16,128]{2,1,0:T(8,128)S(1)}, f32[26,16,128]{2,1,0:T(8,128)S(1)}, u32[]{:S(2)}, u32[]{:S(2)}) collective-permute-start(f32[26,16,128]{2,1,0:T(8,128)S(1)} %get-tuple-element.33), channel_id=1, source_target_pairs={{1,2},{2,1},{3,4},{4,3},{5,6},{6,5},{9,10},{10,9},{11,12},{12,11},... | collective-permute-start | bytes 638984 | tf_op jit(solution)/shard_map/ppermute | solution.py:352
  21.7 2.0 %collective-permute-start.4 = (f32[26,16,128]{2,1,0:T(8,128)S(1)}, f32[26,16,128]{2,1,0:T(8,128)S(1)}, u32[]{:S(2)}, u32[]{:S(2)}) collective-permute-start(f32[26,16,128]{2,1,0:T(8,128)S(1)} %get-tuple-element.30), channel_id=1, source_target_pairs={{1,2},{2,1},{3,4},{4,3},{5,6},{6,5},{9,10},{10,9},{11,12},{12,11},... | collective-permute-start | bytes 638984 | tf_op jit(solution)/shard_map/ppermute | solution.py:352
  23.7 1.9 %collective-permute-done.6.refs_4_ = f32[26,16,128]{2,1,0:T(8,128)S(1)} collective-permute-done((f32[26,16,128]{2,1,0:T(8,128)S(1)}, f32[26,16,128]{2,1,0:T(8,128)S(1)}, u32[]{:S(2)}, u32[]{:S(2)}) %collective-permute-start.6) | collective-permute-done | bytes 213024 | tf_op jit(solution)/shard_map/ppermute | solution.py:352
  25.6 2.6 %shard_map.69 = (f32[32,32,128]{2,1,0:T(8,128)S(1)}, f32[32,32,128]{2,1,0:T(8,128)S(1)}) custom-call(f32[32,32,128]{2,1,0:T(8,128)S(1)} %copy-done, f32[2,13,32,128]{3,2,1,0:T(8,128)S(1)} %collective-permute-done.x_even.refs_0_, f32[2,13,32,128]{3,2,1,0:T(8,128)S(1)} %shard_map.65.x_odd.refs_1_, f32[2,32,16,128]{3,2,1,0:T(8,128)S(1)} %collective-permute-done.2.refs_2_, ...), custom_call_target="tpu_custom_call" | custom-call | tf_op jit(solution)/shard_map/pallas_call | solution.py:295
  28.2 0.6 %collective-permute-done.4.refs_4_ = f32[26,16,128]{2,1,0:T(8,128)S(1)} collective-permute-done((f32[26,16,128]{2,1,0:T(8,128)S(1)}, f32[26,16,128]{2,1,0:T(8,128)S(1)}, u32[]{:S(2)}, u32[]{:S(2)}) %collective-permute-start.4) | collective-permute-done | bytes 213024 | tf_op jit(solution)/shard_map/ppermute | solution.py:352
  28.8 1.6 %shard_map.70 = (f32[32,32,128]{2,1,0:T(8,128)S(1)}, f32[32,32,128]{2,1,0:T(8,128)S(1)}) custom-call(f32[32,32,128]{2,1,0:T(8,128)S(1)} %copy-done.1, f32[2,13,32,128]{3,2,1,0:T(8,128)S(1)} %collective-permute-done.x_even.refs_0_, f32[2,13,32,128]{3,2,1,0:T(8,128)S(1)} %shard_map.65.x_odd.refs_1_, f32[2,32,16,128]{3,2,1,0:T(8,128)S(1)} %collective-permute-done.2.refs_2_, ...), custom_call_target="tpu_custom_call" | custom-call | tf_op jit(solution)/shard_map/pallas_call | solution.py:295
  30.5 3.9 %collective-permute-start.8 = (f32[13,32,128]{2,1,0:T(8,128)S(1)}, f32[13,32,128]{2,1,0:T(8,128)S(1)}, u32[]{:S(2)}, u32[]{:S(2)}) collective-permute-start(f32[13,32,128]{2,1,0:T(8,128)S(1)} %get-tuple-element.43), channel_id=1, source_target_pairs={{8,16},{16,8},{24,32},{32,24},{40,48},{48,40},{56,64},{64,56},{72,... | collective-permute-start | bytes 638984 | tf_op jit(solution)/shard_map/ppermute | solution.py:352
  34.5 0.1 collective-permute-start.7
  34.6 2.9 %collective-permute-start.10 = (f32[32,16,128]{2,1,0:T(8,128)S(1)}, f32[32,16,128]{2,1,0:T(8,128)S(1)}, u32[]{:S(2)}, u32[]{:S(2)}) collective-permute-start(f32[32,16,128]{2,1,0:T(8,128)S(1)} %get-tuple-element.41), channel_id=1, source_target_pairs={{1,2},{2,1},{3,4},{4,3},{5,6},{6,5},{9,10},{10,9},{11,12},{12,11},... | collective-permute-start | bytes 786440 | tf_op jit(solution)/shard_map/ppermute | solution.py:352
  37.6 0.1 collective-permute-start.9
  37.7 4.1 %collective-permute-done.8.x_odd.refs_1_ = f32[13,32,128]{2,1,0:T(8,128)S(1)} collective-permute-done((f32[13,32,128]{2,1,0:T(8,128)S(1)}, f32[13,32,128]{2,1,0:T(8,128)S(1)}, u32[]{:S(2)}, u32[]{:S(2)}) %collective-permute-start.8) | collective-permute-done | bytes 213024 | tf_op jit(solution)/shard_map/ppermute | solution.py:352
  41.8 0.5 %collective-permute-start.11 = (f32[26,16,128]{2,1,0:T(8,128)S(1)}, f32[26,16,128]{2,1,0:T(8,128)S(1)}, u32[]{:S(2)}, u32[]{:S(2)}) collective-permute-start(f32[26,16,128]{2,1,0:T(8,128)S(1)} %get-tuple-element.38), channel_id=1, source_target_pairs={{0,1},{1,0},{2,3},{3,2},{4,5},{5,4},{6,7},{7,6},{8,9},{9,8},{10,11... | collective-permute-start | bytes 638984 | tf_op jit(solution)/shard_map/ppermute | solution.py:352
  42.3 2.8 %collective-permute-start.12 = (f32[26,16,128]{2,1,0:T(8,128)S(1)}, f32[26,16,128]{2,1,0:T(8,128)S(1)}, u32[]{:S(2)}, u32[]{:S(2)}) collective-permute-start(f32[26,16,128]{2,1,0:T(8,128)S(1)} %get-tuple-element.39), channel_id=1, source_target_pairs={{1,2},{2,1},{3,4},{4,3},{5,6},{6,5},{9,10},{10,9},{11,12},{12,11},... | collective-permute-start | bytes 638984 | tf_op jit(solution)/shard_map/ppermute | solution.py:352
  45.2 4.3 %collective-permute-done.12.refs_5_ = f32[26,16,128]{2,1,0:T(8,128)S(1)} collective-permute-done((f32[26,16,128]{2,1,0:T(8,128)S(1)}, f32[26,16,128]{2,1,0:T(8,128)S(1)}, u32[]{:S(2)}, u32[]{:S(2)}) %collective-permute-start.12) | collective-permute-done | bytes 213024 | tf_op jit(solution)/shard_map/ppermute | solution.py:352
  49.5 3.4 %shard_map.72 = f32[32,32,128]{2,1,0:T(8,128)} custom-call(f32[32,32,128]{2,1,0:T(8,128)S(1)} %get-tuple-element.37.own, f32[13,32,128]{2,1,0:T(8,128)S(1)} %collective-permute-done.7.x_even.refs_0_, f32[13,32,128]{2,1,0:T(8,128)S(1)} %collective-permute-done.8.x_odd.refs_1_, f32[32,16,128]{2,1,0:T(8,128)S(1)} %collective-permute-done.9.refs_2_, ...), custom_call_target="tpu_custom_call" | custom-call | tf_op jit(solution)/shard_map/pallas_call | solution.py:295
  (27 shorter events, 0.4 us)
Async XLA Ops:
  1.3 4.6 %copy-start = (f32[32,32,128]{2,1,0:T(8,128)S(1)}, f32[32,32,128]{2,1,0:T(8,128)}, u32[]{:S(2)}) copy-start(f32[32,32,128]{2,1,0:T(8,128)} %own.6) | copy-start | bytes 1572868
  1.3 4.7 %copy-start.1 = (f32[32,32,128]{2,1,0:T(8,128)S(1)}, f32[32,32,128]{2,1,0:T(8,128)}, u32[]{:S(2)}) copy-start(f32[32,32,128]{2,1,0:T(8,128)} %own.7) | copy-start | bytes 1572868
  1.4 14.8 %collective-permute-start.1 = (f32[2,13,32,128]{3,2,1,0:T(8,128)S(1)}, f32[2,13,32,128]{3,2,1,0:T(8,128)S(1)}, u32[]{:S(2)}, u32[]{:S(2)}) collective-permute-start(f32[2,13,32,128]{3,2,1,0:T(8,128)S(1)} %get-tuple-element.24), channel_id=1, source_target_pairs={{8,16},{16,8},{24,32},{32,24},{40,48},{48,40},{56,64},{64,56},{72,... | collective-permute-start | bytes 1277960 | tf_op jit(solution)/shard_map/ppermute | solution.py:352
  5.5 10.8 %collective-permute-start = (f32[2,13,32,128]{3,2,1,0:T(8,128)S(1)}, f32[2,13,32,128]{3,2,1,0:T(8,128)S(1)}, u32[]{:S(2)}, u32[]{:S(2)}) collective-permute-start(f32[2,13,32,128]{3,2,1,0:T(8,128)S(1)} %get-tuple-element.23), channel_id=1, source_target_pairs={{0,8},{8,0},{16,24},{24,16},{32,40},{40,32},{48,56},{56,48},{64,72... | collective-permute-start | bytes 1277960 | tf_op jit(solution)/shard_map/ppermute | solution.py:352
  6.0 5.1 %copy-start.2 = (s32[2,2,4]{2,1,0:T(2,128)S(1)}, s32[2,2,4]{2,1,0:T(2,128)}, u32[]{:S(2)}) copy-start(s32[2,2,4]{2,1,0:T(2,128)} %band.1) | copy-start | bytes 196
  6.1 5.0 %copy-start.3 = (f32[25]{0:T(128)S(1)}, f32[25]{0:T(128)}, u32[]{:S(2)}) copy-start(f32[25]{0:T(128)} %smooth.1) | copy-start | bytes 304
  6.1 5.0 %copy-start.4 = (f32[25]{0:T(128)S(1)}, f32[25]{0:T(128)}, u32[]{:S(2)}) copy-start(f32[25]{0:T(128)} %slope.1) | copy-start | bytes 304
  6.1 17.6 %collective-permute-start.2 = (f32[2,32,16,128]{3,2,1,0:T(8,128)S(1)}, f32[2,32,16,128]{3,2,1,0:T(8,128)S(1)}, u32[]{:S(2)}, u32[]{:S(2)}) collective-permute-start(f32[2,32,16,128]{3,2,1,0:T(8,128)S(1)} %pad_maximum_fusion), channel_id=1, source_target_pairs={{1,2},{2,1},{3,4},{4,3},{5,6},{6,5},{9,10},{10,9},{11,12},{12,11},... | collective-permute-start | bytes 1572872 | tf_op jit(solution)/shard_map/ppermute | solution.py:352
  16.3 9.2 %collective-permute-start.5 = (f32[58,16,128]{2,1,0:T(8,128)S(1)}, f32[58,16,128]{2,1,0:T(8,128)S(1)}, u32[]{:S(2)}, u32[]{:S(2)}) collective-permute-start(f32[58,16,128]{2,1,0:T(8,128)S(1)} %get-tuple-element.32), channel_id=1, source_target_pairs={{0,1},{1,0},{2,3},{3,2},{4,5},{5,4},{6,7},{7,6},{8,9},{9,8},{10,11... | collective-permute-start | bytes 1425416 | tf_op jit(solution)/shard_map/ppermute | solution.py:352
  18.0 10.8 %collective-permute-start.3 = (f32[58,16,128]{2,1,0:T(8,128)S(1)}, f32[58,16,128]{2,1,0:T(8,128)S(1)}, u32[]{:S(2)}, u32[]{:S(2)}) collective-permute-start(f32[58,16,128]{2,1,0:T(8,128)S(1)} %get-tuple-element.29), channel_id=1, source_target_pairs={{0,1},{1,0},{2,3},{3,2},{4,5},{5,4},{6,7},{7,6},{8,9},{9,8},{10,11... | collective-permute-start | bytes 1425416 | tf_op jit(solution)/shard_map/ppermute | solution.py:352
  18.1 7.4 %collective-permute-start.6 = (f32[26,16,128]{2,1,0:T(8,128)S(1)}, f32[26,16,128]{2,1,0:T(8,128)S(1)}, u32[]{:S(2)}, u32[]{:S(2)}) collective-permute-start(f32[26,16,128]{2,1,0:T(8,128)S(1)} %get-tuple-element.33), channel_id=1, source_target_pairs={{1,2},{2,1},{3,4},{4,3},{5,6},{6,5},{9,10},{10,9},{11,12},{12,11},... | collective-permute-start | bytes 638984 | tf_op jit(solution)/shard_map/ppermute | solution.py:352
  21.7 7.2 %collective-permute-start.4 = (f32[26,16,128]{2,1,0:T(8,128)S(1)}, f32[26,16,128]{2,1,0:T(8,128)S(1)}, u32[]{:S(2)}, u32[]{:S(2)}) collective-permute-start(f32[26,16,128]{2,1,0:T(8,128)S(1)} %get-tuple-element.30), channel_id=1, source_target_pairs={{1,2},{2,1},{3,4},{4,3},{5,6},{6,5},{9,10},{10,9},{11,12},{12,11},... | collective-permute-start | bytes 638984 | tf_op jit(solution)/shard_map/ppermute | solution.py:352
  30.5 11.2 %collective-permute-start.8 = (f32[13,32,128]{2,1,0:T(8,128)S(1)}, f32[13,32,128]{2,1,0:T(8,128)S(1)}, u32[]{:S(2)}, u32[]{:S(2)}) collective-permute-start(f32[13,32,128]{2,1,0:T(8,128)S(1)} %get-tuple-element.43), channel_id=1, source_target_pairs={{8,16},{16,8},{24,32},{32,24},{40,48},{48,40},{56,64},{64,56},{72,... | collective-permute-start | bytes 638984 | tf_op jit(solution)/shard_map/ppermute | solution.py:352
  34.5 7.3 %collective-permute-start.7 = (f32[13,32,128]{2,1,0:T(8,128)S(1)}, f32[13,32,128]{2,1,0:T(8,128)S(1)}, u32[]{:S(2)}, u32[]{:S(2)}) collective-permute-start(f32[13,32,128]{2,1,0:T(8,128)S(1)} %get-tuple-element.44), channel_id=1, source_target_pairs={{0,8},{8,0},{16,24},{24,16},{32,40},{40,32},{48,56},{56,48},{64,72... | collective-permute-start | bytes 638984 | tf_op jit(solution)/shard_map/ppermute | solution.py:352
  34.6 10.5 %collective-permute-start.10 = (f32[32,16,128]{2,1,0:T(8,128)S(1)}, f32[32,16,128]{2,1,0:T(8,128)S(1)}, u32[]{:S(2)}, u32[]{:S(2)}) collective-permute-start(f32[32,16,128]{2,1,0:T(8,128)S(1)} %get-tuple-element.41), channel_id=1, source_target_pairs={{1,2},{2,1},{3,4},{4,3},{5,6},{6,5},{9,10},{10,9},{11,12},{12,11},... | collective-permute-start | bytes 786440 | tf_op jit(solution)/shard_map/ppermute | solution.py:352
  37.6 7.6 %collective-permute-start.9 = (f32[32,16,128]{2,1,0:T(8,128)S(1)}, f32[32,16,128]{2,1,0:T(8,128)S(1)}, u32[]{:S(2)}, u32[]{:S(2)}) collective-permute-start(f32[32,16,128]{2,1,0:T(8,128)S(1)} %get-tuple-element.42), channel_id=1, source_target_pairs={{0,1},{1,0},{2,3},{3,2},{4,5},{5,4},{6,7},{7,6},{8,9},{9,8},{10,11... | collective-permute-start | bytes 786440 | tf_op jit(solution)/shard_map/ppermute | solution.py:352
  41.8 3.4 %collective-permute-start.11 = (f32[26,16,128]{2,1,0:T(8,128)S(1)}, f32[26,16,128]{2,1,0:T(8,128)S(1)}, u32[]{:S(2)}, u32[]{:S(2)}) collective-permute-start(f32[26,16,128]{2,1,0:T(8,128)S(1)} %get-tuple-element.38), channel_id=1, source_target_pairs={{0,1},{1,0},{2,3},{3,2},{4,5},{5,4},{6,7},{7,6},{8,9},{9,8},{10,11... | collective-permute-start | bytes 638984 | tf_op jit(solution)/shard_map/ppermute | solution.py:352
  42.3 7.2 %collective-permute-start.12 = (f32[26,16,128]{2,1,0:T(8,128)S(1)}, f32[26,16,128]{2,1,0:T(8,128)S(1)}, u32[]{:S(2)}, u32[]{:S(2)}) collective-permute-start(f32[26,16,128]{2,1,0:T(8,128)S(1)} %get-tuple-element.39), channel_id=1, source_target_pairs={{1,2},{2,1},{3,4},{4,3},{5,6},{6,5},{9,10},{10,9},{11,12},{12,11},... | collective-permute-start | bytes 638984 | tf_op jit(solution)/shard_map/ppermute | solution.py:352

commit v6 on v5

--- a/solution.py
+++ b/solution.py
@@ -1,5 +1,3 @@
-import functools
-
 import jax
 import jax.numpy as jnp
 from jax import lax
@@ -244,9 +242,8 @@
 
 
 def stacked_halos(halos, part):
-    x_even, x_odd, y_odd = [halo[part] for halo in halos[:3]]
-    even_slab, odd_corner = [halo[...] for halo in halos[3:]]
-    return x_even, x_odd, even_slab[0:SIDE], y_odd, even_slab[SIDE:], odd_corner
+    x_even, x_odd, even_slab, odd_corner = [halos[at][...] for at in (0, 1, 3, 4)]
+    return x_even, x_odd, even_slab[0:SIDE], halos[2][part], even_slab[SIDE:], odd_corner
 
 
 def bend_kernel(own, *refs):
@@ -302,7 +299,7 @@
     )(*arrays)
 
 
-def corner_kernel(part, own, x_even, x_odd, even, odd):
+def corner_kernel(own, x_even, x_odd, even, odd):
     parity = lax.axis_index("gy") & 1
     starts = [
         pl.multiple_of(jnp.where(parity == side, SIDE - SLAB, 0), SLAB) for side in range(2)
@@ -310,17 +307,15 @@
     offset = even.shape[0] - 2 * REACH
     if offset:
         even[0:SIDE, :, :] = own[:, pl.ds(starts[0], SLAB), :]
-    for at, x_halo in enumerate((x_even, x_odd)):
-        source = x_halo if part is None else x_halo.at[part]
+    for at, source in enumerate((x_even, x_odd)):
         rows = slice(at * REACH, (at + 1) * REACH)
         even[offset + rows.start : offset + rows.stop, :, :] = source[:, pl.ds(starts[0], SLAB), :]
         odd[rows, :, :] = source[:, pl.ds(starts[1], SLAB), :]
 
 
-def corner_sides(own, x_halos, part=None):
-    offset = 0 if part is None else SIDE
+def corner_sides(own, x_halos, offset=0):
     return pl.pallas_call(
-        functools.partial(corner_kernel, part),
+        corner_kernel,
         out_shape=(
             jax.ShapeDtypeStruct((offset + 2 * REACH, SLAB, DEPTH), jnp.float32),
             jax.ShapeDtypeStruct((2 * REACH, SLAB, DEPTH), jnp.float32),
@@ -361,25 +356,6 @@
     )
 
 
-def stack_kernel(*refs):
-    count = (len(refs) - 2) // 2
-    for at in range(count):
-        for side in range(2):
-            refs[2 * count + side][at] = refs[2 * at + side][...]
-
-
-def stacked_sides(blocks, dim, width, parity):
-    pieces = [piece for block in blocks for piece in both_sides(block, dim, width, parity)]
-    out = jax.ShapeDtypeStruct((len(blocks), *pieces[0].shape), jnp.float32)
-    return pl.pallas_call(
-        stack_kernel,
-        out_shape=(out, out),
-        in_specs=[VMEM] * len(pieces),
-        out_specs=(VMEM, VMEM),
-        compiler_params=SMALL,
-    )(*pieces)
-
-
 def swap_sides(pieces, axis):
     odd = swap(pieces[1], axis, 1)
     even = swap(pieces[0], axis, 0)
@@ -389,14 +365,17 @@
 def per_device(level_set, sensitivity, smooth_taps, slope_taps, band, time_step):
     parity = [lax.axis_index(axis) & 1 for axis in ("gx", "gy")]
     fields = [sensitivity, level_set]
-    x_halos = swap_sides(stacked_sides(fields, 0, REACH, parity[0]), "gx")
+    x_halos = swap_sides(both_sides(level_set, 0, REACH, parity[0]), "gx")
+    x_halos_s = swap_sides(both_sides(sensitivity, 0, REACH, parity[0]), "gx")
     y_odd = swap(jnp.stack([both_sides(f, 1, SLAB, parity[1])[1] for f in fields]), "gy", 1)
     matrices = prepare(smooth_taps, slope_taps, band, time_step)
     x_halos = (x_halos[0], settle(x_halos[1]))
-    x_halos, matrices = lax.optimization_barrier((x_halos, matrices))
     matrices, gain = matrices
-    corners = swap_sides(corner_sides(level_set, x_halos, 1), "gy")
-    corners_s = swap_sides(corner_sides(sensitivity, x_halos, 0), "gy")
+    pieces = corner_sides(level_set, x_halos, SIDE)
+    corners = swap_sides(pieces, "gy")
+    x_odd, matrices, gain = lax.optimization_barrier((x_halos_s[1], matrices, gain))
+    x_halos_s = (x_halos_s[0], settle(x_odd))
+    corners_s = swap_sides(corner_sides(sensitivity, x_halos_s, SIDE), "gy")
     rim = SIDE + 2
     gradient_scratch = [
         (WIDE, WIDE + 8, DEPTH), (WIDE, 2 * RIM + 8, DEPTH), (rim, 2 * RIM, DEPTH),
@@ -409,7 +388,7 @@
         bend_kernel, (level_set, *x_halos, y_odd, *corners, matrices, gain), 2, gradient_scratch
     )
     phi, speed = call_kernel(
-        speed_kernel, (sensitivity, *x_halos, y_odd, *corners_s, matrices, base, push), 2,
+        speed_kernel, (sensitivity, *x_halos_s, y_odd, *corners_s, matrices, base, push), 2,
         speed_scratch,
     )
     for _ in range(1, UPDATES):

time: 53.5 us -> 52.7 us (0.985)
  waiting for transfers between devices: 14.7 us -> 9.45 us
  starting transfers between devices: 26.6 us -> 31.4 us
    ppermute x13 -> x15, waiting for transfers between devices: 14.7 us -> 9.45 us  [swap(): return lax.ppermute(block, axis, pairs)]
    ppermute x13 -> x15, starting transfers between devices: 26.6 us -> 31.4 us  [swap(): return lax.ppermute(block, axis, pairs)]
    dynamic_slice x3 -> x4, local copies, waits for them, and re-layouts: 1.39 us -> 1.22 us  [both_sides(): lax.dynamic_slice_in_dim(block, length - width - high, width, dim)]
  transfers between devices with their start and end apart: 13 -> 15, of which waited for: 5 -> 3; matrix products, arithmetic and copies ran while one was open for 0% -> 0% of each run, Pallas kernels for 8% -> 8%
where the time goes in v6:
time: 52.7 us; the launch traced here: 52.3 us
  starting transfers between devices  31.4 us (60%)
  waiting for transfers between devices  9.45 us (18%)
  Pallas kernels  9.25 us (18%)
  local copies, waits for them, and re-layouts  1.3 us (2%)
  between operations  0.95 us (2%)
    ppermute x15, starting transfers between devices, swap(): return lax.ppermute(block, axis, pairs)  31.4 us
    ppermute x15, waiting for transfers between devices, swap(): return lax.ppermute(block, axis, pairs)  9.45 us
    pallas_call x3, Pallas kernels, call_kernel(): pl.pallas_call(body, out_shape=(shape,) * outputs, in_specs=[VMEM] * len(...  7.72 us
    pallas_call x1, Pallas kernels, prepare(): pl.pallas_call(prepare_kernel, out_shape=(jax.ShapeDtypeStruct((4 * RIM +...  1.36 us
    dynamic_slice x4, local copies, waits for them, and re-layouts, both_sides(): lax.dynamic_slice_in_dim(block, length - width - high, width, dim)  1.22 us
  transfers between devices with their start and end apart: 15, of which 3 were waited for; matrix products, arithmetic and copies ran while one was open for 0% of the time, Pallas kernels for 8%

profile of v6, /device:TPU:41, one launch (start us, length us, event | category | flops | bytes accessed | tf_op | source)
XLA Modules:
  0.0 52.3 jit_solution(5247651138861530541)
XLA Ops:
  0.0 1.1 %constant_dynamic-slice_fusion.4 = (f32[13,32,128]{2,1,0:T(8,128)S(1)}, f32[13,32,128]{2,1,0:T(8,128)S(1)}) fusion(f32[32,32,128]{2,1,0:T(8,128)} %own.6, s32[]{:T(128)S(6)} %select_n.26, s32[]{:T(128)S(6)} %select_n.25), kind=kLoop, calls=%fused_computation.7 | loop fusion | bytes 851976 | tf_op jit(solution)/shard_map/dynamic_slice | solution.py:355
  1.1 4.1 %collective-permute-start.6 = (f32[13,32,128]{2,1,0:T(8,128)S(1)}, f32[13,32,128]{2,1,0:T(8,128)S(1)}, u32[]{:S(2)}, u32[]{:S(2)}) collective-permute-start(f32[13,32,128]{2,1,0:T(8,128)S(1)} %get-tuple-element.39), channel_id=1, source_target_pairs={{8,16},{16,8},{24,32},{32,24},{40,48},{48,40},{56,64},{64,56},{72,... | collective-permute-start | bytes 638984 | tf_op jit(solution)/shard_map/ppermute | solution.py:347
  5.2 0.5 collective-permute-start.5
  5.7 3.1 %collective-permute-start.1 = (f32[13,32,128]{2,1,0:T(8,128)S(1)}, f32[13,32,128]{2,1,0:T(8,128)S(1)}, u32[]{:S(2)}, u32[]{:S(2)}) collective-permute-start(f32[13,32,128]{2,1,0:T(8,128)S(1)} %get-tuple-element.41), channel_id=1, source_target_pairs={{8,16},{16,8},{24,32},{32,24},{40,48},{48,40},{56,64},{64,56},{72,... | collective-permute-start | bytes 638984 | tf_op jit(solution)/shard_map/ppermute | solution.py:347
  8.8 1.4 %collective-permute-start = (f32[13,32,128]{2,1,0:T(8,128)S(1)}, f32[13,32,128]{2,1,0:T(8,128)S(1)}, u32[]{:S(2)}, u32[]{:S(2)}) collective-permute-start(f32[13,32,128]{2,1,0:T(8,128)S(1)} %get-tuple-element.42), channel_id=1, source_target_pairs={{0,8},{8,0},{16,24},{24,16},{32,40},{40,32},{48,56},{56,48},{64,72... | collective-permute-start | bytes 638984 | tf_op jit(solution)/shard_map/ppermute | solution.py:347
  10.3 4.9 %collective-permute-start.2 = (f32[2,32,16,128]{3,2,1,0:T(8,128)S(1)}, f32[2,32,16,128]{3,2,1,0:T(8,128)S(1)}, u32[]{:S(2)}, u32[]{:S(2)}) collective-permute-start(f32[2,32,16,128]{3,2,1,0:T(8,128)S(1)} %pad_maximum_fusion), channel_id=1, source_target_pairs={{1,2},{2,1},{3,4},{4,3},{5,6},{6,5},{9,10},{10,9},{11,12},{12,11},... | collective-permute-start | bytes 1572872 | tf_op jit(solution)/shard_map/ppermute | solution.py:347
  15.9 1.4 %shard_map.64 = (bf16[544,256]{1,0:T(8,128)(2,1)S(1)}, f32[2,32,128]{2,1,0:T(8,128)S(1)}) custom-call(f32[25]{0:T(128)S(1)} %copy-done.3, f32[25]{0:T(128)S(1)} %copy-done.4, s32[2,2,4]{2,1,0:T(2,128)S(1)} %copy-done.2, f32[1]{0:T(128)S(6)} %copy.7.step), custom_call_target="tpu_custom_call" | custom-call | flops 1000000 | bytes 1000000 | tf_op jit(solution)/shard_map/pallas_call | solution.py:99
  17.3 0.1 shard_map.68
  17.4 0.1 collective-permute-start.7
  17.6 0.6 %collective-permute-start.3 = (f32[58,16,128]{2,1,0:T(8,128)S(1)}, f32[58,16,128]{2,1,0:T(8,128)S(1)}, u32[]{:S(2)}, u32[]{:S(2)}) collective-permute-start(f32[58,16,128]{2,1,0:T(8,128)S(1)} %get-tuple-element.23), channel_id=1, source_target_pairs={{0,1},{1,0},{2,3},{3,2},{4,5},{5,4},{6,7},{7,6},{8,9},{9,8},{10,11... | collective-permute-start | bytes 1425416 | tf_op jit(solution)/shard_map/ppermute | solution.py:347
  18.1 2.8 %collective-permute-start.8 = (f32[26,16,128]{2,1,0:T(8,128)S(1)}, f32[26,16,128]{2,1,0:T(8,128)S(1)}, u32[]{:S(2)}, u32[]{:S(2)}) collective-permute-start(f32[26,16,128]{2,1,0:T(8,128)S(1)} %get-tuple-element.27), channel_id=1, source_target_pairs={{1,2},{2,1},{3,4},{4,3},{5,6},{6,5},{9,10},{10,9},{11,12},{12,11},... | collective-permute-start | bytes 638984 | tf_op jit(solution)/shard_map/ppermute | solution.py:347
  21.0 2.7 %collective-permute-start.4 = (f32[26,16,128]{2,1,0:T(8,128)S(1)}, f32[26,16,128]{2,1,0:T(8,128)S(1)}, u32[]{:S(2)}, u32[]{:S(2)}) collective-permute-start(f32[26,16,128]{2,1,0:T(8,128)S(1)} %get-tuple-element.24), channel_id=1, source_target_pairs={{1,2},{2,1},{3,4},{4,3},{5,6},{6,5},{9,10},{10,9},{11,12},{12,11},... | collective-permute-start | bytes 638984 | tf_op jit(solution)/shard_map/ppermute | solution.py:347
  23.7 1.9 %collective-permute-done.8.refs_4_ = f32[26,16,128]{2,1,0:T(8,128)S(1)} collective-permute-done((f32[26,16,128]{2,1,0:T(8,128)S(1)}, f32[26,16,128]{2,1,0:T(8,128)S(1)}, u32[]{:S(2)}, u32[]{:S(2)}) %collective-permute-start.8) | collective-permute-done | bytes 213024 | tf_op jit(solution)/shard_map/ppermute | solution.py:347
  25.6 2.7 %shard_map.69 = (f32[32,32,128]{2,1,0:T(8,128)S(1)}, f32[32,32,128]{2,1,0:T(8,128)S(1)}) custom-call(f32[32,32,128]{2,1,0:T(8,128)S(1)} %copy-done, f32[13,32,128]{2,1,0:T(8,128)S(1)} %collective-permute-done.5.x_even.refs_0_, f32[13,32,128]{2,1,0:T(8,128)S(1)} %shard_map.67.x_odd.refs_1_, f32[2,32,16,128]{3,2,1,0:T(8,128)S(1)} %collective-permute-done.2.refs_2_, ...), custom_call_target="tpu_custom_call" | custom-call | tf_op jit(solution)/shard_map/pallas_call | solution.py:292
  28.3 1.6 %shard_map.70 = (f32[32,32,128]{2,1,0:T(8,128)S(1)}, f32[32,32,128]{2,1,0:T(8,128)S(1)}) custom-call(f32[32,32,128]{2,1,0:T(8,128)S(1)} %copy-done.1, f32[13,32,128]{2,1,0:T(8,128)S(1)} %collective-permute-done.x_even.refs_0_, f32[13,32,128]{2,1,0:T(8,128)S(1)} %shard_map.65.x_odd.refs_1_, f32[2,32,16,128]{3,2,1,0:T(8,128)S(1)} %collective-permute-done.2.refs_2_, ...), custom_call_target="tpu_custom_call" | custom-call | tf_op jit(solution)/shard_map/pallas_call | solution.py:292
  30.0 3.6 %collective-permute-start.10 = (f32[13,32,128]{2,1,0:T(8,128)S(1)}, f32[13,32,128]{2,1,0:T(8,128)S(1)}, u32[]{:S(2)}, u32[]{:S(2)}) collective-permute-start(f32[13,32,128]{2,1,0:T(8,128)S(1)} %get-tuple-element.37), channel_id=1, source_target_pairs={{8,16},{16,8},{24,32},{32,24},{40,48},{48,40},{56,64},{64,56},{72,... | collective-permute-start | bytes 638984 | tf_op jit(solution)/shard_map/ppermute | solution.py:347
  33.6 0.8 %collective-permute-start.9 = (f32[13,32,128]{2,1,0:T(8,128)S(1)}, f32[13,32,128]{2,1,0:T(8,128)S(1)}, u32[]{:S(2)}, u32[]{:S(2)}) collective-permute-start(f32[13,32,128]{2,1,0:T(8,128)S(1)} %get-tuple-element.38), channel_id=1, source_target_pairs={{0,8},{8,0},{16,24},{24,16},{32,40},{40,32},{48,56},{56,48},{64,72... | collective-permute-start | bytes 638984 | tf_op jit(solution)/shard_map/ppermute | solution.py:347
  34.4 0.4 collective-permute-start.11
  34.8 3.0 %collective-permute-start.12 = (f32[32,16,128]{2,1,0:T(8,128)S(1)}, f32[32,16,128]{2,1,0:T(8,128)S(1)}, u32[]{:S(2)}, u32[]{:S(2)}) collective-permute-start(f32[32,16,128]{2,1,0:T(8,128)S(1)} %get-tuple-element.35), channel_id=1, source_target_pairs={{1,2},{2,1},{3,4},{4,3},{5,6},{6,5},{9,10},{10,9},{11,12},{12,11},... | collective-permute-start | bytes 786440 | tf_op jit(solution)/shard_map/ppermute | solution.py:347
  37.8 3.2 %collective-permute-done.10.x_odd.refs_1_ = f32[13,32,128]{2,1,0:T(8,128)S(1)} collective-permute-done((f32[13,32,128]{2,1,0:T(8,128)S(1)}, f32[13,32,128]{2,1,0:T(8,128)S(1)}, u32[]{:S(2)}, u32[]{:S(2)}) %collective-permute-start.10) | collective-permute-done | bytes 213024 | tf_op jit(solution)/shard_map/ppermute | solution.py:347
  41.1 0.7 %collective-permute-start.13 = (f32[26,16,128]{2,1,0:T(8,128)S(1)}, f32[26,16,128]{2,1,0:T(8,128)S(1)}, u32[]{:S(2)}, u32[]{:S(2)}) collective-permute-start(f32[26,16,128]{2,1,0:T(8,128)S(1)} %get-tuple-element.32), channel_id=1, source_target_pairs={{0,1},{1,0},{2,3},{3,2},{4,5},{5,4},{6,7},{7,6},{8,9},{9,8},{10,11... | collective-permute-start | bytes 638984 | tf_op jit(solution)/shard_map/ppermute | solution.py:347
  41.7 2.8 %collective-permute-start.14 = (f32[26,16,128]{2,1,0:T(8,128)S(1)}, f32[26,16,128]{2,1,0:T(8,128)S(1)}, u32[]{:S(2)}, u32[]{:S(2)}) collective-permute-start(f32[26,16,128]{2,1,0:T(8,128)S(1)} %get-tuple-element.33), channel_id=1, source_target_pairs={{1,2},{2,1},{3,4},{4,3},{5,6},{6,5},{9,10},{10,9},{11,12},{12,11},... | collective-permute-start | bytes 638984 | tf_op jit(solution)/shard_map/ppermute | solution.py:347
  44.6 4.3 %collective-permute-done.14.refs_5_ = f32[26,16,128]{2,1,0:T(8,128)S(1)} collective-permute-done((f32[26,16,128]{2,1,0:T(8,128)S(1)}, f32[26,16,128]{2,1,0:T(8,128)S(1)}, u32[]{:S(2)}, u32[]{:S(2)}) %collective-permute-start.14) | collective-permute-done | bytes 213024 | tf_op jit(solution)/shard_map/ppermute | solution.py:347
  48.9 3.4 %shard_map.72 = f32[32,32,128]{2,1,0:T(8,128)} custom-call(f32[32,32,128]{2,1,0:T(8,128)S(1)} %get-tuple-element.31.own, f32[13,32,128]{2,1,0:T(8,128)S(1)} %collective-permute-done.9.x_even.refs_0_, f32[13,32,128]{2,1,0:T(8,128)S(1)} %collective-permute-done.10.x_odd.refs_1_, f32[32,16,128]{2,1,0:T(8,128)S(1)} %collective-permute-done.11.refs_2_, ...), custom_call_target="tpu_custom_call" | custom-call | tf_op jit(solution)/shard_map/pallas_call | solution.py:292
  (32 shorter events, 0.4 us)
Async XLA Ops:
  0.0 5.7 %copy-start.1 = (f32[32,32,128]{2,1,0:T(8,128)S(1)}, f32[32,32,128]{2,1,0:T(8,128)}, u32[]{:S(2)}) copy-start(f32[32,32,128]{2,1,0:T(8,128)} %own.7) | copy-start | bytes 1572868
  1.1 9.1 %copy-start = (f32[32,32,128]{2,1,0:T(8,128)S(1)}, f32[32,32,128]{2,1,0:T(8,128)}, u32[]{:S(2)}) copy-start(f32[32,32,128]{2,1,0:T(8,128)} %own.6) | copy-start | bytes 1572868
  1.1 16.1 %collective-permute-start.6 = (f32[13,32,128]{2,1,0:T(8,128)S(1)}, f32[13,32,128]{2,1,0:T(8,128)S(1)}, u32[]{:S(2)}, u32[]{:S(2)}) collective-permute-start(f32[13,32,128]{2,1,0:T(8,128)S(1)} %get-tuple-element.39), channel_id=1, source_target_pairs={{8,16},{16,8},{24,32},{32,24},{40,48},{48,40},{56,64},{64,56},{72,... | collective-permute-start | bytes 638984 | tf_op jit(solution)/shard_map/ppermute | solution.py:347
  5.2 12.1 %collective-permute-start.5 = (f32[13,32,128]{2,1,0:T(8,128)S(1)}, f32[13,32,128]{2,1,0:T(8,128)S(1)}, u32[]{:S(2)}, u32[]{:S(2)}) collective-permute-start(f32[13,32,128]{2,1,0:T(8,128)S(1)} %get-tuple-element.40), channel_id=1, source_target_pairs={{0,8},{8,0},{16,24},{24,16},{32,40},{40,32},{48,56},{56,48},{64,72... | collective-permute-start | bytes 638984 | tf_op jit(solution)/shard_map/ppermute | solution.py:347
  5.7 11.8 %collective-permute-start.1 = (f32[13,32,128]{2,1,0:T(8,128)S(1)}, f32[13,32,128]{2,1,0:T(8,128)S(1)}, u32[]{:S(2)}, u32[]{:S(2)}) collective-permute-start(f32[13,32,128]{2,1,0:T(8,128)S(1)} %get-tuple-element.41), channel_id=1, source_target_pairs={{8,16},{16,8},{24,32},{32,24},{40,48},{48,40},{56,64},{64,56},{72,... | collective-permute-start | bytes 638984 | tf_op jit(solution)/shard_map/ppermute | solution.py:347
  8.8 8.7 %collective-permute-start = (f32[13,32,128]{2,1,0:T(8,128)S(1)}, f32[13,32,128]{2,1,0:T(8,128)S(1)}, u32[]{:S(2)}, u32[]{:S(2)}) collective-permute-start(f32[13,32,128]{2,1,0:T(8,128)S(1)} %get-tuple-element.42), channel_id=1, source_target_pairs={{0,8},{8,0},{16,24},{24,16},{32,40},{40,32},{48,56},{56,48},{64,72... | collective-permute-start | bytes 638984 | tf_op jit(solution)/shard_map/ppermute | solution.py:347
  10.3 5.6 %copy-start.2 = (s32[2,2,4]{2,1,0:T(2,128)S(1)}, s32[2,2,4]{2,1,0:T(2,128)}, u32[]{:S(2)}) copy-start(s32[2,2,4]{2,1,0:T(2,128)} %band.1) | copy-start | bytes 196
  10.3 5.6 %copy-start.3 = (f32[25]{0:T(128)S(1)}, f32[25]{0:T(128)}, u32[]{:S(2)}) copy-start(f32[25]{0:T(128)} %smooth.1) | copy-start | bytes 304
  10.3 5.6 %copy-start.4 = (f32[25]{0:T(128)S(1)}, f32[25]{0:T(128)}, u32[]{:S(2)}) copy-start(f32[25]{0:T(128)} %slope.1) | copy-start | bytes 304
  10.3 15.3 %collective-permute-start.2 = (f32[2,32,16,128]{3,2,1,0:T(8,128)S(1)}, f32[2,32,16,128]{3,2,1,0:T(8,128)S(1)}, u32[]{:S(2)}, u32[]{:S(2)}) collective-permute-start(f32[2,32,16,128]{3,2,1,0:T(8,128)S(1)} %pad_maximum_fusion), channel_id=1, source_target_pairs={{1,2},{2,1},{3,4},{4,3},{5,6},{6,5},{9,10},{10,9},{11,12},{12,11},... | collective-permute-start | bytes 1572872 | tf_op jit(solution)/shard_map/ppermute | solution.py:347
  17.4 8.2 %collective-permute-start.7 = (f32[58,16,128]{2,1,0:T(8,128)S(1)}, f32[58,16,128]{2,1,0:T(8,128)S(1)}, u32[]{:S(2)}, u32[]{:S(2)}) collective-permute-start(f32[58,16,128]{2,1,0:T(8,128)S(1)} %get-tuple-element.26), channel_id=1, source_target_pairs={{0,1},{1,0},{2,3},{3,2},{4,5},{5,4},{6,7},{7,6},{8,9},{9,8},{10,11... | collective-permute-start | bytes 1425416 | tf_op jit(solution)/shard_map/ppermute | solution.py:347
  17.6 10.7 %collective-permute-start.3 = (f32[58,16,128]{2,1,0:T(8,128)S(1)}, f32[58,16,128]{2,1,0:T(8,128)S(1)}, u32[]{:S(2)}, u32[]{:S(2)}) collective-permute-start(f32[58,16,128]{2,1,0:T(8,128)S(1)} %get-tuple-element.23), channel_id=1, source_target_pairs={{0,1},{1,0},{2,3},{3,2},{4,5},{5,4},{6,7},{7,6},{8,9},{9,8},{10,11... | collective-permute-start | bytes 1425416 | tf_op jit(solution)/shard_map/ppermute | solution.py:347
  18.1 7.4 %collective-permute-start.8 = (f32[26,16,128]{2,1,0:T(8,128)S(1)}, f32[26,16,128]{2,1,0:T(8,128)S(1)}, u32[]{:S(2)}, u32[]{:S(2)}) collective-permute-start(f32[26,16,128]{2,1,0:T(8,128)S(1)} %get-tuple-element.27), channel_id=1, source_target_pairs={{1,2},{2,1},{3,4},{4,3},{5,6},{6,5},{9,10},{10,9},{11,12},{12,11},... | collective-permute-start | bytes 638984 | tf_op jit(solution)/shard_map/ppermute | solution.py:347
  21.0 7.3 %collective-permute-start.4 = (f32[26,16,128]{2,1,0:T(8,128)S(1)}, f32[26,16,128]{2,1,0:T(8,128)S(1)}, u32[]{:S(2)}, u32[]{:S(2)}) collective-permute-start(f32[26,16,128]{2,1,0:T(8,128)S(1)} %get-tuple-element.24), channel_id=1, source_target_pairs={{1,2},{2,1},{3,4},{4,3},{5,6},{6,5},{9,10},{10,9},{11,12},{12,11},... | collective-permute-start | bytes 638984 | tf_op jit(solution)/shard_map/ppermute | solution.py:347
  30.0 11.1 %collective-permute-start.10 = (f32[13,32,128]{2,1,0:T(8,128)S(1)}, f32[13,32,128]{2,1,0:T(8,128)S(1)}, u32[]{:S(2)}, u32[]{:S(2)}) collective-permute-start(f32[13,32,128]{2,1,0:T(8,128)S(1)} %get-tuple-element.37), channel_id=1, source_target_pairs={{8,16},{16,8},{24,32},{32,24},{40,48},{48,40},{56,64},{64,56},{72,... | collective-permute-start | bytes 638984 | tf_op jit(solution)/shard_map/ppermute | solution.py:347
  33.6 7.5 %collective-permute-start.9 = (f32[13,32,128]{2,1,0:T(8,128)S(1)}, f32[13,32,128]{2,1,0:T(8,128)S(1)}, u32[]{:S(2)}, u32[]{:S(2)}) collective-permute-start(f32[13,32,128]{2,1,0:T(8,128)S(1)} %get-tuple-element.38), channel_id=1, source_target_pairs={{0,8},{8,0},{16,24},{24,16},{32,40},{40,32},{48,56},{56,48},{64,72... | collective-permute-start | bytes 638984 | tf_op jit(solution)/shard_map/ppermute | solution.py:347
  34.4 10.2 %collective-permute-start.11 = (f32[32,16,128]{2,1,0:T(8,128)S(1)}, f32[32,16,128]{2,1,0:T(8,128)S(1)}, u32[]{:S(2)}, u32[]{:S(2)}) collective-permute-start(f32[32,16,128]{2,1,0:T(8,128)S(1)} %get-tuple-element.36), channel_id=1, source_target_pairs={{0,1},{1,0},{2,3},{3,2},{4,5},{5,4},{6,7},{7,6},{8,9},{9,8},{10,11... | collective-permute-start | bytes 786440 | tf_op jit(solution)/shard_map/ppermute | solution.py:347
  34.8 9.8 %collective-permute-start.12 = (f32[32,16,128]{2,1,0:T(8,128)S(1)}, f32[32,16,128]{2,1,0:T(8,128)S(1)}, u32[]{:S(2)}, u32[]{:S(2)}) collective-permute-start(f32[32,16,128]{2,1,0:T(8,128)S(1)} %get-tuple-element.35), channel_id=1, source_target_pairs={{1,2},{2,1},{3,4},{4,3},{5,6},{6,5},{9,10},{10,9},{11,12},{12,11},... | collective-permute-start | bytes 786440 | tf_op jit(solution)/shard_map/ppermute | solution.py:347
  41.1 3.5 %collective-permute-start.13 = (f32[26,16,128]{2,1,0:T(8,128)S(1)}, f32[26,16,128]{2,1,0:T(8,128)S(1)}, u32[]{:S(2)}, u32[]{:S(2)}) collective-permute-start(f32[26,16,128]{2,1,0:T(8,128)S(1)} %get-tuple-element.32), channel_id=1, source_target_pairs={{0,1},{1,0},{2,3},{3,2},{4,5},{5,4},{6,7},{7,6},{8,9},{9,8},{10,11... | collective-permute-start | bytes 638984 | tf_op jit(solution)/shard_map/ppermute | solution.py:347
  41.7 7.2 %collective-permute-start.14 = (f32[26,16,128]{2,1,0:T(8,128)S(1)}, f32[26,16,128]{2,1,0:T(8,128)S(1)}, u32[]{:S(2)}, u32[]{:S(2)}) collective-permute-start(f32[26,16,128]{2,1,0:T(8,128)S(1)} %get-tuple-element.33), channel_id=1, source_target_pairs={{1,2},{2,1},{3,4},{4,3},{5,6},{6,5},{9,10},{10,9},{11,12},{12,11},... | collective-permute-start | bytes 638984 | tf_op jit(solution)/shard_map/ppermute | solution.py:347

commit v7 on v6

--- a/solution.py
+++ b/solution.py
@@ -235,7 +235,7 @@
     total += (pltpu.roll(rim, RIM - 1, 0) + pltpu.roll(rim, 1, 0))[0:SIDE]
     total += jnp.where(lane < DEPTH - 1, pltpu.roll(centre, DEPTH - 1, 1), 0.0)
     total += jnp.where(lane > 0, pltpu.roll(centre, 1, 1), 0.0)
-    return total / 7.0
+    return total * (1.0 / 7.0)
 
 
 HALOS = 5
@@ -394,7 +394,9 @@
     for _ in range(1, UPDATES):
         x_halos = swap_sides(both_sides(phi, 0, REACH, parity[0]), "gx")
         y_halos = swap_sides(both_sides(phi, 1, SLAB, parity[1]), "gy")
+        x_halos = (x_halos[0], settle(x_halos[1]))
         corners = swap_sides(corner_sides(phi, x_halos), "gy")
+        y_halos = (y_halos[0], settle(y_halos[1]))
         (phi,) = call_kernel(
             later_kernel, (phi, *x_halos, *y_halos, *corners, matrices, gain, speed), 1, gradient_scratch,
         )

time: 52.7 us -> 52.7 us (level)
  no operation moved by 1% of the time
where the time goes in v7:
time: 52.7 us; the launch traced here: 52.4 us
  starting transfers between devices  31.2 us (59%)
  waiting for transfers between devices  9.56 us (18%)
  Pallas kernels  9.3 us (18%)
  local copies, waits for them, and re-layouts  1.3 us (2%)
  between operations  0.98 us (2%)
    ppermute x15, starting transfers between devices, swap(): return lax.ppermute(block, axis, pairs)  31.2 us
    ppermute x15, waiting for transfers between devices, swap(): return lax.ppermute(block, axis, pairs)  9.56 us
    pallas_call x3, Pallas kernels, call_kernel(): pl.pallas_call(body, out_shape=(shape,) * outputs, in_specs=[VMEM] * len(...  7.72 us
    pallas_call x1, Pallas kernels, prepare(): pl.pallas_call(prepare_kernel, out_shape=(jax.ShapeDtypeStruct((4 * RIM +...  1.36 us
    dynamic_slice x4, local copies, waits for them, and re-layouts, both_sides(): lax.dynamic_slice_in_dim(block, length - width - high, width, dim)  1.22 us
  transfers between devices with their start and end apart: 15, of which 3 were waited for; matrix products, arithmetic and copies ran while one was open for 0% of the time, Pallas kernels for 8%

profile of v7, /device:TPU:41, one launch (start us, length us, event | category | flops | bytes accessed | tf_op | source)
XLA Modules:
  0.0 52.4 jit_solution(7901290508883969792)
XLA Ops:
  0.0 1.1 %constant_dynamic-slice_fusion.4 = (f32[13,32,128]{2,1,0:T(8,128)S(1)}, f32[13,32,128]{2,1,0:T(8,128)S(1)}) fusion(f32[32,32,128]{2,1,0:T(8,128)} %own.6, s32[]{:T(128)S(6)} %select_n.26, s32[]{:T(128)S(6)} %select_n.25), kind=kLoop, calls=%fused_computation.7 | loop fusion | bytes 851976 | tf_op jit(solution)/shard_map/dynamic_slice | solution.py:355
  1.1 4.1 %collective-permute-start.6 = (f32[13,32,128]{2,1,0:T(8,128)S(1)}, f32[13,32,128]{2,1,0:T(8,128)S(1)}, u32[]{:S(2)}, u32[]{:S(2)}) collective-permute-start(f32[13,32,128]{2,1,0:T(8,128)S(1)} %get-tuple-element.39), channel_id=1, source_target_pairs={{8,16},{16,8},{24,32},{32,24},{40,48},{48,40},{56,64},{64,56},{72,... | collective-permute-start | bytes 638984 | tf_op jit(solution)/shard_map/ppermute | solution.py:347
  5.2 0.5 collective-permute-start.5
  5.7 3.1 %collective-permute-start.1 = (f32[13,32,128]{2,1,0:T(8,128)S(1)}, f32[13,32,128]{2,1,0:T(8,128)S(1)}, u32[]{:S(2)}, u32[]{:S(2)}) collective-permute-start(f32[13,32,128]{2,1,0:T(8,128)S(1)} %get-tuple-element.41), channel_id=1, source_target_pairs={{8,16},{16,8},{24,32},{32,24},{40,48},{48,40},{56,64},{64,56},{72,... | collective-permute-start | bytes 638984 | tf_op jit(solution)/shard_map/ppermute | solution.py:347
  8.8 1.4 %collective-permute-start = (f32[13,32,128]{2,1,0:T(8,128)S(1)}, f32[13,32,128]{2,1,0:T(8,128)S(1)}, u32[]{:S(2)}, u32[]{:S(2)}) collective-permute-start(f32[13,32,128]{2,1,0:T(8,128)S(1)} %get-tuple-element.42), channel_id=1, source_target_pairs={{0,8},{8,0},{16,24},{24,16},{32,40},{40,32},{48,56},{56,48},{64,72... | collective-permute-start | bytes 638984 | tf_op jit(solution)/shard_map/ppermute | solution.py:347
  10.3 4.9 %collective-permute-start.2 = (f32[2,32,16,128]{3,2,1,0:T(8,128)S(1)}, f32[2,32,16,128]{3,2,1,0:T(8,128)S(1)}, u32[]{:S(2)}, u32[]{:S(2)}) collective-permute-start(f32[2,32,16,128]{3,2,1,0:T(8,128)S(1)} %pad_maximum_fusion), channel_id=1, source_target_pairs={{1,2},{2,1},{3,4},{4,3},{5,6},{6,5},{9,10},{10,9},{11,12},{12,11},... | collective-permute-start | bytes 1572872 | tf_op jit(solution)/shard_map/ppermute | solution.py:347
  15.9 1.4 %shard_map.64 = (bf16[544,256]{1,0:T(8,128)(2,1)S(1)}, f32[2,32,128]{2,1,0:T(8,128)S(1)}) custom-call(f32[25]{0:T(128)S(1)} %copy-done.3, f32[25]{0:T(128)S(1)} %copy-done.4, s32[2,2,4]{2,1,0:T(2,128)S(1)} %copy-done.2, f32[1]{0:T(128)S(6)} %copy.7.step), custom_call_target="tpu_custom_call" | custom-call | flops 1000000 | bytes 1000000 | tf_op jit(solution)/shard_map/pallas_call | solution.py:99
  17.3 0.1 shard_map.68
  17.4 0.1 collective-permute-start.7
  17.6 0.6 %collective-permute-start.3 = (f32[58,16,128]{2,1,0:T(8,128)S(1)}, f32[58,16,128]{2,1,0:T(8,128)S(1)}, u32[]{:S(2)}, u32[]{:S(2)}) collective-permute-start(f32[58,16,128]{2,1,0:T(8,128)S(1)} %get-tuple-element.23), channel_id=1, source_target_pairs={{0,1},{1,0},{2,3},{3,2},{4,5},{5,4},{6,7},{7,6},{8,9},{9,8},{10,11... | collective-permute-start | bytes 1425416 | tf_op jit(solution)/shard_map/ppermute | solution.py:347
  18.1 2.8 %collective-permute-start.8 = (f32[26,16,128]{2,1,0:T(8,128)S(1)}, f32[26,16,128]{2,1,0:T(8,128)S(1)}, u32[]{:S(2)}, u32[]{:S(2)}) collective-permute-start(f32[26,16,128]{2,1,0:T(8,128)S(1)} %get-tuple-element.27), channel_id=1, source_target_pairs={{1,2},{2,1},{3,4},{4,3},{5,6},{6,5},{9,10},{10,9},{11,12},{12,11},... | collective-permute-start | bytes 638984 | tf_op jit(solution)/shard_map/ppermute | solution.py:347
  21.0 2.7 %collective-permute-start.4 = (f32[26,16,128]{2,1,0:T(8,128)S(1)}, f32[26,16,128]{2,1,0:T(8,128)S(1)}, u32[]{:S(2)}, u32[]{:S(2)}) collective-permute-start(f32[26,16,128]{2,1,0:T(8,128)S(1)} %get-tuple-element.24), channel_id=1, source_target_pairs={{1,2},{2,1},{3,4},{4,3},{5,6},{6,5},{9,10},{10,9},{11,12},{12,11},... | collective-permute-start | bytes 638984 | tf_op jit(solution)/shard_map/ppermute | solution.py:347
  23.7 1.9 %collective-permute-done.8.refs_4_ = f32[26,16,128]{2,1,0:T(8,128)S(1)} collective-permute-done((f32[26,16,128]{2,1,0:T(8,128)S(1)}, f32[26,16,128]{2,1,0:T(8,128)S(1)}, u32[]{:S(2)}, u32[]{:S(2)}) %collective-permute-start.8) | collective-permute-done | bytes 213024 | tf_op jit(solution)/shard_map/ppermute | solution.py:347
  25.6 2.7 %shard_map.69 = (f32[32,32,128]{2,1,0:T(8,128)S(1)}, f32[32,32,128]{2,1,0:T(8,128)S(1)}) custom-call(f32[32,32,128]{2,1,0:T(8,128)S(1)} %copy-done, f32[13,32,128]{2,1,0:T(8,128)S(1)} %collective-permute-done.5.x_even.refs_0_, f32[13,32,128]{2,1,0:T(8,128)S(1)} %shard_map.67.x_odd.refs_1_, f32[2,32,16,128]{3,2,1,0:T(8,128)S(1)} %collective-permute-done.2.refs_2_, ...), custom_call_target="tpu_custom_call" | custom-call | tf_op jit(solution)/shard_map/pallas_call | solution.py:292
  28.3 1.6 %shard_map.70 = (f32[32,32,128]{2,1,0:T(8,128)S(1)}, f32[32,32,128]{2,1,0:T(8,128)S(1)}) custom-call(f32[32,32,128]{2,1,0:T(8,128)S(1)} %copy-done.1, f32[13,32,128]{2,1,0:T(8,128)S(1)} %collective-permute-done.x_even.refs_0_, f32[13,32,128]{2,1,0:T(8,128)S(1)} %shard_map.65.x_odd.refs_1_, f32[2,32,16,128]{3,2,1,0:T(8,128)S(1)} %collective-permute-done.2.refs_2_, ...), custom_call_target="tpu_custom_call" | custom-call | tf_op jit(solution)/shard_map/pallas_call | solution.py:292
  30.0 3.6 %collective-permute-start.10 = (f32[13,32,128]{2,1,0:T(8,128)S(1)}, f32[13,32,128]{2,1,0:T(8,128)S(1)}, u32[]{:S(2)}, u32[]{:S(2)}) collective-permute-start(f32[13,32,128]{2,1,0:T(8,128)S(1)} %get-tuple-element.37), channel_id=1, source_target_pairs={{8,16},{16,8},{24,32},{32,24},{40,48},{48,40},{56,64},{64,56},{72,... | collective-permute-start | bytes 638984 | tf_op jit(solution)/shard_map/ppermute | solution.py:347
  33.6 0.8 %collective-permute-start.9 = (f32[13,32,128]{2,1,0:T(8,128)S(1)}, f32[13,32,128]{2,1,0:T(8,128)S(1)}, u32[]{:S(2)}, u32[]{:S(2)}) collective-permute-start(f32[13,32,128]{2,1,0:T(8,128)S(1)} %get-tuple-element.38), channel_id=1, source_target_pairs={{0,8},{8,0},{16,24},{24,16},{32,40},{40,32},{48,56},{56,48},{64,72... | collective-permute-start | bytes 638984 | tf_op jit(solution)/shard_map/ppermute | solution.py:347
  34.4 3.2 %collective-permute-start.12 = (f32[32,16,128]{2,1,0:T(8,128)S(1)}, f32[32,16,128]{2,1,0:T(8,128)S(1)}, u32[]{:S(2)}, u32[]{:S(2)}) collective-permute-start(f32[32,16,128]{2,1,0:T(8,128)S(1)} %get-tuple-element.35), channel_id=1, source_target_pairs={{1,2},{2,1},{3,4},{4,3},{5,6},{6,5},{9,10},{10,9},{11,12},{12,11},... | collective-permute-start | bytes 786440 | tf_op jit(solution)/shard_map/ppermute | solution.py:347
  37.6 0.1 collective-permute-start.11
  37.7 3.4 %collective-permute-done.10.source = f32[13,32,128]{2,1,0:T(8,128)S(1)} collective-permute-done((f32[13,32,128]{2,1,0:T(8,128)S(1)}, f32[13,32,128]{2,1,0:T(8,128)S(1)}, u32[]{:S(2)}, u32[]{:S(2)}) %collective-permute-start.10) | collective-permute-done | bytes 213024 | tf_op jit(solution)/shard_map/ppermute | solution.py:347
  41.1 0.7 %collective-permute-start.13 = (f32[26,16,128]{2,1,0:T(8,128)S(1)}, f32[26,16,128]{2,1,0:T(8,128)S(1)}, u32[]{:S(2)}, u32[]{:S(2)}) collective-permute-start(f32[26,16,128]{2,1,0:T(8,128)S(1)} %get-tuple-element.32), channel_id=1, source_target_pairs={{0,1},{1,0},{2,3},{3,2},{4,5},{5,4},{6,7},{7,6},{8,9},{9,8},{10,11... | collective-permute-start | bytes 638984 | tf_op jit(solution)/shard_map/ppermute | solution.py:347
  41.8 2.8 %collective-permute-start.14 = (f32[26,16,128]{2,1,0:T(8,128)S(1)}, f32[26,16,128]{2,1,0:T(8,128)S(1)}, u32[]{:S(2)}, u32[]{:S(2)}) collective-permute-start(f32[26,16,128]{2,1,0:T(8,128)S(1)} %get-tuple-element.33), channel_id=1, source_target_pairs={{1,2},{2,1},{3,4},{4,3},{5,6},{6,5},{9,10},{10,9},{11,12},{12,11},... | collective-permute-start | bytes 638984 | tf_op jit(solution)/shard_map/ppermute | solution.py:347
  44.7 4.3 %collective-permute-done.14.refs_5_ = f32[26,16,128]{2,1,0:T(8,128)S(1)} collective-permute-done((f32[26,16,128]{2,1,0:T(8,128)S(1)}, f32[26,16,128]{2,1,0:T(8,128)S(1)}, u32[]{:S(2)}, u32[]{:S(2)}) %collective-permute-start.14) | collective-permute-done | bytes 213024 | tf_op jit(solution)/shard_map/ppermute | solution.py:347
  48.9 3.4 %shard_map.74 = f32[32,32,128]{2,1,0:T(8,128)} custom-call(f32[32,32,128]{2,1,0:T(8,128)S(1)} %get-tuple-element.31.own, f32[13,32,128]{2,1,0:T(8,128)S(1)} %collective-permute-done.9.x_even.refs_0_, f32[13,32,128]{2,1,0:T(8,128)S(1)} %shard_map.71.x_odd.refs_1_, f32[32,16,128]{2,1,0:T(8,128)S(1)} %collective-permute-done.11.refs_2_, ...), custom_call_target="tpu_custom_call" | custom-call | tf_op jit(solution)/shard_map/pallas_call | solution.py:292
  (34 shorter events, 0.4 us)
Async XLA Ops:
  0.0 5.7 %copy-start.1 = (f32[32,32,128]{2,1,0:T(8,128)S(1)}, f32[32,32,128]{2,1,0:T(8,128)}, u32[]{:S(2)}) copy-start(f32[32,32,128]{2,1,0:T(8,128)} %own.7) | copy-start | bytes 1572868
  1.1 9.1 %copy-start = (f32[32,32,128]{2,1,0:T(8,128)S(1)}, f32[32,32,128]{2,1,0:T(8,128)}, u32[]{:S(2)}) copy-start(f32[32,32,128]{2,1,0:T(8,128)} %own.6) | copy-start | bytes 1572868
  1.1 16.1 %collective-permute-start.6 = (f32[13,32,128]{2,1,0:T(8,128)S(1)}, f32[13,32,128]{2,1,0:T(8,128)S(1)}, u32[]{:S(2)}, u32[]{:S(2)}) collective-permute-start(f32[13,32,128]{2,1,0:T(8,128)S(1)} %get-tuple-element.39), channel_id=1, source_target_pairs={{8,16},{16,8},{24,32},{32,24},{40,48},{48,40},{56,64},{64,56},{72,... | collective-permute-start | bytes 638984 | tf_op jit(solution)/shard_map/ppermute | solution.py:347
  5.2 12.1 %collective-permute-start.5 = (f32[13,32,128]{2,1,0:T(8,128)S(1)}, f32[13,32,128]{2,1,0:T(8,128)S(1)}, u32[]{:S(2)}, u32[]{:S(2)}) collective-permute-start(f32[13,32,128]{2,1,0:T(8,128)S(1)} %get-tuple-element.40), channel_id=1, source_target_pairs={{0,8},{8,0},{16,24},{24,16},{32,40},{40,32},{48,56},{56,48},{64,72... | collective-permute-start | bytes 638984 | tf_op jit(solution)/shard_map/ppermute | solution.py:347
  5.7 11.8 %collective-permute-start.1 = (f32[13,32,128]{2,1,0:T(8,128)S(1)}, f32[13,32,128]{2,1,0:T(8,128)S(1)}, u32[]{:S(2)}, u32[]{:S(2)}) collective-permute-start(f32[13,32,128]{2,1,0:T(8,128)S(1)} %get-tuple-element.41), channel_id=1, source_target_pairs={{8,16},{16,8},{24,32},{32,24},{40,48},{48,40},{56,64},{64,56},{72,... | collective-permute-start | bytes 638984 | tf_op jit(solution)/shard_map/ppermute | solution.py:347
  8.8 8.7 %collective-permute-start = (f32[13,32,128]{2,1,0:T(8,128)S(1)}, f32[13,32,128]{2,1,0:T(8,128)S(1)}, u32[]{:S(2)}, u32[]{:S(2)}) collective-permute-start(f32[13,32,128]{2,1,0:T(8,128)S(1)} %get-tuple-element.42), channel_id=1, source_target_pairs={{0,8},{8,0},{16,24},{24,16},{32,40},{40,32},{48,56},{56,48},{64,72... | collective-permute-start | bytes 638984 | tf_op jit(solution)/shard_map/ppermute | solution.py:347
  10.3 5.6 %copy-start.2 = (s32[2,2,4]{2,1,0:T(2,128)S(1)}, s32[2,2,4]{2,1,0:T(2,128)}, u32[]{:S(2)}) copy-start(s32[2,2,4]{2,1,0:T(2,128)} %band.1) | copy-start | bytes 196
  10.3 5.6 %copy-start.3 = (f32[25]{0:T(128)S(1)}, f32[25]{0:T(128)}, u32[]{:S(2)}) copy-start(f32[25]{0:T(128)} %smooth.1) | copy-start | bytes 304
  10.3 5.6 %copy-start.4 = (f32[25]{0:T(128)S(1)}, f32[25]{0:T(128)}, u32[]{:S(2)}) copy-start(f32[25]{0:T(128)} %slope.1) | copy-start | bytes 304
  10.3 15.3 %collective-permute-start.2 = (f32[2,32,16,128]{3,2,1,0:T(8,128)S(1)}, f32[2,32,16,128]{3,2,1,0:T(8,128)S(1)}, u32[]{:S(2)}, u32[]{:S(2)}) collective-permute-start(f32[2,32,16,128]{3,2,1,0:T(8,128)S(1)} %pad_maximum_fusion), channel_id=1, source_target_pairs={{1,2},{2,1},{3,4},{4,3},{5,6},{6,5},{9,10},{10,9},{11,12},{12,11},... | collective-permute-start | bytes 1572872 | tf_op jit(solution)/shard_map/ppermute | solution.py:347
  17.4 8.2 %collective-permute-start.7 = (f32[58,16,128]{2,1,0:T(8,128)S(1)}, f32[58,16,128]{2,1,0:T(8,128)S(1)}, u32[]{:S(2)}, u32[]{:S(2)}) collective-permute-start(f32[58,16,128]{2,1,0:T(8,128)S(1)} %get-tuple-element.26), channel_id=1, source_target_pairs={{0,1},{1,0},{2,3},{3,2},{4,5},{5,4},{6,7},{7,6},{8,9},{9,8},{10,11... | collective-permute-start | bytes 1425416 | tf_op jit(solution)/shard_map/ppermute | solution.py:347
  17.6 10.7 %collective-permute-start.3 = (f32[58,16,128]{2,1,0:T(8,128)S(1)}, f32[58,16,128]{2,1,0:T(8,128)S(1)}, u32[]{:S(2)}, u32[]{:S(2)}) collective-permute-start(f32[58,16,128]{2,1,0:T(8,128)S(1)} %get-tuple-element.23), channel_id=1, source_target_pairs={{0,1},{1,0},{2,3},{3,2},{4,5},{5,4},{6,7},{7,6},{8,9},{9,8},{10,11... | collective-permute-start | bytes 1425416 | tf_op jit(solution)/shard_map/ppermute | solution.py:347
  18.1 7.4 %collective-permute-start.8 = (f32[26,16,128]{2,1,0:T(8,128)S(1)}, f32[26,16,128]{2,1,0:T(8,128)S(1)}, u32[]{:S(2)}, u32[]{:S(2)}) collective-permute-start(f32[26,16,128]{2,1,0:T(8,128)S(1)} %get-tuple-element.27), channel_id=1, source_target_pairs={{1,2},{2,1},{3,4},{4,3},{5,6},{6,5},{9,10},{10,9},{11,12},{12,11},... | collective-permute-start | bytes 638984 | tf_op jit(solution)/shard_map/ppermute | solution.py:347
  21.0 7.3 %collective-permute-start.4 = (f32[26,16,128]{2,1,0:T(8,128)S(1)}, f32[26,16,128]{2,1,0:T(8,128)S(1)}, u32[]{:S(2)}, u32[]{:S(2)}) collective-permute-start(f32[26,16,128]{2,1,0:T(8,128)S(1)} %get-tuple-element.24), channel_id=1, source_target_pairs={{1,2},{2,1},{3,4},{4,3},{5,6},{6,5},{9,10},{10,9},{11,12},{12,11},... | collective-permute-start | bytes 638984 | tf_op jit(solution)/shard_map/ppermute | solution.py:347
  30.0 11.1 %collective-permute-start.10 = (f32[13,32,128]{2,1,0:T(8,128)S(1)}, f32[13,32,128]{2,1,0:T(8,128)S(1)}, u32[]{:S(2)}, u32[]{:S(2)}) collective-permute-start(f32[13,32,128]{2,1,0:T(8,128)S(1)} %get-tuple-element.37), channel_id=1, source_target_pairs={{8,16},{16,8},{24,32},{32,24},{40,48},{48,40},{56,64},{64,56},{72,... | collective-permute-start | bytes 638984 | tf_op jit(solution)/shard_map/ppermute | solution.py:347
  33.6 7.5 %collective-permute-start.9 = (f32[13,32,128]{2,1,0:T(8,128)S(1)}, f32[13,32,128]{2,1,0:T(8,128)S(1)}, u32[]{:S(2)}, u32[]{:S(2)}) collective-permute-start(f32[13,32,128]{2,1,0:T(8,128)S(1)} %get-tuple-element.38), channel_id=1, source_target_pairs={{0,8},{8,0},{16,24},{24,16},{32,40},{40,32},{48,56},{56,48},{64,72... | collective-permute-start | bytes 638984 | tf_op jit(solution)/shard_map/ppermute | solution.py:347
  34.4 10.2 %collective-permute-start.12 = (f32[32,16,128]{2,1,0:T(8,128)S(1)}, f32[32,16,128]{2,1,0:T(8,128)S(1)}, u32[]{:S(2)}, u32[]{:S(2)}) collective-permute-start(f32[32,16,128]{2,1,0:T(8,128)S(1)} %get-tuple-element.35), channel_id=1, source_target_pairs={{1,2},{2,1},{3,4},{4,3},{5,6},{6,5},{9,10},{10,9},{11,12},{12,11},... | collective-permute-start | bytes 786440 | tf_op jit(solution)/shard_map/ppermute | solution.py:347
  37.6 7.1 %collective-permute-start.11 = (f32[32,16,128]{2,1,0:T(8,128)S(1)}, f32[32,16,128]{2,1,0:T(8,128)S(1)}, u32[]{:S(2)}, u32[]{:S(2)}) collective-permute-start(f32[32,16,128]{2,1,0:T(8,128)S(1)} %get-tuple-element.36), channel_id=1, source_target_pairs={{0,1},{1,0},{2,3},{3,2},{4,5},{5,4},{6,7},{7,6},{8,9},{9,8},{10,11... | collective-permute-start | bytes 786440 | tf_op jit(solution)/shard_map/ppermute | solution.py:347
  41.1 3.5 %collective-permute-start.13 = (f32[26,16,128]{2,1,0:T(8,128)S(1)}, f32[26,16,128]{2,1,0:T(8,128)S(1)}, u32[]{:S(2)}, u32[]{:S(2)}) collective-permute-start(f32[26,16,128]{2,1,0:T(8,128)S(1)} %get-tuple-element.32), channel_id=1, source_target_pairs={{0,1},{1,0},{2,3},{3,2},{4,5},{5,4},{6,7},{7,6},{8,9},{9,8},{10,11... | collective-permute-start | bytes 638984 | tf_op jit(solution)/shard_map/ppermute | solution.py:347
  41.8 7.2 %collective-permute-start.14 = (f32[26,16,128]{2,1,0:T(8,128)S(1)}, f32[26,16,128]{2,1,0:T(8,128)S(1)}, u32[]{:S(2)}, u32[]{:S(2)}) collective-permute-start(f32[26,16,128]{2,1,0:T(8,128)S(1)} %get-tuple-element.33), channel_id=1, source_target_pairs={{1,2},{2,1},{3,4},{4,3},{5,6},{6,5},{9,10},{10,9},{11,12},{12,11},... | collective-permute-start | bytes 638984 | tf_op jit(solution)/shard_map/ppermute | solution.py:347

commit v8 on v7

--- a/solution.py
+++ b/solution.py
@@ -274,27 +274,41 @@
     speed_stages(extended, matrices, crossed, flat_s, velocity, finish)
 
 
+CHUNK = 8
+
+
 def later_kernel(own, *refs):
     halos = refs[: HALOS + 1]
     matrices, gain, speed, out = refs[HALOS + 1 : HALOS + 5]
-    extended, crossed, flat_s, flat_g, normals, lengths = refs[HALOS + 5 :]
+    extended, crossed, flat_s, flat_g, normals, lengths, result, sems = refs[HALOS + 5 :]
     fill_extended(extended, own[...], *[halo[...] for halo in halos])
+
+    copies = [
+        pltpu.make_async_copy(
+            result.at[pl.ds(at * CHUNK, CHUNK)], out.at[pl.ds(at * CHUNK, CHUNK)], sems.at[at]
+        )
+        for at in range(SIDE // CHUNK)
+    ]
 
     def finish(x):
         factor = gain[x // (SIDE // 2), :, :] * lengths[x + 1, 0:SIDE, :]
-        out[x, :, :] = own[x, :, :] - factor * (speed[x, :, :] - bending(normals, x))
+        result[x, :, :] = own[x, :, :] - factor * (speed[x, :, :] - bending(normals, x))
+        if x % CHUNK == CHUNK - 1:
+            copies[x // CHUNK].start()
 
     gradient_stages(extended, matrices, crossed, flat_s, flat_g, normals, lengths, finish)
-
-
-def call_kernel(body, arrays, outputs, scratch):
+    for copy in copies:
+        copy.wait()
+
+
+def call_kernel(body, arrays, outputs, scratch, out_spec=VMEM, extra=()):
     shape = jax.ShapeDtypeStruct((SIDE, SIDE, DEPTH), jnp.float32)
     return pl.pallas_call(
         body,
         out_shape=(shape,) * outputs,
         in_specs=[VMEM] * len(arrays),
-        out_specs=(VMEM,) * outputs,
-        scratch_shapes=[pltpu.VMEM(shape, jnp.float32) for shape in scratch],
+        out_specs=(out_spec,) * outputs,
+        scratch_shapes=[pltpu.VMEM(shape, jnp.float32) for shape in scratch] + list(extra),
         compiler_params=pltpu.CompilerParams(vmem_limit_bytes=20 * 1024 * 1024),
     )(*arrays)
 
@@ -398,7 +412,8 @@
         corners = swap_sides(corner_sides(phi, x_halos), "gy")
         y_halos = (y_halos[0], settle(y_halos[1]))
         (phi,) = call_kernel(
-            later_kernel, (phi, *x_halos, *y_halos, *corners, matrices, gain, speed), 1, gradient_scratch,
+            later_kernel, (phi, *x_halos, *y_halos, *corners, matrices, gain, speed), 1, gradient_scratch + [(SIDE, SIDE, DEPTH)],
+            pl.BlockSpec(memory_space=pl.ANY), (pltpu.SemaphoreType.DMA((SIDE // CHUNK,)),),
         )
     return phi
 

time: 52.7 us -> 52.6 us (level)
  no operation moved by 1% of the time
where the time goes in v8:
time: 52.6 us; the launch traced here: 52.3 us
  starting transfers between devices  31.2 us (59%)
  waiting for transfers between devices  9.56 us (18%)
  Pallas kernels  9.2 us (17%)
  local copies, waits for them, and re-layouts  1.3 us (2%)
  between operations  0.98 us (2%)
    ppermute x15, starting transfers between devices, swap(): return lax.ppermute(block, axis, pairs)  31.2 us
    ppermute x15, waiting for transfers between devices, swap(): return lax.ppermute(block, axis, pairs)  9.56 us
    pallas_call x3, Pallas kernels, call_kernel(): pl.pallas_call(body, out_shape=(shape,) * outputs, in_specs=[VMEM] * len(...  7.62 us
    pallas_call x1, Pallas kernels, prepare(): pl.pallas_call(prepare_kernel, out_shape=(jax.ShapeDtypeStruct((4 * RIM +...  1.36 us
    dynamic_slice x4, local copies, waits for them, and re-layouts, both_sides(): lax.dynamic_slice_in_dim(block, length - width - high, width, dim)  1.22 us
  transfers between devices with their start and end apart: 15, of which 3 were waited for; matrix products, arithmetic and copies ran while one was open for 0% of the time, Pallas kernels for 8%

profile of v8, /device:TPU:41, one launch (start us, length us, event | category | flops | bytes accessed | tf_op | source)
XLA Modules:
  0.0 52.3 jit_solution(11007684864242178750)
XLA Ops:
  0.0 1.1 %constant_dynamic-slice_fusion.4 = (f32[13,32,128]{2,1,0:T(8,128)S(1)}, f32[13,32,128]{2,1,0:T(8,128)S(1)}) fusion(f32[32,32,128]{2,1,0:T(8,128)} %own.6, s32[]{:T(128)S(6)} %select_n.26, s32[]{:T(128)S(6)} %select_n.25), kind=kLoop, calls=%fused_computation.7 | loop fusion | bytes 851976 | tf_op jit(solution)/shard_map/dynamic_slice | solution.py:369
  1.1 4.1 %collective-permute-start.6 = (f32[13,32,128]{2,1,0:T(8,128)S(1)}, f32[13,32,128]{2,1,0:T(8,128)S(1)}, u32[]{:S(2)}, u32[]{:S(2)}) collective-permute-start(f32[13,32,128]{2,1,0:T(8,128)S(1)} %get-tuple-element.39), channel_id=1, source_target_pairs={{8,16},{16,8},{24,32},{32,24},{40,48},{48,40},{56,64},{64,56},{72,... | collective-permute-start | bytes 638984 | tf_op jit(solution)/shard_map/ppermute | solution.py:361
  5.2 0.5 collective-permute-start.5
  5.7 3.1 %collective-permute-start.1 = (f32[13,32,128]{2,1,0:T(8,128)S(1)}, f32[13,32,128]{2,1,0:T(8,128)S(1)}, u32[]{:S(2)}, u32[]{:S(2)}) collective-permute-start(f32[13,32,128]{2,1,0:T(8,128)S(1)} %get-tuple-element.41), channel_id=1, source_target_pairs={{8,16},{16,8},{24,32},{32,24},{40,48},{48,40},{56,64},{64,56},{72,... | collective-permute-start | bytes 638984 | tf_op jit(solution)/shard_map/ppermute | solution.py:361
  8.8 1.4 %collective-permute-start = (f32[13,32,128]{2,1,0:T(8,128)S(1)}, f32[13,32,128]{2,1,0:T(8,128)S(1)}, u32[]{:S(2)}, u32[]{:S(2)}) collective-permute-start(f32[13,32,128]{2,1,0:T(8,128)S(1)} %get-tuple-element.42), channel_id=1, source_target_pairs={{0,8},{8,0},{16,24},{24,16},{32,40},{40,32},{48,56},{56,48},{64,72... | collective-permute-start | bytes 638984 | tf_op jit(solution)/shard_map/ppermute | solution.py:361
  10.3 4.9 %collective-permute-start.2 = (f32[2,32,16,128]{3,2,1,0:T(8,128)S(1)}, f32[2,32,16,128]{3,2,1,0:T(8,128)S(1)}, u32[]{:S(2)}, u32[]{:S(2)}) collective-permute-start(f32[2,32,16,128]{3,2,1,0:T(8,128)S(1)} %pad_maximum_fusion), channel_id=1, source_target_pairs={{1,2},{2,1},{3,4},{4,3},{5,6},{6,5},{9,10},{10,9},{11,12},{12,11},... | collective-permute-start | bytes 1572872 | tf_op jit(solution)/shard_map/ppermute | solution.py:361
  15.9 1.4 %shard_map.64 = (bf16[544,256]{1,0:T(8,128)(2,1)S(1)}, f32[2,32,128]{2,1,0:T(8,128)S(1)}) custom-call(f32[25]{0:T(128)S(1)} %copy-done.3, f32[25]{0:T(128)S(1)} %copy-done.4, s32[2,2,4]{2,1,0:T(2,128)S(1)} %copy-done.2, f32[1]{0:T(128)S(6)} %copy.7.step), custom_call_target="tpu_custom_call" | custom-call | flops 1000000 | bytes 1000000 | tf_op jit(solution)/shard_map/pallas_call | solution.py:99
  17.3 0.1 shard_map.68
  17.4 0.1 collective-permute-start.7
  17.6 0.6 %collective-permute-start.3 = (f32[58,16,128]{2,1,0:T(8,128)S(1)}, f32[58,16,128]{2,1,0:T(8,128)S(1)}, u32[]{:S(2)}, u32[]{:S(2)}) collective-permute-start(f32[58,16,128]{2,1,0:T(8,128)S(1)} %get-tuple-element.23), channel_id=1, source_target_pairs={{0,1},{1,0},{2,3},{3,2},{4,5},{5,4},{6,7},{7,6},{8,9},{9,8},{10,11... | collective-permute-start | bytes 1425416 | tf_op jit(solution)/shard_map/ppermute | solution.py:361
  18.1 2.8 %collective-permute-start.8 = (f32[26,16,128]{2,1,0:T(8,128)S(1)}, f32[26,16,128]{2,1,0:T(8,128)S(1)}, u32[]{:S(2)}, u32[]{:S(2)}) collective-permute-start(f32[26,16,128]{2,1,0:T(8,128)S(1)} %get-tuple-element.27), channel_id=1, source_target_pairs={{1,2},{2,1},{3,4},{4,3},{5,6},{6,5},{9,10},{10,9},{11,12},{12,11},... | collective-permute-start | bytes 638984 | tf_op jit(solution)/shard_map/ppermute | solution.py:361
  21.0 2.7 %collective-permute-start.4 = (f32[26,16,128]{2,1,0:T(8,128)S(1)}, f32[26,16,128]{2,1,0:T(8,128)S(1)}, u32[]{:S(2)}, u32[]{:S(2)}) collective-permute-start(f32[26,16,128]{2,1,0:T(8,128)S(1)} %get-tuple-element.24), channel_id=1, source_target_pairs={{1,2},{2,1},{3,4},{4,3},{5,6},{6,5},{9,10},{10,9},{11,12},{12,11},... | collective-permute-start | bytes 638984 | tf_op jit(solution)/shard_map/ppermute | solution.py:361
  23.7 1.9 %collective-permute-done.8.refs_4_ = f32[26,16,128]{2,1,0:T(8,128)S(1)} collective-permute-done((f32[26,16,128]{2,1,0:T(8,128)S(1)}, f32[26,16,128]{2,1,0:T(8,128)S(1)}, u32[]{:S(2)}, u32[]{:S(2)}) %collective-permute-start.8) | collective-permute-done | bytes 213024 | tf_op jit(solution)/shard_map/ppermute | solution.py:361
  25.6 2.7 %shard_map.69 = (f32[32,32,128]{2,1,0:T(8,128)S(1)}, f32[32,32,128]{2,1,0:T(8,128)S(1)}) custom-call(f32[32,32,128]{2,1,0:T(8,128)S(1)} %copy-done, f32[13,32,128]{2,1,0:T(8,128)S(1)} %collective-permute-done.5.x_even.refs_0_, f32[13,32,128]{2,1,0:T(8,128)S(1)} %shard_map.67.x_odd.refs_1_, f32[2,32,16,128]{3,2,1,0:T(8,128)S(1)} %collective-permute-done.2.refs_2_, ...), custom_call_target="tpu_custom_call" | custom-call | tf_op jit(solution)/shard_map/pallas_call | solution.py:306
  28.3 1.6 %shard_map.70 = (f32[32,32,128]{2,1,0:T(8,128)S(1)}, f32[32,32,128]{2,1,0:T(8,128)S(1)}) custom-call(f32[32,32,128]{2,1,0:T(8,128)S(1)} %copy-done.1, f32[13,32,128]{2,1,0:T(8,128)S(1)} %collective-permute-done.x_even.refs_0_, f32[13,32,128]{2,1,0:T(8,128)S(1)} %shard_map.65.x_odd.refs_1_, f32[2,32,16,128]{3,2,1,0:T(8,128)S(1)} %collective-permute-done.2.refs_2_, ...), custom_call_target="tpu_custom_call" | custom-call | tf_op jit(solution)/shard_map/pallas_call | solution.py:306
  30.0 3.6 %collective-permute-start.10 = (f32[13,32,128]{2,1,0:T(8,128)S(1)}, f32[13,32,128]{2,1,0:T(8,128)S(1)}, u32[]{:S(2)}, u32[]{:S(2)}) collective-permute-start(f32[13,32,128]{2,1,0:T(8,128)S(1)} %get-tuple-element.37), channel_id=1, source_target_pairs={{8,16},{16,8},{24,32},{32,24},{40,48},{48,40},{56,64},{64,56},{72,... | collective-permute-start | bytes 638984 | tf_op jit(solution)/shard_map/ppermute | solution.py:361
  33.6 0.8 %collective-permute-start.9 = (f32[13,32,128]{2,1,0:T(8,128)S(1)}, f32[13,32,128]{2,1,0:T(8,128)S(1)}, u32[]{:S(2)}, u32[]{:S(2)}) collective-permute-start(f32[13,32,128]{2,1,0:T(8,128)S(1)} %get-tuple-element.38), channel_id=1, source_target_pairs={{0,8},{8,0},{16,24},{24,16},{32,40},{40,32},{48,56},{56,48},{64,72... | collective-permute-start | bytes 638984 | tf_op jit(solution)/shard_map/ppermute | solution.py:361
  34.4 3.2 %collective-permute-start.12 = (f32[32,16,128]{2,1,0:T(8,128)S(1)}, f32[32,16,128]{2,1,0:T(8,128)S(1)}, u32[]{:S(2)}, u32[]{:S(2)}) collective-permute-start(f32[32,16,128]{2,1,0:T(8,128)S(1)} %get-tuple-element.35), channel_id=1, source_target_pairs={{1,2},{2,1},{3,4},{4,3},{5,6},{6,5},{9,10},{10,9},{11,12},{12,11},... | collective-permute-start | bytes 786440 | tf_op jit(solution)/shard_map/ppermute | solution.py:361
  37.6 0.1 collective-permute-start.11
  37.7 3.4 %collective-permute-done.10.source = f32[13,32,128]{2,1,0:T(8,128)S(1)} collective-permute-done((f32[13,32,128]{2,1,0:T(8,128)S(1)}, f32[13,32,128]{2,1,0:T(8,128)S(1)}, u32[]{:S(2)}, u32[]{:S(2)}) %collective-permute-start.10) | collective-permute-done | bytes 213024 | tf_op jit(solution)/shard_map/ppermute | solution.py:361
  41.1 0.7 %collective-permute-start.13 = (f32[26,16,128]{2,1,0:T(8,128)S(1)}, f32[26,16,128]{2,1,0:T(8,128)S(1)}, u32[]{:S(2)}, u32[]{:S(2)}) collective-permute-start(f32[26,16,128]{2,1,0:T(8,128)S(1)} %get-tuple-element.32), channel_id=1, source_target_pairs={{0,1},{1,0},{2,3},{3,2},{4,5},{5,4},{6,7},{7,6},{8,9},{9,8},{10,11... | collective-permute-start | bytes 638984 | tf_op jit(solution)/shard_map/ppermute | solution.py:361
  41.8 2.8 %collective-permute-start.14 = (f32[26,16,128]{2,1,0:T(8,128)S(1)}, f32[26,16,128]{2,1,0:T(8,128)S(1)}, u32[]{:S(2)}, u32[]{:S(2)}) collective-permute-start(f32[26,16,128]{2,1,0:T(8,128)S(1)} %get-tuple-element.33), channel_id=1, source_target_pairs={{1,2},{2,1},{3,4},{4,3},{5,6},{6,5},{9,10},{10,9},{11,12},{12,11},... | collective-permute-start | bytes 638984 | tf_op jit(solution)/shard_map/ppermute | solution.py:361
  44.7 4.3 %collective-permute-done.14.refs_5_ = f32[26,16,128]{2,1,0:T(8,128)S(1)} collective-permute-done((f32[26,16,128]{2,1,0:T(8,128)S(1)}, f32[26,16,128]{2,1,0:T(8,128)S(1)}, u32[]{:S(2)}, u32[]{:S(2)}) %collective-permute-start.14) | collective-permute-done | bytes 213024 | tf_op jit(solution)/shard_map/ppermute | solution.py:361
  48.9 3.3 %shard_map.74 = f32[32,32,128]{2,1,0:T(8,128)} custom-call(f32[32,32,128]{2,1,0:T(8,128)S(1)} %get-tuple-element.31.own, f32[13,32,128]{2,1,0:T(8,128)S(1)} %collective-permute-done.9.x_even.refs_0_, f32[13,32,128]{2,1,0:T(8,128)S(1)} %shard_map.71.x_odd.refs_1_, f32[32,16,128]{2,1,0:T(8,128)S(1)} %collective-permute-done.11.refs_2_, ...), custom_call_target="tpu_custom_call" | custom-call | tf_op jit(solution)/shard_map/pallas_call | solution.py:306
  (34 shorter events, 0.4 us)
Async XLA Ops:
  0.0 5.7 %copy-start.1 = (f32[32,32,128]{2,1,0:T(8,128)S(1)}, f32[32,32,128]{2,1,0:T(8,128)}, u32[]{:S(2)}) copy-start(f32[32,32,128]{2,1,0:T(8,128)} %own.7) | copy-start | bytes 1572868
  1.1 9.1 %copy-start = (f32[32,32,128]{2,1,0:T(8,128)S(1)}, f32[32,32,128]{2,1,0:T(8,128)}, u32[]{:S(2)}) copy-start(f32[32,32,128]{2,1,0:T(8,128)} %own.6) | copy-start | bytes 1572868
  1.1 16.1 %collective-permute-start.6 = (f32[13,32,128]{2,1,0:T(8,128)S(1)}, f32[13,32,128]{2,1,0:T(8,128)S(1)}, u32[]{:S(2)}, u32[]{:S(2)}) collective-permute-start(f32[13,32,128]{2,1,0:T(8,128)S(1)} %get-tuple-element.39), channel_id=1, source_target_pairs={{8,16},{16,8},{24,32},{32,24},{40,48},{48,40},{56,64},{64,56},{72,... | collective-permute-start | bytes 638984 | tf_op jit(solution)/shard_map/ppermute | solution.py:361
  5.2 12.1 %collective-permute-start.5 = (f32[13,32,128]{2,1,0:T(8,128)S(1)}, f32[13,32,128]{2,1,0:T(8,128)S(1)}, u32[]{:S(2)}, u32[]{:S(2)}) collective-permute-start(f32[13,32,128]{2,1,0:T(8,128)S(1)} %get-tuple-element.40), channel_id=1, source_target_pairs={{0,8},{8,0},{16,24},{24,16},{32,40},{40,32},{48,56},{56,48},{64,72... | collective-permute-start | bytes 638984 | tf_op jit(solution)/shard_map/ppermute | solution.py:361
  5.7 11.8 %collective-permute-start.1 = (f32[13,32,128]{2,1,0:T(8,128)S(1)}, f32[13,32,128]{2,1,0:T(8,128)S(1)}, u32[]{:S(2)}, u32[]{:S(2)}) collective-permute-start(f32[13,32,128]{2,1,0:T(8,128)S(1)} %get-tuple-element.41), channel_id=1, source_target_pairs={{8,16},{16,8},{24,32},{32,24},{40,48},{48,40},{56,64},{64,56},{72,... | collective-permute-start | bytes 638984 | tf_op jit(solution)/shard_map/ppermute | solution.py:361
  8.8 8.7 %collective-permute-start = (f32[13,32,128]{2,1,0:T(8,128)S(1)}, f32[13,32,128]{2,1,0:T(8,128)S(1)}, u32[]{:S(2)}, u32[]{:S(2)}) collective-permute-start(f32[13,32,128]{2,1,0:T(8,128)S(1)} %get-tuple-element.42), channel_id=1, source_target_pairs={{0,8},{8,0},{16,24},{24,16},{32,40},{40,32},{48,56},{56,48},{64,72... | collective-permute-start | bytes 638984 | tf_op jit(solution)/shard_map/ppermute | solution.py:361
  10.3 5.6 %copy-start.2 = (s32[2,2,4]{2,1,0:T(2,128)S(1)}, s32[2,2,4]{2,1,0:T(2,128)}, u32[]{:S(2)}) copy-start(s32[2,2,4]{2,1,0:T(2,128)} %band.1) | copy-start | bytes 196
  10.3 5.6 %copy-start.3 = (f32[25]{0:T(128)S(1)}, f32[25]{0:T(128)}, u32[]{:S(2)}) copy-start(f32[25]{0:T(128)} %smooth.1) | copy-start | bytes 304
  10.3 5.6 %copy-start.4 = (f32[25]{0:T(128)S(1)}, f32[25]{0:T(128)}, u32[]{:S(2)}) copy-start(f32[25]{0:T(128)} %slope.1) | copy-start | bytes 304
  10.3 15.3 %collective-permute-start.2 = (f32[2,32,16,128]{3,2,1,0:T(8,128)S(1)}, f32[2,32,16,128]{3,2,1,0:T(8,128)S(1)}, u32[]{:S(2)}, u32[]{:S(2)}) collective-permute-start(f32[2,32,16,128]{3,2,1,0:T(8,128)S(1)} %pad_maximum_fusion), channel_id=1, source_target_pairs={{1,2},{2,1},{3,4},{4,3},{5,6},{6,5},{9,10},{10,9},{11,12},{12,11},... | collective-permute-start | bytes 1572872 | tf_op jit(solution)/shard_map/ppermute | solution.py:361
  17.4 8.2 %collective-permute-start.7 = (f32[58,16,128]{2,1,0:T(8,128)S(1)}, f32[58,16,128]{2,1,0:T(8,128)S(1)}, u32[]{:S(2)}, u32[]{:S(2)}) collective-permute-start(f32[58,16,128]{2,1,0:T(8,128)S(1)} %get-tuple-element.26), channel_id=1, source_target_pairs={{0,1},{1,0},{2,3},{3,2},{4,5},{5,4},{6,7},{7,6},{8,9},{9,8},{10,11... | collective-permute-start | bytes 1425416 | tf_op jit(solution)/shard_map/ppermute | solution.py:361
  17.6 10.7 %collective-permute-start.3 = (f32[58,16,128]{2,1,0:T(8,128)S(1)}, f32[58,16,128]{2,1,0:T(8,128)S(1)}, u32[]{:S(2)}, u32[]{:S(2)}) collective-permute-start(f32[58,16,128]{2,1,0:T(8,128)S(1)} %get-tuple-element.23), channel_id=1, source_target_pairs={{0,1},{1,0},{2,3},{3,2},{4,5},{5,4},{6,7},{7,6},{8,9},{9,8},{10,11... | collective-permute-start | bytes 1425416 | tf_op jit(solution)/shard_map/ppermute | solution.py:361
  18.1 7.4 %collective-permute-start.8 = (f32[26,16,128]{2,1,0:T(8,128)S(1)}, f32[26,16,128]{2,1,0:T(8,128)S(1)}, u32[]{:S(2)}, u32[]{:S(2)}) collective-permute-start(f32[26,16,128]{2,1,0:T(8,128)S(1)} %get-tuple-element.27), channel_id=1, source_target_pairs={{1,2},{2,1},{3,4},{4,3},{5,6},{6,5},{9,10},{10,9},{11,12},{12,11},... | collective-permute-start | bytes 638984 | tf_op jit(solution)/shard_map/ppermute | solution.py:361
  21.0 7.3 %collective-permute-start.4 = (f32[26,16,128]{2,1,0:T(8,128)S(1)}, f32[26,16,128]{2,1,0:T(8,128)S(1)}, u32[]{:S(2)}, u32[]{:S(2)}) collective-permute-start(f32[26,16,128]{2,1,0:T(8,128)S(1)} %get-tuple-element.24), channel_id=1, source_target_pairs={{1,2},{2,1},{3,4},{4,3},{5,6},{6,5},{9,10},{10,9},{11,12},{12,11},... | collective-permute-start | bytes 638984 | tf_op jit(solution)/shard_map/ppermute | solution.py:361
  30.0 11.1 %collective-permute-start.10 = (f32[13,32,128]{2,1,0:T(8,128)S(1)}, f32[13,32,128]{2,1,0:T(8,128)S(1)}, u32[]{:S(2)}, u32[]{:S(2)}) collective-permute-start(f32[13,32,128]{2,1,0:T(8,128)S(1)} %get-tuple-element.37), channel_id=1, source_target_pairs={{8,16},{16,8},{24,32},{32,24},{40,48},{48,40},{56,64},{64,56},{72,... | collective-permute-start | bytes 638984 | tf_op jit(solution)/shard_map/ppermute | solution.py:361
  33.6 7.5 %collective-permute-start.9 = (f32[13,32,128]{2,1,0:T(8,128)S(1)}, f32[13,32,128]{2,1,0:T(8,128)S(1)}, u32[]{:S(2)}, u32[]{:S(2)}) collective-permute-start(f32[13,32,128]{2,1,0:T(8,128)S(1)} %get-tuple-element.38), channel_id=1, source_target_pairs={{0,8},{8,0},{16,24},{24,16},{32,40},{40,32},{48,56},{56,48},{64,72... | collective-permute-start | bytes 638984 | tf_op jit(solution)/shard_map/ppermute | solution.py:361
  34.4 10.2 %collective-permute-start.12 = (f32[32,16,128]{2,1,0:T(8,128)S(1)}, f32[32,16,128]{2,1,0:T(8,128)S(1)}, u32[]{:S(2)}, u32[]{:S(2)}) collective-permute-start(f32[32,16,128]{2,1,0:T(8,128)S(1)} %get-tuple-element.35), channel_id=1, source_target_pairs={{1,2},{2,1},{3,4},{4,3},{5,6},{6,5},{9,10},{10,9},{11,12},{12,11},... | collective-permute-start | bytes 786440 | tf_op jit(solution)/shard_map/ppermute | solution.py:361
  37.6 7.1 %collective-permute-start.11 = (f32[32,16,128]{2,1,0:T(8,128)S(1)}, f32[32,16,128]{2,1,0:T(8,128)S(1)}, u32[]{:S(2)}, u32[]{:S(2)}) collective-permute-start(f32[32,16,128]{2,1,0:T(8,128)S(1)} %get-tuple-element.36), channel_id=1, source_target_pairs={{0,1},{1,0},{2,3},{3,2},{4,5},{5,4},{6,7},{7,6},{8,9},{9,8},{10,11... | collective-permute-start | bytes 786440 | tf_op jit(solution)/shard_map/ppermute | solution.py:361
  41.1 3.5 %collective-permute-start.13 = (f32[26,16,128]{2,1,0:T(8,128)S(1)}, f32[26,16,128]{2,1,0:T(8,128)S(1)}, u32[]{:S(2)}, u32[]{:S(2)}) collective-permute-start(f32[26,16,128]{2,1,0:T(8,128)S(1)} %get-tuple-element.32), channel_id=1, source_target_pairs={{0,1},{1,0},{2,3},{3,2},{4,5},{5,4},{6,7},{7,6},{8,9},{9,8},{10,11... | collective-permute-start | bytes 638984 | tf_op jit(solution)/shard_map/ppermute | solution.py:361
  41.8 7.2 %collective-permute-start.14 = (f32[26,16,128]{2,1,0:T(8,128)S(1)}, f32[26,16,128]{2,1,0:T(8,128)S(1)}, u32[]{:S(2)}, u32[]{:S(2)}) collective-permute-start(f32[26,16,128]{2,1,0:T(8,128)S(1)} %get-tuple-element.33), channel_id=1, source_target_pairs={{1,2},{2,1},{3,4},{4,3},{5,6},{6,5},{9,10},{10,9},{11,12},{12,11},... | collective-permute-start | bytes 638984 | tf_op jit(solution)/shard_map/ppermute | solution.py:361

commit v9 on v7

--- a/solution.py
+++ b/solution.py
@@ -396,7 +396,6 @@
         y_halos = swap_sides(both_sides(phi, 1, SLAB, parity[1]), "gy")
         x_halos = (x_halos[0], settle(x_halos[1]))
         corners = swap_sides(corner_sides(phi, x_halos), "gy")
-        y_halos = (y_halos[0], settle(y_halos[1]))
         (phi,) = call_kernel(
             later_kernel, (phi, *x_halos, *y_halos, *corners, matrices, gain, speed), 1, gradient_scratch,
         )

time: 52.7 us -> 52.7 us (level)
  no operation moved by 1% of the time
where the time goes in v9:
time: 52.7 us; the launch traced here: 52.4 us
  starting transfers between devices  31.4 us (60%)
  waiting for transfers between devices  9.45 us (18%)
  Pallas kernels  9.28 us (18%)
  local copies, waits for them, and re-layouts  1.3 us (2%)
  between operations  0.96 us (2%)
    ppermute x15, starting transfers between devices, swap(): return lax.ppermute(block, axis, pairs)  31.4 us
    ppermute x15, waiting for transfers between devices, swap(): return lax.ppermute(block, axis, pairs)  9.45 us
    pallas_call x3, Pallas kernels, call_kernel(): pl.pallas_call(body, out_shape=(shape,) * outputs, in_specs=[VMEM] * len(...  7.72 us
    pallas_call x1, Pallas kernels, prepare(): pl.pallas_call(prepare_kernel, out_shape=(jax.ShapeDtypeStruct((4 * RIM +...  1.36 us
    dynamic_slice x4, local copies, waits for them, and re-layouts, both_sides(): lax.dynamic_slice_in_dim(block, length - width - high, width, dim)  1.22 us
  transfers between devices with their start and end apart: 15, of which 3 were waited for; matrix products, arithmetic and copies ran while one was open for 0% of the time, Pallas kernels for 8%

profile of v9, /device:TPU:41, one launch (start us, length us, event | category | flops | bytes accessed | tf_op | source)
XLA Modules:
  0.0 52.4 jit_solution(7802956941760783826)
XLA Ops:
  0.0 1.1 %constant_dynamic-slice_fusion.4 = (f32[13,32,128]{2,1,0:T(8,128)S(1)}, f32[13,32,128]{2,1,0:T(8,128)S(1)}) fusion(f32[32,32,128]{2,1,0:T(8,128)} %own.6, s32[]{:T(128)S(6)} %select_n.26, s32[]{:T(128)S(6)} %select_n.25), kind=kLoop, calls=%fused_computation.7 | loop fusion | bytes 851976 | tf_op jit(solution)/shard_map/dynamic_slice | solution.py:355
  1.1 4.1 %collective-permute-start.6 = (f32[13,32,128]{2,1,0:T(8,128)S(1)}, f32[13,32,128]{2,1,0:T(8,128)S(1)}, u32[]{:S(2)}, u32[]{:S(2)}) collective-permute-start(f32[13,32,128]{2,1,0:T(8,128)S(1)} %get-tuple-element.39), channel_id=1, source_target_pairs={{8,16},{16,8},{24,32},{32,24},{40,48},{48,40},{56,64},{64,56},{72,... | collective-permute-start | bytes 638984 | tf_op jit(solution)/shard_map/ppermute | solution.py:347
  5.2 0.5 collective-permute-start.5
  5.7 3.1 %collective-permute-start.1 = (f32[13,32,128]{2,1,0:T(8,128)S(1)}, f32[13,32,128]{2,1,0:T(8,128)S(1)}, u32[]{:S(2)}, u32[]{:S(2)}) collective-permute-start(f32[13,32,128]{2,1,0:T(8,128)S(1)} %get-tuple-element.41), channel_id=1, source_target_pairs={{8,16},{16,8},{24,32},{32,24},{40,48},{48,40},{56,64},{64,56},{72,... | collective-permute-start | bytes 638984 | tf_op jit(solution)/shard_map/ppermute | solution.py:347
  8.8 1.4 %collective-permute-start = (f32[13,32,128]{2,1,0:T(8,128)S(1)}, f32[13,32,128]{2,1,0:T(8,128)S(1)}, u32[]{:S(2)}, u32[]{:S(2)}) collective-permute-start(f32[13,32,128]{2,1,0:T(8,128)S(1)} %get-tuple-element.42), channel_id=1, source_target_pairs={{0,8},{8,0},{16,24},{24,16},{32,40},{40,32},{48,56},{56,48},{64,72... | collective-permute-start | bytes 638984 | tf_op jit(solution)/shard_map/ppermute | solution.py:347
  10.3 4.9 %collective-permute-start.2 = (f32[2,32,16,128]{3,2,1,0:T(8,128)S(1)}, f32[2,32,16,128]{3,2,1,0:T(8,128)S(1)}, u32[]{:S(2)}, u32[]{:S(2)}) collective-permute-start(f32[2,32,16,128]{3,2,1,0:T(8,128)S(1)} %pad_maximum_fusion), channel_id=1, source_target_pairs={{1,2},{2,1},{3,4},{4,3},{5,6},{6,5},{9,10},{10,9},{11,12},{12,11},... | collective-permute-start | bytes 1572872 | tf_op jit(solution)/shard_map/ppermute | solution.py:347
  15.9 1.4 %shard_map.64 = (bf16[544,256]{1,0:T(8,128)(2,1)S(1)}, f32[2,32,128]{2,1,0:T(8,128)S(1)}) custom-call(f32[25]{0:T(128)S(1)} %copy-done.3, f32[25]{0:T(128)S(1)} %copy-done.4, s32[2,2,4]{2,1,0:T(2,128)S(1)} %copy-done.2, f32[1]{0:T(128)S(6)} %copy.7.step), custom_call_target="tpu_custom_call" | custom-call | flops 1000000 | bytes 1000000 | tf_op jit(solution)/shard_map/pallas_call | solution.py:99
  17.3 0.1 shard_map.68
  17.4 0.1 collective-permute-start.7
  17.6 0.6 %collective-permute-start.3 = (f32[58,16,128]{2,1,0:T(8,128)S(1)}, f32[58,16,128]{2,1,0:T(8,128)S(1)}, u32[]{:S(2)}, u32[]{:S(2)}) collective-permute-start(f32[58,16,128]{2,1,0:T(8,128)S(1)} %get-tuple-element.23), channel_id=1, source_target_pairs={{0,1},{1,0},{2,3},{3,2},{4,5},{5,4},{6,7},{7,6},{8,9},{9,8},{10,11... | collective-permute-start | bytes 1425416 | tf_op jit(solution)/shard_map/ppermute | solution.py:347
  18.1 2.8 %collective-permute-start.8 = (f32[26,16,128]{2,1,0:T(8,128)S(1)}, f32[26,16,128]{2,1,0:T(8,128)S(1)}, u32[]{:S(2)}, u32[]{:S(2)}) collective-permute-start(f32[26,16,128]{2,1,0:T(8,128)S(1)} %get-tuple-element.27), channel_id=1, source_target_pairs={{1,2},{2,1},{3,4},{4,3},{5,6},{6,5},{9,10},{10,9},{11,12},{12,11},... | collective-permute-start | bytes 638984 | tf_op jit(solution)/shard_map/ppermute | solution.py:347
  21.0 2.7 %collective-permute-start.4 = (f32[26,16,128]{2,1,0:T(8,128)S(1)}, f32[26,16,128]{2,1,0:T(8,128)S(1)}, u32[]{:S(2)}, u32[]{:S(2)}) collective-permute-start(f32[26,16,128]{2,1,0:T(8,128)S(1)} %get-tuple-element.24), channel_id=1, source_target_pairs={{1,2},{2,1},{3,4},{4,3},{5,6},{6,5},{9,10},{10,9},{11,12},{12,11},... | collective-permute-start | bytes 638984 | tf_op jit(solution)/shard_map/ppermute | solution.py:347
  23.7 1.9 %collective-permute-done.8.refs_4_ = f32[26,16,128]{2,1,0:T(8,128)S(1)} collective-permute-done((f32[26,16,128]{2,1,0:T(8,128)S(1)}, f32[26,16,128]{2,1,0:T(8,128)S(1)}, u32[]{:S(2)}, u32[]{:S(2)}) %collective-permute-start.8) | collective-permute-done | bytes 213024 | tf_op jit(solution)/shard_map/ppermute | solution.py:347
  25.6 2.7 %shard_map.69 = (f32[32,32,128]{2,1,0:T(8,128)S(1)}, f32[32,32,128]{2,1,0:T(8,128)S(1)}) custom-call(f32[32,32,128]{2,1,0:T(8,128)S(1)} %copy-done, f32[13,32,128]{2,1,0:T(8,128)S(1)} %collective-permute-done.5.x_even.refs_0_, f32[13,32,128]{2,1,0:T(8,128)S(1)} %shard_map.67.x_odd.refs_1_, f32[2,32,16,128]{3,2,1,0:T(8,128)S(1)} %collective-permute-done.2.refs_2_, ...), custom_call_target="tpu_custom_call" | custom-call | tf_op jit(solution)/shard_map/pallas_call | solution.py:292
  28.3 1.6 %shard_map.70 = (f32[32,32,128]{2,1,0:T(8,128)S(1)}, f32[32,32,128]{2,1,0:T(8,128)S(1)}) custom-call(f32[32,32,128]{2,1,0:T(8,128)S(1)} %copy-done.1, f32[13,32,128]{2,1,0:T(8,128)S(1)} %collective-permute-done.x_even.refs_0_, f32[13,32,128]{2,1,0:T(8,128)S(1)} %shard_map.65.x_odd.refs_1_, f32[2,32,16,128]{3,2,1,0:T(8,128)S(1)} %collective-permute-done.2.refs_2_, ...), custom_call_target="tpu_custom_call" | custom-call | tf_op jit(solution)/shard_map/pallas_call | solution.py:292
  30.0 3.6 %collective-permute-start.10 = (f32[13,32,128]{2,1,0:T(8,128)S(1)}, f32[13,32,128]{2,1,0:T(8,128)S(1)}, u32[]{:S(2)}, u32[]{:S(2)}) collective-permute-start(f32[13,32,128]{2,1,0:T(8,128)S(1)} %get-tuple-element.37), channel_id=1, source_target_pairs={{8,16},{16,8},{24,32},{32,24},{40,48},{48,40},{56,64},{64,56},{72,... | collective-permute-start | bytes 638984 | tf_op jit(solution)/shard_map/ppermute | solution.py:347
  33.6 0.8 %collective-permute-start.9 = (f32[13,32,128]{2,1,0:T(8,128)S(1)}, f32[13,32,128]{2,1,0:T(8,128)S(1)}, u32[]{:S(2)}, u32[]{:S(2)}) collective-permute-start(f32[13,32,128]{2,1,0:T(8,128)S(1)} %get-tuple-element.38), channel_id=1, source_target_pairs={{0,8},{8,0},{16,24},{24,16},{32,40},{40,32},{48,56},{56,48},{64,72... | collective-permute-start | bytes 638984 | tf_op jit(solution)/shard_map/ppermute | solution.py:347
  34.4 0.4 collective-permute-start.11
  34.8 3.0 %collective-permute-start.12 = (f32[32,16,128]{2,1,0:T(8,128)S(1)}, f32[32,16,128]{2,1,0:T(8,128)S(1)}, u32[]{:S(2)}, u32[]{:S(2)}) collective-permute-start(f32[32,16,128]{2,1,0:T(8,128)S(1)} %get-tuple-element.35), channel_id=1, source_target_pairs={{1,2},{2,1},{3,4},{4,3},{5,6},{6,5},{9,10},{10,9},{11,12},{12,11},... | collective-permute-start | bytes 786440 | tf_op jit(solution)/shard_map/ppermute | solution.py:347
  37.8 3.2 %collective-permute-done.10.source = f32[13,32,128]{2,1,0:T(8,128)S(1)} collective-permute-done((f32[13,32,128]{2,1,0:T(8,128)S(1)}, f32[13,32,128]{2,1,0:T(8,128)S(1)}, u32[]{:S(2)}, u32[]{:S(2)}) %collective-permute-start.10) | collective-permute-done | bytes 213024 | tf_op jit(solution)/shard_map/ppermute | solution.py:347
  41.1 0.7 %collective-permute-start.13 = (f32[26,16,128]{2,1,0:T(8,128)S(1)}, f32[26,16,128]{2,1,0:T(8,128)S(1)}, u32[]{:S(2)}, u32[]{:S(2)}) collective-permute-start(f32[26,16,128]{2,1,0:T(8,128)S(1)} %get-tuple-element.32), channel_id=1, source_target_pairs={{0,1},{1,0},{2,3},{3,2},{4,5},{5,4},{6,7},{7,6},{8,9},{9,8},{10,11... | collective-permute-start | bytes 638984 | tf_op jit(solution)/shard_map/ppermute | solution.py:347
  41.8 2.8 %collective-permute-start.14 = (f32[26,16,128]{2,1,0:T(8,128)S(1)}, f32[26,16,128]{2,1,0:T(8,128)S(1)}, u32[]{:S(2)}, u32[]{:S(2)}) collective-permute-start(f32[26,16,128]{2,1,0:T(8,128)S(1)} %get-tuple-element.33), channel_id=1, source_target_pairs={{1,2},{2,1},{3,4},{4,3},{5,6},{6,5},{9,10},{10,9},{11,12},{12,11},... | collective-permute-start | bytes 638984 | tf_op jit(solution)/shard_map/ppermute | solution.py:347
  44.6 4.3 %collective-permute-done.14.refs_5_ = f32[26,16,128]{2,1,0:T(8,128)S(1)} collective-permute-done((f32[26,16,128]{2,1,0:T(8,128)S(1)}, f32[26,16,128]{2,1,0:T(8,128)S(1)}, u32[]{:S(2)}, u32[]{:S(2)}) %collective-permute-start.14) | collective-permute-done | bytes 213024 | tf_op jit(solution)/shard_map/ppermute | solution.py:347
  48.9 3.4 %shard_map.73 = f32[32,32,128]{2,1,0:T(8,128)} custom-call(f32[32,32,128]{2,1,0:T(8,128)S(1)} %get-tuple-element.31.own, f32[13,32,128]{2,1,0:T(8,128)S(1)} %collective-permute-done.9.x_even.refs_0_, f32[13,32,128]{2,1,0:T(8,128)S(1)} %shard_map.71.x_odd.refs_1_, f32[32,16,128]{2,1,0:T(8,128)S(1)} %collective-permute-done.11.refs_2_, ...), custom_call_target="tpu_custom_call" | custom-call | tf_op jit(solution)/shard_map/pallas_call | solution.py:292
  (33 shorter events, 0.4 us)
Async XLA Ops:
  0.0 5.7 %copy-start.1 = (f32[32,32,128]{2,1,0:T(8,128)S(1)}, f32[32,32,128]{2,1,0:T(8,128)}, u32[]{:S(2)}) copy-start(f32[32,32,128]{2,1,0:T(8,128)} %own.7) | copy-start | bytes 1572868
  1.1 9.1 %copy-start = (f32[32,32,128]{2,1,0:T(8,128)S(1)}, f32[32,32,128]{2,1,0:T(8,128)}, u32[]{:S(2)}) copy-start(f32[32,32,128]{2,1,0:T(8,128)} %own.6) | copy-start | bytes 1572868
  1.1 16.1 %collective-permute-start.6 = (f32[13,32,128]{2,1,0:T(8,128)S(1)}, f32[13,32,128]{2,1,0:T(8,128)S(1)}, u32[]{:S(2)}, u32[]{:S(2)}) collective-permute-start(f32[13,32,128]{2,1,0:T(8,128)S(1)} %get-tuple-element.39), channel_id=1, source_target_pairs={{8,16},{16,8},{24,32},{32,24},{40,48},{48,40},{56,64},{64,56},{72,... | collective-permute-start | bytes 638984 | tf_op jit(solution)/shard_map/ppermute | solution.py:347
  5.2 12.1 %collective-permute-start.5 = (f32[13,32,128]{2,1,0:T(8,128)S(1)}, f32[13,32,128]{2,1,0:T(8,128)S(1)}, u32[]{:S(2)}, u32[]{:S(2)}) collective-permute-start(f32[13,32,128]{2,1,0:T(8,128)S(1)} %get-tuple-element.40), channel_id=1, source_target_pairs={{0,8},{8,0},{16,24},{24,16},{32,40},{40,32},{48,56},{56,48},{64,72... | collective-permute-start | bytes 638984 | tf_op jit(solution)/shard_map/ppermute | solution.py:347
  5.7 11.8 %collective-permute-start.1 = (f32[13,32,128]{2,1,0:T(8,128)S(1)}, f32[13,32,128]{2,1,0:T(8,128)S(1)}, u32[]{:S(2)}, u32[]{:S(2)}) collective-permute-start(f32[13,32,128]{2,1,0:T(8,128)S(1)} %get-tuple-element.41), channel_id=1, source_target_pairs={{8,16},{16,8},{24,32},{32,24},{40,48},{48,40},{56,64},{64,56},{72,... | collective-permute-start | bytes 638984 | tf_op jit(solution)/shard_map/ppermute | solution.py:347
  8.8 8.7 %collective-permute-start = (f32[13,32,128]{2,1,0:T(8,128)S(1)}, f32[13,32,128]{2,1,0:T(8,128)S(1)}, u32[]{:S(2)}, u32[]{:S(2)}) collective-permute-start(f32[13,32,128]{2,1,0:T(8,128)S(1)} %get-tuple-element.42), channel_id=1, source_target_pairs={{0,8},{8,0},{16,24},{24,16},{32,40},{40,32},{48,56},{56,48},{64,72... | collective-permute-start | bytes 638984 | tf_op jit(solution)/shard_map/ppermute | solution.py:347
  10.3 5.6 %copy-start.2 = (s32[2,2,4]{2,1,0:T(2,128)S(1)}, s32[2,2,4]{2,1,0:T(2,128)}, u32[]{:S(2)}) copy-start(s32[2,2,4]{2,1,0:T(2,128)} %band.1) | copy-start | bytes 196
  10.3 5.6 %copy-start.3 = (f32[25]{0:T(128)S(1)}, f32[25]{0:T(128)}, u32[]{:S(2)}) copy-start(f32[25]{0:T(128)} %smooth.1) | copy-start | bytes 304
  10.3 5.6 %copy-start.4 = (f32[25]{0:T(128)S(1)}, f32[25]{0:T(128)}, u32[]{:S(2)}) copy-start(f32[25]{0:T(128)} %slope.1) | copy-start | bytes 304
  10.3 15.3 %collective-permute-start.2 = (f32[2,32,16,128]{3,2,1,0:T(8,128)S(1)}, f32[2,32,16,128]{3,2,1,0:T(8,128)S(1)}, u32[]{:S(2)}, u32[]{:S(2)}) collective-permute-start(f32[2,32,16,128]{3,2,1,0:T(8,128)S(1)} %pad_maximum_fusion), channel_id=1, source_target_pairs={{1,2},{2,1},{3,4},{4,3},{5,6},{6,5},{9,10},{10,9},{11,12},{12,11},... | collective-permute-start | bytes 1572872 | tf_op jit(solution)/shard_map/ppermute | solution.py:347
  17.4 8.2 %collective-permute-start.7 = (f32[58,16,128]{2,1,0:T(8,128)S(1)}, f32[58,16,128]{2,1,0:T(8,128)S(1)}, u32[]{:S(2)}, u32[]{:S(2)}) collective-permute-start(f32[58,16,128]{2,1,0:T(8,128)S(1)} %get-tuple-element.26), channel_id=1, source_target_pairs={{0,1},{1,0},{2,3},{3,2},{4,5},{5,4},{6,7},{7,6},{8,9},{9,8},{10,11... | collective-permute-start | bytes 1425416 | tf_op jit(solution)/shard_map/ppermute | solution.py:347
  17.6 10.7 %collective-permute-start.3 = (f32[58,16,128]{2,1,0:T(8,128)S(1)}, f32[58,16,128]{2,1,0:T(8,128)S(1)}, u32[]{:S(2)}, u32[]{:S(2)}) collective-permute-start(f32[58,16,128]{2,1,0:T(8,128)S(1)} %get-tuple-element.23), channel_id=1, source_target_pairs={{0,1},{1,0},{2,3},{3,2},{4,5},{5,4},{6,7},{7,6},{8,9},{9,8},{10,11... | collective-permute-start | bytes 1425416 | tf_op jit(solution)/shard_map/ppermute | solution.py:347
  18.1 7.4 %collective-permute-start.8 = (f32[26,16,128]{2,1,0:T(8,128)S(1)}, f32[26,16,128]{2,1,0:T(8,128)S(1)}, u32[]{:S(2)}, u32[]{:S(2)}) collective-permute-start(f32[26,16,128]{2,1,0:T(8,128)S(1)} %get-tuple-element.27), channel_id=1, source_target_pairs={{1,2},{2,1},{3,4},{4,3},{5,6},{6,5},{9,10},{10,9},{11,12},{12,11},... | collective-permute-start | bytes 638984 | tf_op jit(solution)/shard_map/ppermute | solution.py:347
  21.0 7.3 %collective-permute-start.4 = (f32[26,16,128]{2,1,0:T(8,128)S(1)}, f32[26,16,128]{2,1,0:T(8,128)S(1)}, u32[]{:S(2)}, u32[]{:S(2)}) collective-permute-start(f32[26,16,128]{2,1,0:T(8,128)S(1)} %get-tuple-element.24), channel_id=1, source_target_pairs={{1,2},{2,1},{3,4},{4,3},{5,6},{6,5},{9,10},{10,9},{11,12},{12,11},... | collective-permute-start | bytes 638984 | tf_op jit(solution)/shard_map/ppermute | solution.py:347
  30.0 11.1 %collective-permute-start.10 = (f32[13,32,128]{2,1,0:T(8,128)S(1)}, f32[13,32,128]{2,1,0:T(8,128)S(1)}, u32[]{:S(2)}, u32[]{:S(2)}) collective-permute-start(f32[13,32,128]{2,1,0:T(8,128)S(1)} %get-tuple-element.37), channel_id=1, source_target_pairs={{8,16},{16,8},{24,32},{32,24},{40,48},{48,40},{56,64},{64,56},{72,... | collective-permute-start | bytes 638984 | tf_op jit(solution)/shard_map/ppermute | solution.py:347
  33.6 7.5 %collective-permute-start.9 = (f32[13,32,128]{2,1,0:T(8,128)S(1)}, f32[13,32,128]{2,1,0:T(8,128)S(1)}, u32[]{:S(2)}, u32[]{:S(2)}) collective-permute-start(f32[13,32,128]{2,1,0:T(8,128)S(1)} %get-tuple-element.38), channel_id=1, source_target_pairs={{0,8},{8,0},{16,24},{24,16},{32,40},{40,32},{48,56},{56,48},{64,72... | collective-permute-start | bytes 638984 | tf_op jit(solution)/shard_map/ppermute | solution.py:347
  34.4 10.2 %collective-permute-start.11 = (f32[32,16,128]{2,1,0:T(8,128)S(1)}, f32[32,16,128]{2,1,0:T(8,128)S(1)}, u32[]{:S(2)}, u32[]{:S(2)}) collective-permute-start(f32[32,16,128]{2,1,0:T(8,128)S(1)} %get-tuple-element.36), channel_id=1, source_target_pairs={{0,1},{1,0},{2,3},{3,2},{4,5},{5,4},{6,7},{7,6},{8,9},{9,8},{10,11... | collective-permute-start | bytes 786440 | tf_op jit(solution)/shard_map/ppermute | solution.py:347
  34.8 9.8 %collective-permute-start.12 = (f32[32,16,128]{2,1,0:T(8,128)S(1)}, f32[32,16,128]{2,1,0:T(8,128)S(1)}, u32[]{:S(2)}, u32[]{:S(2)}) collective-permute-start(f32[32,16,128]{2,1,0:T(8,128)S(1)} %get-tuple-element.35), channel_id=1, source_target_pairs={{1,2},{2,1},{3,4},{4,3},{5,6},{6,5},{9,10},{10,9},{11,12},{12,11},... | collective-permute-start | bytes 786440 | tf_op jit(solution)/shard_map/ppermute | solution.py:347
  41.1 3.5 %collective-permute-start.13 = (f32[26,16,128]{2,1,0:T(8,128)S(1)}, f32[26,16,128]{2,1,0:T(8,128)S(1)}, u32[]{:S(2)}, u32[]{:S(2)}) collective-permute-start(f32[26,16,128]{2,1,0:T(8,128)S(1)} %get-tuple-element.32), channel_id=1, source_target_pairs={{0,1},{1,0},{2,3},{3,2},{4,5},{5,4},{6,7},{7,6},{8,9},{9,8},{10,11... | collective-permute-start | bytes 638984 | tf_op jit(solution)/shard_map/ppermute | solution.py:347
  41.8 7.2 %collective-permute-start.14 = (f32[26,16,128]{2,1,0:T(8,128)S(1)}, f32[26,16,128]{2,1,0:T(8,128)S(1)}, u32[]{:S(2)}, u32[]{:S(2)}) collective-permute-start(f32[26,16,128]{2,1,0:T(8,128)S(1)} %get-tuple-element.33), channel_id=1, source_target_pairs={{1,2},{2,1},{3,4},{4,3},{5,6},{6,5},{9,10},{10,9},{11,12},{12,11},... | collective-permute-start | bytes 638984 | tf_op jit(solution)/shard_map/ppermute | solution.py:347
